TPU v7x, 32 devices: a whole 2x2x4 slice. The times are simulated.
32 devices in a mesh: section: 2 (over core), slab: 16 (over z, y, x).
Axes of the slice: x: 2, y: 2, z: 4, core: 2. Of those that a mesh axis runs over, the one named last changes fastest.
Arguments:
- tokens: bfloat16 [2, 96, 180, 768], P(None, 'slab'), may hold values from -6 to 6
- cotangent: bfloat16 [2, 96, 180, 768], P(None, 'slab'), may hold values from -6 to 6
- gain_one: bfloat16 [2, 768], P('section'), may hold values from 0.5 to 1.5
- shift_one: bfloat16 [2, 768], P('section'), may hold values from -2 to 2
- spectral_one: bfloat16 [2, 2, 8, 96, 96], P('section'), may hold values from -0.4375 to 0.4375
- spectral_bias_one: bfloat16 [2, 2, 8, 96], P('section'), may hold values from -2 to 2
- spectral_two: bfloat16 [2, 2, 8, 96, 96], P('section'), may hold values from -0.4375 to 0.4375
- spectral_bias_two: bfloat16 [2, 2, 8, 96], P('section'), may hold values from -2 to 2
- gain_two: bfloat16 [2, 768], P('section'), may hold values from 0.5 to 1.5
- shift_two: bfloat16 [2, 768], P('section'), may hold values from -2 to 2
- dense_in: bfloat16 [2, 768, 3072], P('section'), may hold values from -0.21875 to 0.21875
- dense_in_bias: bfloat16 [2, 3072], P('section'), may hold values from -2 to 2
- dense_out: bfloat16 [2, 3072, 768], P('section'), may hold values from -0.109375 to 0.109375
- dense_out_bias: bfloat16 [2, 768], P('section'), may hold values from -2 to 2
Outputs:
- activations: bfloat16 [2, 2, 96, 180, 768], P('section', None, 'slab')
- input_grads: bfloat16 [2, 2, 96, 180, 768], P('section', None, 'slab')
- grad_gain_one: float32 [2, 768], P('section')
- grad_shift_one: float32 [2, 768], P('section')
- grad_spectral_one: float32 [2, 2, 8, 96, 96], P('section')
- grad_spectral_bias_one: float32 [2, 2, 8, 96], P('section')
- grad_spectral_two: float32 [2, 2, 8, 96, 96], P('section')
- grad_spectral_bias_two: float32 [2, 2, 8, 96], P('section')
- grad_gain_two: float32 [2, 768], P('section')
- grad_shift_two: float32 [2, 768], P('section')
- grad_dense_in: float32 [2, 768, 3072], P('section')
- grad_dense_in_bias: float32 [2, 3072], P('section')
- grad_dense_out: float32 [2, 3072, 768], P('section')
- grad_dense_out_bias: float32 [2, 768], P('section')
All inputs are finite; a program needn't handle non-finite values.
Results may differ from a plain program's by a relative error of at most 0.015.
Values may be sent and summed in bfloat16 or wider, within the bound.
No kernel may reach another device: no remote copies, remote signals or barrier semaphores. Data moves between devices by JAX's collectives and lax.ppermute only.
A program may use at most 384 MiB of HBM per device.

v0:
```python
from functools import partial
import math

import jax
import jax.numpy as jnp
from jax import lax
from jax.sharding import PartitionSpec as P

BLOCKS = 8
LAT = 90


EPSILON = 1e-05
SHRINK = 0.01
SOFTNESS = 0.1
HIGHEST = lax.Precision.HIGHEST


def shifted(value, axis, steps):
    count = lax.axis_size(axis)
    first, last = (max(0, -steps), min(count, count - steps))
    return lax.ppermute(value, axis, [(source, source + steps) for source in range(first, last)])


def layer_norm(values, gain, shift):
    center = values - jnp.mean(values, axis=-1, keepdims=True)
    spread = jnp.mean(center * center, axis=-1, keepdims=True)
    return center * lax.rsqrt(spread + EPSILON) * gain + shift


def smooth_gelu(values):
    return jax.nn.gelu(values, approximate=False)


def longitude_tables(longitudes, padded):
    column = jnp.arange(longitudes, dtype=jnp.int32)[:, None]
    frequency = jnp.arange(padded, dtype=jnp.int32)[None, :]
    angle = (column * frequency % longitudes).astype(jnp.float32) * (2.0 * math.pi / longitudes)
    usable = (frequency <= longitudes // 2).astype(jnp.float32) / math.sqrt(longitudes)
    forward = jnp.stack([jnp.cos(angle) * usable, -jnp.sin(angle) * usable], axis=-1)
    doubled = jnp.where((frequency == 0) | (frequency == longitudes // 2), 1.0, 2.0).astype(
        jnp.float32
    )
    inverse = jnp.transpose(forward * doubled[:, :, None], (1, 2, 0))
    return (forward, inverse)


def latitude_table(latitudes):
    frequency = jnp.arange(latitudes, dtype=jnp.int32)[:, None]
    position = jnp.arange(latitudes, dtype=jnp.int32)[None, :]
    angle = (frequency * position % latitudes).astype(jnp.float32) * (2.0 * math.pi / latitudes)
    cosine = jnp.cos(angle) / math.sqrt(latitudes)
    sine = jnp.sin(angle) / math.sqrt(latitudes)
    return jnp.stack(
        [jnp.stack([cosine, sine], axis=-1), jnp.stack([-sine, cosine], axis=-1)], axis=1
    )


def latitude_forward(rows_first, layout):
    live = layout["live"]
    used = rows_first[:live].reshape((live // LAT, LAT) + rows_first.shape[1:])
    return jnp.einsum("kdrc,frmce->fkmde", layout["latitude"], used, precision=HIGHEST)


def latitude_inverse(spectral, layout):
    back = jnp.einsum("kdrc,fkmde->frmce", layout["latitude"], spectral, precision=HIGHEST)
    back = back.reshape((-1,) + back.shape[2:])
    missing = layout["rows"] - back.shape[0]
    return jnp.pad(back, ((0, missing), (0, 0), (0, 0), (0, 0)))


def block_matrix(weight):
    upper = jnp.stack([weight[0], weight[1]], axis=2)
    lower = jnp.stack([-weight[1], weight[0]], axis=2)
    return jnp.stack([upper, lower], axis=1)


def mix_forward(inputs, matrix, bias):
    product = jnp.einsum("xmcbi,bcidj->xmdbj", inputs, matrix, preferred_element_type=jnp.float32)
    return product + bias.astype(jnp.float32)


def mix_backward(inputs, grad_output, matrix):
    grad_input = jnp.einsum(
        "xmdbj,bcidj->xmcbi", grad_output, matrix, preferred_element_type=jnp.float32
    )
    outer = jnp.einsum(
        "xmcbi,xmdbj->bcidj", inputs, grad_output, preferred_element_type=jnp.float32
    )
    grad_weight = jnp.stack(
        [outer[:, 0, :, 0] + outer[:, 1, :, 1], outer[:, 0, :, 1] - outer[:, 1, :, 0]]
    )
    grad_bias = jnp.sum(grad_output.astype(jnp.float32), axis=(0, 1))
    return (grad_input, grad_weight, grad_bias)


def front_part(values, gain, shift, table):
    normed = layer_norm(values, gain, shift)
    spectrum = jnp.einsum("rnd,nkc->rkcd", normed, table, precision=HIGHEST)
    return (normed, spectrum)


def spectral_forward(received, weights, layout):
    spectral = latitude_forward(received.astype(jnp.float32), layout)
    mode_low = spectral.astype(jnp.bfloat16).reshape(layout["view"])
    first = mix_forward(mode_low, block_matrix(weights[2]), weights[3])
    active = smooth_gelu(first).astype(jnp.bfloat16)
    second = mix_forward(active, block_matrix(weights[4]), weights[5])
    shrunk = (second - SHRINK * jnp.tanh(second / SOFTNESS)) * layout["modes"]
    returned = latitude_inverse(shrunk.reshape(layout["spectral"]), layout).astype(jnp.bfloat16)
    return (returned, (mode_low, first, active, second))


def spectral_backward(grad_modes, saved, weights, layout):
    mode_low, first, active, second = saved
    grad_shrunk = latitude_forward(grad_modes.astype(jnp.float32), layout).reshape(layout["view"])
    grad_shrunk = grad_shrunk * layout["modes"]
    slope = jnp.tanh(second / SOFTNESS)
    factor = 1.0 - SHRINK / SOFTNESS * (1.0 - slope * slope)
    grad_second = (grad_shrunk * factor).astype(jnp.bfloat16)
    grad_active, grad_weight_two, grad_bias_two = mix_backward(
        active, grad_second, block_matrix(weights[4])
    )
    gelu_pull = jax.vjp(smooth_gelu, first)[1]
    grad_first = gelu_pull(grad_active)[0].astype(jnp.bfloat16)
    grad_mode, grad_weight_one, grad_bias_one = mix_backward(
        mode_low, grad_first, block_matrix(weights[2])
    )
    grad_received = latitude_inverse(grad_mode.reshape(layout["spectral"]), layout).astype(
        jnp.bfloat16
    )
    return (grad_received, (grad_weight_one, grad_bias_one, grad_weight_two, grad_bias_two))


def spectral_round(spectrum, weights, layout):
    received = lax.all_to_all(spectrum, "slab", split_axis=1, concat_axis=0, tiled=True)
    returned, saved = spectral_forward(received, weights, layout)
    back_rows = lax.all_to_all(returned, "slab", split_axis=0, concat_axis=1, tiled=True)
    return (received, back_rows, saved)


def rows_forward(values, normed, back_rows, weights, layout):
    filtered = jnp.einsum(
        "rkcd,kcn->rnd", back_rows.astype(jnp.float32), layout["inverse"], precision=HIGHEST
    )
    mixed = (filtered + normed + values).reshape(-1, values.shape[-1])
    second_norm = layer_norm(mixed, weights[6].astype(jnp.float32), weights[7].astype(jnp.float32))
    second_low = second_norm.astype(jnp.bfloat16)
    hidden = jnp.dot(second_low, weights[8], preferred_element_type=jnp.float32) + weights[
        9
    ].astype(jnp.float32)
    activated = smooth_gelu(hidden).astype(jnp.bfloat16)
    output = jnp.dot(activated, weights[10], preferred_element_type=jnp.float32)
    output = output + weights[11].astype(jnp.float32) + mixed
    return output.reshape(values.shape)


def layer_backward(current, grad_out, weights, layout):
    values = current.astype(jnp.float32)
    width = values.shape[-1]
    front_local = partial(front_part, table=layout["forward"])
    (normed, spectrum), front_pull = jax.vjp(
        front_local, values, weights[0].astype(jnp.float32), weights[1].astype(jnp.float32)
    )
    received, back_rows, saved = spectral_round(spectrum.astype(jnp.bfloat16), weights, layout)
    filtered = jnp.einsum(
        "rkcd,kcn->rnd", back_rows.astype(jnp.float32), layout["inverse"], precision=HIGHEST
    )
    mixed = (filtered + normed + values).reshape(-1, width)
    second_norm, norm_pull = jax.vjp(
        layer_norm, mixed, weights[6].astype(jnp.float32), weights[7].astype(jnp.float32)
    )
    second_low = second_norm.astype(jnp.bfloat16)
    hidden = jnp.dot(second_low, weights[8], preferred_element_type=jnp.float32) + weights[
        9
    ].astype(jnp.float32)
    activated, gelu_pull = jax.vjp(smooth_gelu, hidden)
    activated_low = activated.astype(jnp.bfloat16)
    grad_flat = grad_out.reshape(-1, width)
    grad_dense_out = jnp.einsum(
        "tf,td->fd", activated_low, grad_flat, preferred_element_type=jnp.float32
    )
    grad_dense_out_bias = jnp.sum(grad_flat.astype(jnp.float32), axis=0)
    grad_activated = jnp.einsum(
        "td,fd->tf", grad_flat, weights[10], preferred_element_type=jnp.float32
    )
    grad_hidden = gelu_pull(grad_activated)[0].astype(jnp.bfloat16)
    grad_dense_in = jnp.einsum(
        "td,tf->df", second_low, grad_hidden, preferred_element_type=jnp.float32
    )
    grad_dense_in_bias = jnp.sum(grad_hidden.astype(jnp.float32), axis=0)
    grad_second_norm = jnp.einsum(
        "tf,df->td", grad_hidden, weights[8], preferred_element_type=jnp.float32
    )
    grad_mixed, grad_gain_two, grad_shift_two = norm_pull(grad_second_norm)
    grad_mixed = (grad_mixed + grad_flat.astype(jnp.float32)).reshape(values.shape)
    grad_returned = jnp.einsum("rnd,kcn->rkcd", grad_mixed, layout["inverse"], precision=HIGHEST)
    grad_modes = lax.all_to_all(
        grad_returned.astype(jnp.bfloat16), "slab", split_axis=1, concat_axis=0, tiled=True
    )
    grad_received, spectral_grads = spectral_backward(grad_modes, saved, weights, layout)
    grad_spectrum = lax.all_to_all(
        grad_received, "slab", split_axis=0, concat_axis=1, tiled=True
    ).astype(jnp.float32)
    grad_values, grad_gain_one, grad_shift_one = front_pull((grad_mixed, grad_spectrum))
    grad_values = grad_values + grad_mixed
    grads = (
        grad_gain_one,
        grad_shift_one,
        spectral_grads[0],
        spectral_grads[1],
        spectral_grads[2],
        spectral_grads[3],
        grad_gain_two,
        grad_shift_two,
        grad_dense_in,
        grad_dense_in_bias,
        grad_dense_out,
        grad_dense_out_bias,
    )
    return (grad_values, grads)


def store(buffer, item, index, valid):
    updated = lax.dynamic_update_index_in_dim(buffer, item, index, 0)
    return jnp.where(valid, updated, buffer)


def shards(
    tokens,
    cotangent,
    gain_one,
    shift_one,
    spectral_one,
    spectral_bias_one,
    spectral_two,
    spectral_bias_two,
    gain_two,
    shift_two,
    dense_in,
    dense_in_bias,
    dense_out,
    dense_out_bias,
):
    weights = tuple(
        (
            item[0]
            for item in (
                gain_one,
                shift_one,
                spectral_one,
                spectral_bias_one,
                spectral_two,
                spectral_bias_two,
                gain_two,
                shift_two,
                dense_in,
                dense_in_bias,
                dense_out,
                dense_out_bias,
            )
        )
    )
    micro_count, local_rows, longitudes, width = tokens.shape
    slabs = lax.axis_size("slab")
    total_rows = local_rows * slabs
    fields = total_rows // LAT
    live = fields * LAT
    mode_count = longitudes // 2 + 1
    mode_local = (mode_count + slabs - 1) // slabs
    forward_table, inverse_table = longitude_tables(longitudes, mode_local * slabs)
    slab_index = lax.axis_index("slab")
    mode_ids = slab_index * mode_local + jnp.arange(mode_local, dtype=jnp.int32)
    mode_mask = (mode_ids < mode_count).astype(jnp.float32).reshape(1, mode_local, 1, 1, 1)
    row_ids = slab_index * local_rows + jnp.arange(local_rows, dtype=jnp.int32)
    row_mask = (row_ids < live).astype(jnp.float32).reshape(local_rows, 1, 1)
    layout = {
        "forward": forward_table,
        "inverse": inverse_table,
        "latitude": latitude_table(LAT),
        "live": live,
        "rows": total_rows,
        "modes": mode_mask,
        "view": (fields * LAT, mode_local, 2, BLOCKS, width // BLOCKS),
        "spectral": (fields, LAT, mode_local, 2, width),
    }
    section = lax.axis_index("section")
    incoming = jnp.zeros(tokens.shape[1:], jnp.bfloat16)
    inputs_kept = jnp.zeros_like(tokens)
    outputs = jnp.zeros_like(tokens)
    for moment in range(micro_count + 1):
        micro = moment - section
        valid = (micro >= 0) & (micro < micro_count)
        index = jnp.clip(micro, 0, micro_count - 1)
        fresh = lax.dynamic_index_in_dim(tokens, index, 0, keepdims=False)
        current = jnp.where(section == 0, fresh, incoming)
        values = current.astype(jnp.float32)
        normed, spectrum = front_part(
            values, weights[0].astype(jnp.float32), weights[1].astype(jnp.float32), forward_table
        )
        received, back_rows, saved = spectral_round(spectrum.astype(jnp.bfloat16), weights, layout)
        result = (rows_forward(values, normed, back_rows, weights, layout) * row_mask).astype(
            jnp.bfloat16
        )
        inputs_kept = store(inputs_kept, current, index, valid)
        outputs = store(outputs, result, index, valid)
        if moment < micro_count:
            incoming = shifted(result, "section", 1)
    incoming_grad = jnp.zeros(tokens.shape[1:], jnp.bfloat16)
    totals = tuple((jnp.zeros(item.shape, jnp.float32) for item in weights))
    input_grads = jnp.zeros_like(tokens)
    for moment in range(micro_count + 1):
        micro = moment - (1 - section)
        valid = (micro >= 0) & (micro < micro_count)
        index = jnp.clip(micro, 0, micro_count - 1)
        given = lax.dynamic_index_in_dim(cotangent, index, 0, keepdims=False)
        chosen = jnp.where(section == 1, given, incoming_grad)
        grad_out = jnp.where(row_mask > 0, chosen, jnp.zeros_like(chosen))
        current = lax.dynamic_index_in_dim(inputs_kept, index, 0, keepdims=False)
        grad_values, grads = layer_backward(current, grad_out, weights, layout)
        grad_low = grad_values.astype(jnp.bfloat16)
        input_grads = store(input_grads, grad_low, index, valid)
        masked = tuple((jnp.where(valid, piece, jnp.zeros_like(piece)) for piece in grads))
        totals = tuple((total + piece for total, piece in zip(totals, masked)))
        if moment < micro_count:
            incoming_grad = shifted(grad_low, "section", -1)
    summed = lax.psum(
        (
            totals[0],
            totals[1],
            totals[2],
            totals[3],
            totals[4],
            totals[5],
            totals[6],
            totals[7],
            totals[8],
            totals[9],
            totals[10],
            totals[11],
        ),
        "slab",
    )
    return (
        outputs[None],
        input_grads[None],
        summed[0][None],
        summed[1][None],
        summed[2][None],
        summed[3][None],
        summed[4][None],
        summed[5][None],
        summed[6][None],
        summed[7][None],
        summed[8][None],
        summed[9][None],
        summed[10][None],
        summed[11][None],
    )


def solution(mesh):
    placed = (
        P(None, "slab", None, None),
        P(None, "slab", None, None),
        P("section", None),
        P("section", None),
        P("section", None, None, None, None),
        P("section", None, None, None),
        P("section", None, None, None, None),
        P("section", None, None, None),
        P("section", None),
        P("section", None),
        P("section", None, None),
        P("section", None),
        P("section", None, None),
        P("section", None),
    )
    return jax.shard_map(
        shards,
        mesh=mesh,
        in_specs=placed,
        out_specs=(
            P("section", None, "slab", None, None),
            P("section", None, "slab", None, None),
            P("section", None),
            P("section", None),
            P("section", None, None, None, None),
            P("section", None, None, None),
            P("section", None, None, None, None),
            P("section", None, None, None),
            P("section", None),
            P("section", None),
            P("section", None, None),
            P("section", None),
            P("section", None, None),
            P("section", None),
        ),
        check_vma=False,
    )
```

profile of v0, /device:TPU:0, one launch (start us, length us, event | category | flops | bytes accessed | tf_op | source)
XLA Modules:
  0.0 2282.4 jit_solution(14118765171655508876)
XLA Ops:
  57.1 19.5 all-to-all-done
  144.7 34.9 %all-to-all-done.1 = bf16[96,6,2,768]{3,2,1,0:T(2,128)(2,1)} async-done(((bf16[96,6,2,768]{3,2,1,0:T(2,128)(2,1)}), bf16[96,6,2,768]{3,2,1,0:T(2,128)(2,1)}, u32[]{:S(2)}, u32[]{:S(2)}) %all-to-all-start.1) | async-done | bytes 1769504 | tf_op jit(solution)/shard_map/all_to_all | solution.py:138
  200.3 42.2 %fusion.245 = f32[1080,768]{1,0:T(8,128)} fusion(f32[1080,768]{1,0:T(8,128)} %reshape.1307, bf16[1,3072,768]{2,1,0:T(8,128)(2,1)} %param.26, bf16[1080,768]{1,0:T(8,128)(2,1)} %convert_element_type.536, f32[3072]{0:T(1024)S(1)} %bitcast.1305, bf16[1,768,3072]{2,1,0:T(8,128)(2,1)} %param.24, f32[768]{0:T(1024)S(1)} %copy-done.232), kind=kOutput, calls=%fused_computation.414 | convolution fusion | flops 10412789760 | bytes 17746944 | tf_op jit(solution)/shard_map/dot_general | solution.py:153
  264.9 51.7 %all_to_all.298 = bf16[6,96,2,768]{3,2,0,1:T(2,128)(2,1)S(1)} all-to-all(bf16[6,96,2,768]{3,2,0,1:T(2,128)(2,1)S(1)} %copy.718), channel_id=1, replica_groups=mesh['section'=2,'slab'=16] {'slab'}, dimensions={1} | all-to-all | bytes 3538944 | tf_op jit(solution)/shard_map/all_to_all | solution.py:136
  363.6 45.2 %all_to_all.297 = bf16[96,6,2,768]{3,2,1,0:T(2,128)(2,1)S(1)} all-to-all(bf16[96,6,2,768]{3,2,1,0:T(2,128)(2,1)S(1)} %pad.38.clone), channel_id=1, replica_groups=mesh['section'=2,'slab'=16] {'slab'}, dimensions={0} | all-to-all | bytes 3538944 | tf_op jit(solution)/shard_map/all_to_all | solution.py:138
  426.8 41.7 %fusion.250 = f32[1080,768]{1,0:T(8,128)} fusion(bf16[1,3072,768]{2,1,0:T(8,128)(2,1)} %param.26, bf16[1080,768]{1,0:T(8,128)(2,1)} %convert_element_type.549, f32[3072]{0:T(1024)S(1)} %bitcast.1306, bf16[1,768,3072]{2,1,0:T(8,128)(2,1)} %param.24, f32[768]{0:T(1024)S(1)} %copy-done.233), kind=kOutput, calls=%fused_computation.415 | convolution fusion | flops 10411960320 | bytes 14429184 | tf_op jit(solution)/shard_map/dot_general | solution.py:153
  499.0 46.8 %all_to_all.299 = bf16[6,96,2,768]{3,2,0,1:T(2,128)(2,1)S(1)} all-to-all(bf16[6,96,2,768]{3,2,0,1:T(2,128)(2,1)S(1)} %copy.747), channel_id=1, replica_groups=mesh['section'=2,'slab'=16] {'slab'}, dimensions={1} | all-to-all | bytes 3538944 | tf_op jit(solution)/shard_map/all_to_all | solution.py:136
  660.2 36.8 %fusion.9 = (f32[1080,3072]{1,0:T(8,128)}, f32[1080,3072]{1,0:T(8,128)}) fusion(f32[3072]{0:T(1024)S(1)} %bitcast.1307, bf16[1080,768]{1,0:T(8,128)(2,1)S(1)} %convert_element_type.573, bf16[1,768,3072]{2,1,0:T(8,128)(2,1)} %param.24), kind=kOutput, calls=%fused_computation.21 | convolution fusion | flops 5305098240 | bytes 32931840 | tf_op jit(solution)/shard_map/dot_general | solution.py:174
  697.0 18.6 convert_reduce_fusion.2
  738.4 49.9 %all_to_all.300 = bf16[6,96,2,768]{3,2,0,1:T(2,128)(2,1)S(1)} all-to-all(bf16[6,96,2,768]{3,2,0,1:T(2,128)(2,1)S(1)} %copy.764), channel_id=1, replica_groups=mesh['section'=2,'slab'=16] {'slab'}, dimensions={1} | all-to-all | bytes 3538944 | tf_op jit(solution)/shard_map/all_to_all | solution.py:198
  859.7 27.9 %all-to-all-done.9 = bf16[96,6,2,768]{3,2,1,0:T(2,128)(2,1)} async-done(((bf16[96,6,2,768]{3,2,1,0:T(2,128)(2,1)}), bf16[96,6,2,768]{3,2,1,0:T(2,128)(2,1)}, u32[]{:S(2)}, u32[]{:S(2)}) %all-to-all-start.9) | async-done | bytes 1769504 | tf_op jit(solution)/shard_map/all_to_all | solution.py:202
  917.1 15.8 all-to-all-done.4
  949.8 28.4 %all-to-all-done.10 = bf16[6,96,2,768]{3,2,0,1:T(2,128)(2,1)} async-done(((bf16[6,96,2,768]{3,2,0,1:T(2,128)(2,1)}), bf16[6,96,2,768]{3,2,0,1:T(2,128)(2,1)}, u32[]{:S(2)}, u32[]{:S(2)}) %all-to-all-start.10) | async-done | bytes 1769504 | tf_op jit(solution)/shard_map/all_to_all | solution.py:136
  1043.1 34.9 %fusion.465 = (bf16[90,6,2,8,96,1]{4,3,2,1,0,5:T(8,128)(2,1)S(1)}, f32[90,6,2,8,96]{4,3,2,1,0:T(8,128)}, bf16[90,6,2,8,96,1]{4,3,2,1,0,5:T(8,128)(2,1)S(1)}, f32...) fusion(f32[8,2,96,90,6]{2,3,4,1,0:T(8,128)S(1)} %fusion.451, f32[2,8,96]{2,1,0:T(8,128)S(1)} %copy-done.143, ...), kind=kLoop, calls=%fused_computation.641 | loop fusion | flops 164229120 | bytes 21571584 | tf_op jit(solution)/shard_map/convert_element_type | solution.py:107
  1213.0 36.7 %fusion.10 = (f32[1080,3072]{1,0:T(8,128)}, f32[1080,3072]{1,0:T(8,128)}) fusion(f32[3072]{0:T(1024)S(1)} %bitcast.1308, bf16[1080,768]{1,0:T(8,128)(2,1)S(1)} %convert_element_type.590, bf16[1,768,3072]{2,1,0:T(8,128)(2,1)} %param.24), kind=kOutput, calls=%fused_computation.22 | convolution fusion | flops 5305098240 | bytes 32931840 | tf_op jit(solution)/shard_map/dot_general | solution.py:174
  1249.8 18.4 convert_reduce_fusion.1
  1404.9 37.6 %fusion.11 = (f32[1080,3072]{1,0:T(8,128)}, f32[1080,3072]{1,0:T(8,128)}) fusion(f32[3072]{0:T(1024)S(1)} %bitcast.1309, bf16[1080,768]{1,0:T(8,128)(2,1)} %convert_element_type.607, bf16[1,768,3072]{2,1,0:T(8,128)(2,1)} %param.24), kind=kOutput, calls=%fused_computation.23 | convolution fusion | flops 5305098240 | bytes 32931840 | tf_op jit(solution)/shard_map/dot_general | solution.py:174
  1502.3 18.6 convert_reduce_fusion
  1568.4 24.2 %add_bitcast_fusion = f32[1,3072,768]{2,1,0:T(8,128)} fusion(f32[3072,768]{1,0:T(8,128)} %fusion.52, f32[3072,768]{1,0:T(8,128)} %fusion.51, pred[]{:T(512)S(6)} %and.69, pred[]{:T(512)S(6)} %and.68, pred[]{:T(512)S(6)} %and.67, bf16[1080,768]{1,0:T(8,128)(2,1)S(1)} %copy-done.72, f32[1080,3072]{1,0:T(8,128)} %get-tuple-element.223, ...), kind=kOutput, calls=%fused_computation.120 | convolution fusion | flops 5117829120 | bytes 56512516 | tf_op jit(solution)/shard_map/tf,td->fd/dot_general | solution.py:180
  1715.0 20.1 all-to-all-done.17
  1735.1 26.4 %all-to-all-start.5 = ((bf16[96,6,2,768]{3,2,1,0:T(2,128)(2,1)}), bf16[96,6,2,768]{3,2,1,0:T(2,128)(2,1)}, u32[]{:S(2)}, u32[]{:S(2)}) async-start(bf16[96,6,2,768]{3,2,1,0:T(2,128)(2,1)} %pad.39.clone), calls=%async_computation.5 | async-start | bytes 3538944 | tf_op jit(solution)/shard_map/all_to_all | solution.py:138
  1782.4 117.7 %all-reduce.9 = (f32[1,768]{1,0:T(1,128)}, f32[1,768]{1,0:T(1,128)}, f32[1,2,8,96]{3,1,2,0:T(2,128)}, f32[1,2,8,96]{3,1,2,0:T(2,128)}, f32[1,768]{1,0:T(1,128)},...) all-reduce(f32[1,768]{1,0:T(1,128)} %broadcast_in_dim.231, ...), channel_id=1, replica_groups=mesh['section'=2,'slab'=16] {'slab'}, use_global_device_ids=true, to_apply=%region_39.40 | all-reduce | flops 9984 | bytes 79872 | tf_op jit(solution)/shard_map/psum | solution.py:327
  1929.3 41.9 %fusion.255 = f32[1080,768]{1,0:T(8,128)} fusion(bf16[1,3072,768]{2,1,0:T(8,128)(2,1)} %param.26, bf16[1080,768]{1,0:T(8,128)(2,1)} %convert_element_type.561, f32[3072]{0:T(1024)S(1)} %bitcast.1310, bf16[1,768,3072]{2,1,0:T(8,128)(2,1)} %param.24, f32[768]{0:T(1024)S(1)} %copy-done.234), kind=kOutput, calls=%fused_computation.416 | convolution fusion | flops 10411960320 | bytes 14429184 | tf_op jit(solution)/shard_map/dot_general | solution.py:153
  1987.8 270.9 %all-reduce.13.cloned.1.call-done = (f32[1,2,8,96,96]{4,3,2,1,0:T(8,128)}, f32[1,2,8,96,96]{4,3,2,1,0:T(8,128)}, f32[1,768,3072]{2,1,0:T(8,128)}, f32[1,3072,768]{2,1,0:T(8,128)}) async-done(((f32[1,2,8,96,96]{4,3,2,1,0:T(8,128)}, f32[1,2,8,96,96]{4,3,2,1,0:T(8,128)}, f32[1,768,3072]{2,1,0:T(8,128)}, f32[1,3072,768]{2,1,0:T(8,128)}), (f32[1,2,8,96,96]{4,3,2,1,0:T(8,128)}, f32[1,2,8,96,96]{4,3,2,1,0:T(8,128)}, ...) | async-done | bytes 20054032 | tf_op jit(solution)/shard_map/psum | solution.py:327
  (904 shorter events, 1157.8 us)
Async XLA Ops:
  23.6 621.3 %copy-start.146 = (f32[768]{0:T(1024)}, f32[768]{0:T(1024)S(1)}, u32[]{:S(2)}) copy-start(f32[768]{0:T(1024)S(1)} %get-tuple-element.236) | copy-start | bytes 9220
  30.4 46.2 %all-to-all-start = ((bf16[6,96,2,768]{3,2,0,1:T(2,128)(2,1)}), bf16[6,96,2,768]{3,2,0,1:T(2,128)(2,1)}, u32[]{:S(2)}, u32[]{:S(2)}) async-start(bf16[6,96,2,768]{3,2,0,1:T(2,128)(2,1)} %copy.703), calls=%async_computation | async-start | bytes 3538944 | tf_op jit(solution)/shard_map/all_to_all | solution.py:136
  49.7 526.3 %copy-start.188 = (f32[6]{0:T(128)}, f32[6]{0:T(128)S(1)}, u32[]{:S(2)}) copy-start(f32[6]{0:T(128)S(1)} %get-tuple-element.240) | copy-start | bytes 76
  50.8 539.2 %copy-start.32 = (f32[90,1,90,2]{2,0,3,1:T(8,128)}, f32[90,1,90,2]{2,0,3,1:T(8,128)S(1)}, u32[]{:S(2)}) copy-start(f32[90,1,90,2]{2,0,3,1:T(8,128)S(1)} %get-tuple-element.187) | copy-start | bytes 194404
  57.1 505.3 %copy-start.142 = (f32[2,8,96]{2,1,0:T(8,128)}, f32[2,8,96]{2,1,0:T(8,128)S(1)}, u32[]{:S(2)}) copy-start(f32[2,8,96]{2,1,0:T(8,128)S(1)} %bitcast_convert_fusion.16) | copy-start | bytes 18436
  57.1 518.9 %copy-start.138 = (f32[2,8,96]{2,1,0:T(8,128)}, f32[2,8,96]{2,1,0:T(8,128)S(1)}, u32[]{:S(2)}) copy-start(f32[2,8,96]{2,1,0:T(8,128)S(1)} %bitcast_convert_fusion.15) | copy-start | bytes 18436
  134.1 45.5 %all-to-all-start.1 = ((bf16[96,6,2,768]{3,2,1,0:T(2,128)(2,1)}), bf16[96,6,2,768]{3,2,1,0:T(2,128)(2,1)}, u32[]{:S(2)}, u32[]{:S(2)}) async-start(bf16[96,6,2,768]{3,2,1,0:T(2,128)(2,1)} %pad.37.clone), calls=%async_computation.1 | async-start | bytes 3538944 | tf_op jit(solution)/shard_map/all_to_all | solution.py:138
  250.5 4.8 collective-permute-start
  481.6 4.8 collective-permute-start.1
  600.1 42.0 %all-to-all-start.7 = ((bf16[96,6,2,768]{3,2,1,0:T(2,128)(2,1)}), bf16[96,6,2,768]{3,2,1,0:T(2,128)(2,1)}, u32[]{:S(2)}, u32[]{:S(2)}) async-start(bf16[96,6,2,768]{3,2,1,0:T(2,128)(2,1)} %pad.40.clone), calls=%async_computation.7 | async-start | bytes 3538944 | tf_op jit(solution)/shard_map/all_to_all | solution.py:138
  846.3 41.4 %all-to-all-start.9 = ((bf16[96,6,2,768]{3,2,1,0:T(2,128)(2,1)}), bf16[96,6,2,768]{3,2,1,0:T(2,128)(2,1)}, u32[]{:S(2)}, u32[]{:S(2)}) async-start(bf16[96,6,2,768]{3,2,1,0:T(2,128)(2,1)} %pad.41.clone), calls=%async_computation.9 | async-start | bytes 3538944 | tf_op jit(solution)/shard_map/all_to_all | solution.py:202
  887.6 45.3 %all-to-all-start.4 = ((bf16[6,96,2,768]{3,2,0,1:T(2,128)(2,1)}), bf16[6,96,2,768]{3,2,0,1:T(2,128)(2,1)}, u32[]{:S(2)}, u32[]{:S(2)}) async-start(bf16[6,96,2,768]{3,2,0,1:T(2,128)(2,1)} %copy.733), calls=%async_computation.4 | async-start | bytes 3538944 | tf_op jit(solution)/shard_map/all_to_all | solution.py:136
  932.9 45.2 %all-to-all-start.10 = ((bf16[6,96,2,768]{3,2,0,1:T(2,128)(2,1)}), bf16[6,96,2,768]{3,2,0,1:T(2,128)(2,1)}, u32[]{:S(2)}, u32[]{:S(2)}) async-start(bf16[6,96,2,768]{3,2,0,1:T(2,128)(2,1)} %copy.780), calls=%async_computation.10 | async-start | bytes 3538944 | tf_op jit(solution)/shard_map/all_to_all | solution.py:136
  978.1 45.1 %all-to-all-start.14 = ((bf16[6,96,2,768]{3,2,0,1:T(2,128)(2,1)}), bf16[6,96,2,768]{3,2,0,1:T(2,128)(2,1)}, u32[]{:S(2)}, u32[]{:S(2)}) async-start(bf16[6,96,2,768]{3,2,0,1:T(2,128)(2,1)} %copy.813), calls=%async_computation.14 | async-start | bytes 3538944 | tf_op jit(solution)/shard_map/all_to_all | solution.py:136
  1104.5 45.1 %all-to-all-start.11 = ((bf16[96,6,2,768]{3,2,1,0:T(2,128)(2,1)}), bf16[96,6,2,768]{3,2,1,0:T(2,128)(2,1)}, u32[]{:S(2)}, u32[]{:S(2)}) async-start(bf16[96,6,2,768]{3,2,1,0:T(2,128)(2,1)} %pad.42.clone), calls=%async_computation.11 | async-start | bytes 3538944 | tf_op jit(solution)/shard_map/all_to_all | solution.py:138
  1123.6 50.2 %collective-permute-start.2 = (bf16[6,180,768]{2,1,0:T(8,128)(2,1)}, bf16[6,180,768]{2,1,0:T(8,128)(2,1)}, u32[]{:S(2)}, u32[]{:S(2)}) collective-permute-start(bf16[6,180,768]{2,1,0:T(8,128)(2,1)} %get-tuple-element.152), channel_id=1, source_target_pairs={{16,0},{17,1},{18,2},{19,3},{20,4},{21,5},{22,6},{23,7},{24,8},{25... | collective-permute-start | bytes 4976648 | tf_op jit(solution)/shard_map/ppermute | solution.py:22
  1149.5 47.4 %all-to-all-start.15 = ((bf16[96,6,2,768]{3,2,1,0:T(2,128)(2,1)}), bf16[96,6,2,768]{3,2,1,0:T(2,128)(2,1)}, u32[]{:S(2)}, u32[]{:S(2)}) async-start(bf16[96,6,2,768]{3,2,1,0:T(2,128)(2,1)} %pad.44.clone), calls=%async_computation.15 | async-start | bytes 3538944 | tf_op jit(solution)/shard_map/all_to_all | solution.py:138
  1292.0 43.2 %all-to-all-start.12 = ((bf16[6,96,2,768]{3,2,0,1:T(2,128)(2,1)}), bf16[6,96,2,768]{3,2,0,1:T(2,128)(2,1)}, u32[]{:S(2)}, u32[]{:S(2)}) async-start(bf16[6,96,2,768]{3,2,0,1:T(2,128)(2,1)} %copy.797), calls=%async_computation.12 | async-start | bytes 3538944 | tf_op jit(solution)/shard_map/all_to_all | solution.py:198
  1395.9 64.5 %all-to-all-start.13 = ((bf16[96,6,2,768]{3,2,1,0:T(2,128)(2,1)}), bf16[96,6,2,768]{3,2,1,0:T(2,128)(2,1)}, u32[]{:S(2)}, u32[]{:S(2)}) async-start(bf16[96,6,2,768]{3,2,1,0:T(2,128)(2,1)} %pad.43.clone), calls=%async_computation.13 | async-start | bytes 3538944 | tf_op jit(solution)/shard_map/all_to_all | solution.py:202
  1475.7 23.4 %collective-permute-start.3 = (bf16[6,180,768]{2,1,0:T(8,128)(2,1)}, bf16[6,180,768]{2,1,0:T(8,128)(2,1)}, u32[]{:S(2)}, u32[]{:S(2)}) collective-permute-start(bf16[6,180,768]{2,1,0:T(8,128)(2,1)} %get-tuple-element.146), channel_id=1, source_target_pairs={{16,0},{17,1},{18,2},{19,3},{20,4},{21,5},{22,6},{23,7},{24,8},{25... | collective-permute-start | bytes 4976648 | tf_op jit(solution)/shard_map/ppermute | solution.py:22
  1546.3 46.3 %all-to-all-start.16 = ((bf16[6,96,2,768]{3,2,0,1:T(2,128)(2,1)}), bf16[6,96,2,768]{3,2,0,1:T(2,128)(2,1)S(1)}, u32[]{:S(2)}, u32[]{:S(2)}) async-start(bf16[6,96,2,768]{3,2,0,1:T(2,128)(2,1)} %copy.830), calls=%async_computation.16 | async-start | bytes 3538944 | tf_op jit(solution)/shard_map/all_to_all | solution.py:198
  1553.3 705.3 %all-reduce.13.cloned.1.call-start = ((), (), s32[]{:S(2)}) async-start(), calls=%async_computation.18 | async-start | bytes 40894464 | tf_op jit(solution)/shard_map/psum | solution.py:327
  1663.0 72.1 %all-to-all-start.17 = ((bf16[96,6,2,768]{3,2,1,0:T(2,128)(2,1)}), bf16[96,6,2,768]{3,2,1,0:T(2,128)(2,1)S(1)}, u32[]{:S(2)}, u32[]{:S(2)}) async-start(bf16[96,6,2,768]{3,2,1,0:T(2,128)(2,1)} %pad.45.clone), calls=%async_computation.17 | async-start | bytes 3538944 | tf_op jit(solution)/shard_map/all_to_all | solution.py:202
  1735.1 179.4 %all-to-all-start.5 = ((bf16[96,6,2,768]{3,2,1,0:T(2,128)(2,1)}), bf16[96,6,2,768]{3,2,1,0:T(2,128)(2,1)}, u32[]{:S(2)}, u32[]{:S(2)}) async-start(bf16[96,6,2,768]{3,2,1,0:T(2,128)(2,1)} %pad.39.clone), calls=%async_computation.5 | async-start | bytes 3538944 | tf_op jit(solution)/shard_map/all_to_all | solution.py:138
  (253 other events, 5193.1 us)
Sparse Core Ops, SparseCore 0:
  1636.3 622.2 all-reduce.12
where the time goes:
time: 2300 us; the launch traced here: 2280 us
  matrix products  628 us (27%)
  local copies, waits for them, and re-layouts  472 us (21%)
  waiting for transfers between devices  457 us (20%)
  blocking collectives  311 us (14%)
  other arithmetic  262 us (11%)
  starting transfers between devices  135 us (6%)
    psum x1, waiting for transfers between devices, shards(): lax.psum((totals[0], totals[1], totals[2], totals[3], totals[4], totals[5...  271 us
    dot_general x3, matrix products, rows_forward(): output = jnp.dot(activated, weights[10], preferred_element_type=jnp.float32)  126 us
    psum x1, blocking collectives, shards(): lax.psum((totals[0], totals[1], totals[2], totals[3], totals[4], totals[5...  118 us
    dot_general x3, matrix products, layer_backward(): jnp.dot(second_low, weights[8], preferred_element_type=jnp.float32)  111 us
    all_to_all x2, blocking collectives, spectral_round(): lax.all_to_all(spectrum, 'slab', split_axis=1, concat_axis=0, tiled=True)  98.5 us
    another operation x15, local copies, waits for them, and re-layouts  87.6 us
    unnamed x539, local copies, waits for them, and re-layouts  74.2 us
    convert_element_type x4, other arithmetic, spectral_forward(): active = smooth_gelu(first).astype(jnp.bfloat16)  70.1 us
  transfers between devices with their start and end apart: 19, of which 13 were waited for; matrix products, arithmetic and copies ran while one was open for 22% of the time, Pallas kernels for 0%

commit v1 on v0

v1 whole, which is shorter than its diff:
```python
import math

import jax
import jax.numpy as jnp
from jax import lax
from jax.sharding import Mesh, PartitionSpec as P

BLOCKS = 8
LAT = 90
EPSILON = 1e-05
SHRINK = 0.01
SOFTNESS = 0.1
HIGHEST = lax.Precision.HIGHEST
ROWS_AXES = ("section", "lane")
ALL = ("section", "half", "lane")
SLAB = ("half", "lane")
F32 = jnp.float32
BF16 = jnp.bfloat16


def layer_norm(values, gain, shift):
    center = values - jnp.mean(values, axis=-1, keepdims=True)
    spread = jnp.mean(center * center, axis=-1, keepdims=True)
    return center * lax.rsqrt(spread + EPSILON) * gain + shift


def smooth_gelu(values):
    return jax.nn.gelu(values, approximate=False)


def longitude_tables(longitudes, padded):
    column = jnp.arange(longitudes, dtype=jnp.int32)[:, None]
    frequency = jnp.arange(padded, dtype=jnp.int32)[None, :]
    angle = (column * frequency % longitudes).astype(F32) * (2.0 * math.pi / longitudes)
    usable = (frequency <= longitudes // 2).astype(F32) / math.sqrt(longitudes)
    forward = jnp.stack([jnp.cos(angle) * usable, -jnp.sin(angle) * usable], axis=-1)
    doubled = jnp.where((frequency == 0) | (frequency == longitudes // 2), 1.0, 2.0).astype(F32)
    inverse = jnp.transpose(forward * doubled[:, :, None], (1, 2, 0))
    return (forward, inverse)


def latitude_table(latitudes):
    frequency = jnp.arange(latitudes, dtype=jnp.int32)[:, None]
    position = jnp.arange(latitudes, dtype=jnp.int32)[None, :]
    angle = (frequency * position % latitudes).astype(F32) * (2.0 * math.pi / latitudes)
    cosine = jnp.cos(angle) / math.sqrt(latitudes)
    sine = jnp.sin(angle) / math.sqrt(latitudes)
    return jnp.stack([jnp.stack([cosine, sine], axis=-1), jnp.stack([-sine, cosine], axis=-1)], axis=1)


def latitude_forward(rows_first, layout):
    live = layout["live"]
    used = rows_first[:live].reshape((live // LAT, LAT) + rows_first.shape[1:])
    return jnp.einsum("kdrc,frmce->fkmde", layout["latitude"], used, precision=HIGHEST)


def latitude_inverse(spectral, layout):
    back = jnp.einsum("kdrc,fkmde->frmce", layout["latitude"], spectral, precision=HIGHEST)
    back = back.reshape((-1,) + back.shape[2:])
    return jnp.pad(back, ((0, layout["rows"] - back.shape[0]), (0, 0), (0, 0), (0, 0)))


def block_matrix(weight):
    upper = jnp.stack([weight[0], weight[1]], axis=2)
    lower = jnp.stack([-weight[1], weight[0]], axis=2)
    return jnp.stack([upper, lower], axis=1)


def mix_forward(inputs, matrix, bias):
    product = jnp.einsum("xmcbi,bcidj->xmdbj", inputs, matrix, preferred_element_type=F32)
    return product + bias.astype(F32)


def mix_backward(inputs, grad_output, matrix):
    grad_input = jnp.einsum("xmdbj,bcidj->xmcbi", grad_output, matrix, preferred_element_type=F32)
    outer = jnp.einsum("xmcbi,xmdbj->bcidj", inputs, grad_output, preferred_element_type=F32)
    grad_weight = jnp.stack(
        [outer[:, 0, :, 0] + outer[:, 1, :, 1], outer[:, 0, :, 1] - outer[:, 1, :, 0]]
    )
    grad_bias = jnp.sum(grad_output.astype(F32), axis=(0, 1))
    return (grad_input, grad_weight, grad_bias)


def to_modes(spectrum, layout):
    rows, modes, _, width = spectrum.shape
    lanes, per = layout["lanes"], layout["per"]
    parts = spectrum.astype(BF16).reshape(rows, lanes, per, 2, 2, width // 2)
    parts = jnp.transpose(parts, (4, 1, 0, 2, 3, 5)).reshape(2 * lanes, rows * per, width)
    moved = lax.all_to_all(parts, ROWS_AXES, 0, 0, tiled=True)
    return moved.reshape(2 * lanes * rows, per, 2, width // 2)


def to_rows(modes, layout):
    total, per, _, half_width = modes.shape
    lanes = layout["lanes"]
    rows = total // (2 * lanes)
    parts = modes.astype(BF16).reshape(2 * lanes, rows * per, 2 * half_width)
    moved = lax.all_to_all(parts, ROWS_AXES, 0, 0, tiled=True)
    moved = moved.reshape(2, lanes, rows, per, 2, half_width)
    return jnp.transpose(moved, (2, 1, 3, 4, 0, 5)).reshape(rows, lanes * per, 2, 2 * half_width)


def layer_forward(values, weights, layout):
    normed = layer_norm(values, weights[0].astype(F32), weights[1].astype(F32))
    spectrum = jnp.einsum("rnd,nkc->rkcd", normed, layout["forward"], precision=HIGHEST)
    received = to_modes(spectrum, layout)
    mode_low = latitude_forward(received.astype(F32), layout).astype(BF16).reshape(layout["view"])
    first = mix_forward(mode_low, weights[2], weights[3])
    active = smooth_gelu(first).astype(BF16)
    second = mix_forward(active, weights[4], weights[5])
    shrunk = (second - SHRINK * jnp.tanh(second / SOFTNESS)) * layout["modes"]
    back = to_rows(latitude_inverse(shrunk.reshape(layout["spectral"]), layout), layout)
    filtered = jnp.einsum("rkcd,kcn->rnd", back.astype(F32), layout["inverse"], precision=HIGHEST)
    mixed = (filtered + normed + values).reshape(-1, values.shape[-1])
    second_norm = layer_norm(mixed, weights[6].astype(F32), weights[7].astype(F32)).astype(BF16)
    hidden = jnp.dot(second_norm, weights[8], preferred_element_type=F32) + weights[9].astype(F32)
    activated = smooth_gelu(hidden).astype(BF16)
    output = jnp.dot(activated, weights[10], preferred_element_type=F32)
    output = (output + weights[11].astype(F32) + mixed).reshape(values.shape)
    output = (output * layout["live_rows"]).astype(BF16)
    return output, (values, mode_low, first, active, second, mixed, second_norm, hidden, activated)


def layer_backward(saved, grad_out, weights, layout):
    values, mode_low, first, active, second, mixed, second_norm, hidden, activated = saved
    width = values.shape[-1]
    grad_flat = grad_out.reshape(-1, width)
    gelu_pull = jax.vjp(smooth_gelu, hidden)[1]
    grad_activated = jnp.einsum("td,fd->tf", grad_flat, weights[10], preferred_element_type=F32)
    grad_hidden = gelu_pull(grad_activated)[0].astype(BF16)
    grad_second_norm = jnp.einsum("tf,df->td", grad_hidden, weights[8], preferred_element_type=F32)
    norm_pull = jax.vjp(layer_norm, mixed, weights[6].astype(F32), weights[7].astype(F32))[1]
    grad_mixed, grad_gain_two, grad_shift_two = norm_pull(grad_second_norm)
    grad_mixed = (grad_mixed + grad_flat.astype(F32)).reshape(values.shape)
    grad_returned = jnp.einsum("rnd,kcn->rkcd", grad_mixed, layout["inverse"], precision=HIGHEST)
    grad_modes = to_modes(grad_returned, layout)
    grad_dense_out = jnp.einsum("tf,td->fd", activated, grad_flat, preferred_element_type=F32)
    grad_dense_out_bias = jnp.sum(grad_flat.astype(F32), axis=0)
    grad_dense_in = jnp.einsum("td,tf->df", second_norm, grad_hidden, preferred_element_type=F32)
    grad_dense_in_bias = jnp.sum(grad_hidden.astype(F32), axis=0)
    grad_shrunk = latitude_forward(grad_modes.astype(F32), layout).reshape(layout["view"])
    grad_shrunk = grad_shrunk * layout["modes"]
    slope = jnp.tanh(second / SOFTNESS)
    grad_second = (grad_shrunk * (1.0 - SHRINK / SOFTNESS * (1.0 - slope * slope))).astype(BF16)
    grad_active, grad_two, grad_bias_two = mix_backward(active, grad_second, weights[4])
    grad_first = jax.vjp(smooth_gelu, first)[1](grad_active)[0].astype(BF16)
    grad_mode, grad_one, grad_bias_one = mix_backward(mode_low, grad_first, weights[2])
    back = to_rows(latitude_inverse(grad_mode.reshape(layout["spectral"]), layout), layout)
    front_pull = jax.vjp(layer_norm, values, weights[0].astype(F32), weights[1].astype(F32))[1]
    grad_normed = jnp.einsum("rkcd,nkc->rnd", back.astype(F32), layout["forward"], precision=HIGHEST)
    grad_values, grad_gain_one, grad_shift_one = front_pull(grad_normed + grad_mixed)
    grad_values = grad_values + grad_mixed
    small = (grad_gain_one, grad_shift_one, grad_gain_two, grad_shift_two, grad_dense_in_bias, grad_dense_out_bias)
    return grad_values.astype(BF16), small, (grad_one, grad_two), (grad_bias_one, grad_bias_two), (grad_dense_in, grad_dense_out)


def both_layers(item, core):
    other = lax.ppermute(item, "section", [(0, 1), (1, 0)])
    return (jnp.where(core == 0, item, other), jnp.where(core == 0, other, item))


def fetch(pair, core, half):
    own = lax.dynamic_index_in_dim(pair, half, 0, keepdims=False)
    give = lax.dynamic_index_in_dim(pair, 1 - half, 0, keepdims=False)
    got = lax.ppermute(give, ("section", "half"), [(0, 1), (3, 2)])
    return jnp.where(core == half, own, got)


def deliver(layer_zero, layer_one, core):
    parts = []
    for micro in range(2):
        first = lax.ppermute(layer_zero, ("section", "half"), [(micro, 0), (2 + micro, 1)])
        second = lax.ppermute(layer_one, ("section", "half"), [(micro, 2), (2 + micro, 3)])
        parts.append(jnp.where(core == 0, first, second))
    return jnp.stack(parts)[None]


def shards(tokens, cotangent, *params):
    core = lax.axis_index("section")
    half = lax.axis_index("half")
    lane = lax.axis_index("lane")
    lanes = lax.axis_size("lane")
    micro_count, local_rows, longitudes, width = tokens.shape
    total_rows = local_rows * lanes * 2
    fields = total_rows // LAT
    live = fields * LAT
    mode_count = longitudes // 2 + 1
    per = (mode_count + lanes - 1) // lanes
    forward_table, inverse_table = longitude_tables(longitudes, per * lanes)
    mode_ids = lane * per + jnp.arange(per, dtype=jnp.int32)
    row_ids = (core * lanes + lane) * local_rows + jnp.arange(local_rows, dtype=jnp.int32)
    row_mask = row_ids < live
    blocks = BLOCKS // 2
    layout = {
        "forward": forward_table,
        "inverse": inverse_table,
        "latitude": latitude_table(LAT),
        "live": live,
        "rows": total_rows,
        "lanes": lanes,
        "per": per,
        "modes": (mode_ids < mode_count).astype(F32).reshape(1, per, 1, 1, 1),
        "live_rows": row_mask.astype(F32).reshape(local_rows, 1, 1),
        "view": (fields * LAT, per, 2, blocks, width // BLOCKS),
        "spectral": (fields, LAT, per, 2, width // 2),
    }
    values = fetch(tokens, core, half)
    grad_out = fetch(cotangent, core, half)
    grad_out = jnp.where(row_mask.reshape(local_rows, 1, 1), grad_out, jnp.zeros_like(grad_out))
    pairs = [both_layers(item[0], core) for item in params]
    layers = []
    for level in range(2):
        w = [pair[level] for pair in pairs]
        for at in (2, 4):
            part = lax.dynamic_slice_in_dim(w[at], core * blocks, blocks, 1)
            w[at] = block_matrix(part)
        for at in (3, 5):
            w[at] = lax.dynamic_slice_in_dim(w[at], core * blocks, blocks, 1)
        layers.append(w)
    out_one, saved_one = layer_forward(values.astype(F32), layers[0], layout)
    out_two, saved_two = layer_forward(out_one.astype(F32), layers[1], layout)
    grad_two, small_two, spec_two, bias_two, dense_two = layer_backward(saved_two, grad_out, layers[1], layout)
    grad_one, small_one, spec_one, bias_one, dense_one = layer_backward(saved_one, grad_two, layers[0], layout)
    outputs = deliver(out_one, out_two, core)
    input_grads = deliver(grad_one, grad_two, core)

    def spread_bias(item):
        full = jnp.zeros((2, BLOCKS, width // BLOCKS), F32)
        return lax.dynamic_update_slice_in_dim(full, item, core * blocks, 1)

    small = [a.reshape(-1) for a in small_one] + [spread_bias(b).reshape(-1) for b in bias_one]
    small = small + [a.reshape(-1) for a in small_two] + [spread_bias(b).reshape(-1) for b in bias_two]
    sizes = [a.shape[0] for a in small]
    merged = lax.psum(jnp.concatenate(small), ALL)
    ends = [sum(sizes[: i + 1]) for i in range(len(sizes))]
    pieces = [merged[e - s : e] for e, s in zip(ends, sizes)]
    pieces = [jnp.where(core == 0, a, b)[None] for a, b in zip(pieces[:8], pieces[8:])]
    spec = lax.psum(jnp.stack([jnp.stack(spec_one), jnp.stack(spec_two)]), SLAB)
    given = lax.ppermute(jnp.where(core == 0, spec[1], spec[0]), "section", [(0, 1), (1, 0)])
    kept = jnp.where(core == 0, spec[0], spec[1])
    spec = jnp.where(core == 0, jnp.concatenate([kept, given], 2), jnp.concatenate([given, kept], 2))
    dense = []
    for at in range(2):
        a = lax.psum(dense_one[at].astype(BF16), ALL)
        b = lax.psum(dense_two[at].astype(BF16), ALL)
        dense.append(jnp.where(core == 0, a, b).astype(F32)[None])
    shape = (1, 2, BLOCKS, width // BLOCKS)
    return (
        outputs, input_grads, pieces[0], pieces[1], spec[0][None], pieces[6].reshape(shape),
        spec[1][None], pieces[7].reshape(shape), pieces[2], pieces[3], dense[0], pieces[4], dense[1], pieces[5],
    )


def solution(mesh):
    devices = mesh.devices
    slabs = devices.shape[1]
    wide = Mesh(devices.reshape(2, 2, slabs // 2), ALL)
    rows = P(None, ("half", "lane"))
    own = P("section")
    return jax.shard_map(
        shards,
        mesh=wide,
        in_specs=(rows, rows) + (own,) * 12,
        out_specs=(P("section", None, ("half", "lane")),) * 2 + (own,) * 12,
        check_vma=False,
    )
```

time: 2300 us -> 1580 us (0.69)
  matrix products: 628 us -> 329 us
  blocking collectives: 311 us -> 33 us
  waiting for transfers between devices: 457 us -> 685 us
  local copies, waits for them, and re-layouts: 472 us -> 296 us
  other arithmetic: 262 us -> 96 us
  starting transfers between devices: 135 us -> 110 us
    psum x1 -> x3, waiting for transfers between devices: 271 us -> 564 us  [the longest x1 302 us: shards(): a = lax.psum(dense_one[at].astype(BF16), ALL)]
    dot_general x45 -> x22, matrix products: 508 us -> 255 us  [the longest x2 81.1 us: layer_forward(): jnp.dot(second_norm, weights[8], preferred_element_type=F32)]
    all_to_all x4 -> x1, blocking collectives: 194 us -> 33 us  [to_modes(): moved = lax.all_to_all(parts, ROWS_AXES, 0, 0, tiled=True)]
    psum x1 -> x0, blocking collectives: 118 us -> none  [shards(): lax.psum((totals[0], totals[1], totals[2], totals[3], totals[4], totals[5...]
    all_to_all x14 -> x7, waiting for transfers between devices: 181 us -> 70 us  [the longest x3 43.6 us: to_modes(): moved = lax.all_to_all(parts, ROWS_AXES, 0, 0, tiled=True)]
    all_to_all x14 -> x7, starting transfers between devices: 127 us -> 59 us  [the longest x3 36.8 us: to_modes(): moved = lax.all_to_all(parts, ROWS_AXES, 0, 0, tiled=True)]
    convert_element_type x15 -> x14, other arithmetic: 88 us -> 36.7 us  [the longest x2 23 us: layer_forward(): active = smooth_gelu(first).astype(BF16)]
    unnamed x539 -> x337, local copies, waits for them, and re-layouts: 74.2 us -> 25.1 us
  transfers between devices with their start and end apart: 19 -> 33, of which waited for: 13 -> 15; matrix products, arithmetic and copies ran while one was open for 22% -> 17% of each run, Pallas kernels for 0% -> 0%
where the time goes in v1:
time: 1580 us; the launch traced here: 1570 us
  waiting for transfers between devices  685 us (43%)
  matrix products  329 us (21%)
  local copies, waits for them, and re-layouts  296 us (19%)
  starting transfers between devices  110 us (7%)
  other arithmetic  96 us (6%)
  blocking collectives  33 us (2%)
  between operations  16.6 us (1%)
    psum x1, waiting for transfers between devices, shards(): a = lax.psum(dense_one[at].astype(BF16), ALL)  302 us
    psum x1, waiting for transfers between devices, shards(): merged = lax.psum(jnp.concatenate(small), ALL)  163 us
    psum x1, waiting for transfers between devices, shards(): spec = lax.psum(jnp.stack([jnp.stack(spec_one), jnp.stack(spec_two)]), SLAB)  99.3 us
    dot_general x2, matrix products, layer_forward(): jnp.dot(second_norm, weights[8], preferred_element_type=F32)  81.1 us
    another operation x16, local copies, waits for them, and re-layouts  57.8 us
    ppermute x2, waiting for transfers between devices, fetch(): got = lax.ppermute(give, ('section', 'half'), [(0, 1), (3, 2)])  50.2 us
    all_to_all x3, waiting for transfers between devices, to_modes(): moved = lax.all_to_all(parts, ROWS_AXES, 0, 0, tiled=True)  43.6 us
    dot_general x2, matrix products, layer_backward(): jnp.einsum('td,fd->tf', grad_flat, weights[10], preferred_element_type=F32)  37.5 us
  transfers between devices with their start and end apart: 33, of which 15 were waited for; matrix products, arithmetic and copies ran while one was open for 17% of the time, Pallas kernels for 0%

profile of v1, /device:TPU:0, one launch (start us, length us, event | category | flops | bytes accessed | tf_op | source)
XLA Modules:
  0.0 1565.5 jit_solution(3796427598576783417)
XLA Ops:
  7.2 17.1 %constant_dynamic-slice_fusion.1 = (bf16[1,6,180,768]{3,0,2,1:T(2,128)(2,1)}, bf16[1,6,180,768]{3,0,2,1:T(2,128)(2,1)}, bf16[1,6,180,768]{3,0,2,1:T(2,128)(2,1)S(1)}, bf16[1,6,180,768]{3,0,2,1:T(2,128)(2,1)}) fusion(bf16[2,6,180,768]{3,0,2,1:T(2,128)(2,1)} %param.15, s32[]{:T(128)S(6)} %select_n.336, s32[]{:T(128)S(6)} %select_n.337, ...), kind=kLoop, calls=%fused_computation.419 | loop fusion | bytes 13271048 | tf_op jit(solution)/shard_map/jit(dynamic_index_in_dim)/dynamic_slice | solution.py:163
  34.2 17.0 %collective-permute-done.2 = bf16[6,180,768]{2,1,0:T(8,128)(2,1)S(1)} collective-permute-done((bf16[6,180,768]{2,1,0:T(8,128)(2,1)}, bf16[6,180,768]{2,1,0:T(8,128)(2,1)S(1)}, u32[]{:S(2)}, u32[]{:S(2)}) %collective-permute-start.2) | collective-permute-done | bytes 1658912 | tf_op jit(solution)/shard_map/ppermute | solution.py:165
  73.1 23.4 %all-to-all-start = ((bf16[16,72,768]{2,1,0:T(8,128)(2,1)}), bf16[16,72,768]{2,1,0:T(8,128)(2,1)}, u32[]{:S(2)}, u32[]{:S(2)}) async-start(bf16[16,72,768]{2,1,0:T(8,128)(2,1)} %reshape.865), calls=%async_computation | async-start | bytes 3538944 | tf_op jit(solution)/shard_map/all_to_all | solution.py:89
  102.5 16.7 %all-to-all-done = bf16[16,72,768]{2,1,0:T(8,128)(2,1)} async-done(((bf16[16,72,768]{2,1,0:T(8,128)(2,1)}), bf16[16,72,768]{2,1,0:T(8,128)(2,1)}, u32[]{:S(2)}, u32[]{:S(2)}) %all-to-all-start) | async-done | bytes 1769504 | tf_op jit(solution)/shard_map/all_to_all | solution.py:89
  140.7 11.4 fusion.82
  192.5 18.2 %all-to-all-done.1 = bf16[16,72,768]{2,1,0:T(8,128)(2,1)} async-done(((bf16[16,72,768]{2,1,0:T(8,128)(2,1)}), bf16[16,72,768]{2,1,0:T(8,128)(2,1)}, u32[]{:S(2)}, u32[]{:S(2)}) %all-to-all-start.1) | async-done | bytes 1769504 | tf_op jit(solution)/shard_map/all_to_all | solution.py:98
  236.3 40.2 %multiply_convert_fusion.1 = (bf16[1080,3072]{1,0:T(8,128)(2,1)S(1)}, f32[1080,3072]{1,0:T(8,128)}, f32[1080,3072]{1,0:T(8,128)}) fusion(f32[3072]{0:T(1024)S(1)} %get-tuple-element.154, bf16[768,3072]{1,0:T(8,128)(2,1)} %collective-permute-done.9, pred[]{:T(512)S(6)} %eq.26, bf16[1,768,3072]{2,1,0:T(8,128)(2,1)} %param.24, f32[1080,768]{1,0:T(8,128)} %reshape.873, ...), kind=kOutput, calls=%fused_computation.23 | convolution fusion | flops 5321558016 | bytes 45959616 | tf_op jit(solution)/shard_map/dot_general | solution.py:116
  276.6 12.2 convert_reduce_fusion.7
  322.2 22.3 %all-to-all-done.2 = bf16[16,72,768]{2,1,0:T(8,128)(2,1)S(1)} async-done(((bf16[16,72,768]{2,1,0:T(8,128)(2,1)}), bf16[16,72,768]{2,1,0:T(8,128)(2,1)S(1)}, u32[]{:S(2)}, u32[]{:S(2)}) %all-to-all-start.2) | async-done | bytes 1769504 | tf_op jit(solution)/shard_map/all_to_all | solution.py:89
  360.2 11.6 fusion.83
  411.8 33.1 %collective-permute-done.17 = bf16[6,180,768]{2,1,0:T(8,128)(2,1)S(1)} collective-permute-done((bf16[6,180,768]{2,1,0:T(8,128)(2,1)S(1)}, bf16[6,180,768]{2,1,0:T(8,128)(2,1)S(1)}, u32[]{:S(2)}, u32[]{:S(2)}) %collective-permute-start.17) | collective-permute-done | bytes 1658912 | tf_op jit(solution)/shard_map/ppermute | solution.py:165
  463.8 40.9 %multiply_convert_fusion = (bf16[1080,3072]{1,0:T(8,128)(2,1)}, f32[1080,3072]{1,0:T(8,128)}, f32[1080,3072]{1,0:T(8,128)}) fusion(f32[3072]{0:T(1024)S(1)} %copy-done.127, bf16[768,3072]{1,0:T(8,128)(2,1)} %collective-permute-done.9, pred[]{:T(512)S(6)} %eq.26, bf16[1,768,3072]{2,1,0:T(8,128)(2,1)} %param.24, f32[1080,768]{1,0:T(8,128)} %reshape.884, ...), kind=kOutput, calls=%fused_computation.10 | convolution fusion | flops 5321558016 | bytes 45959616 | tf_op jit(solution)/shard_map/dot_general | solution.py:116
  504.7 19.5 %convert_reduce_fusion = (f32[3072]{0:T(1024)}, bf16[1080,3072]{1,0:T(8,128)(2,1)}) fusion(f32[1080,3072]{1,0:T(8,128)} %get-tuple-element.101, f32[1080,3072]{1,0:T(8,128)} %get-tuple-element.182, bf16[1080,768]{1,0:T(8,128)(2,1)} %reshape.886, bf16[3072,768]{1,0:T(8,128)(2,1)} %collective-permute-done.11, pred[]{:T(512)S(6)} %eq.26, ...), kind=kOutput, calls=%fused_computation.6 | convolution fusion | flops 5151519744 | bytes 44285952 | tf_op jit(solution)/shard_map/td,fd->tf/dot_general | solution.py:129
  524.2 12.2 multiply_reduce_fusion.2
  556.7 33.0 %all_to_all.40 = bf16[16,72,768]{2,1,0:T(8,128)(2,1)S(1)} all-to-all(bf16[16,72,768]{2,1,0:T(8,128)(2,1)S(1)} %reshape.889), channel_id=1, replica_groups=mesh['section'=2,'half'=2,'lane'=8] {'section','lane'}, dimensions={0} | all-to-all | bytes 3538944 | tf_op jit(solution)/shard_map/all_to_all | solution.py:89
  644.7 11.7 convolution_convert_fusion.2
  693.1 18.0 %convert_reduce_fusion.1 = (f32[3072]{0:T(1024)}, bf16[1080,3072]{1,0:T(8,128)(2,1)}) fusion(f32[1080,3072]{1,0:T(8,128)} %get-tuple-element.105, f32[1080,3072]{1,0:T(8,128)} %get-tuple-element.175, bf16[1080,768]{1,0:T(8,128)(2,1)} %reshape.897, bf16[3072,768]{1,0:T(8,128)(2,1)} %collective-permute-done.11, pred[]{:T(512)S(6)} %eq.26, ...), kind=kOutput, calls=%fused_computation.7 | convolution fusion | flops 5151519744 | bytes 44285952 | tf_op jit(solution)/shard_map/td,fd->tf/dot_general | solution.py:129
  842.8 12.2 convolution_convert_fusion.3
  885.9 11.4 convolution_convert_fusion.1
  897.2 14.2 collective-permute-start.13
  911.4 12.1 fusion.51
  949.8 99.3 %all-reduce.11.cloned.1.call-done = f32[2,2,2,4,96,96]{5,4,3,2,1,0:T(8,128)} async-done(((f32[2,2,2,4,96,96]{5,4,3,2,1,0:T(8,128)}), f32[2,2,2,4,96,96]{5,4,3,2,1,0:T(8,128)}) %all-reduce.11.cloned.1.call-update) | async-done | bytes 1179664 | tf_op jit(solution)/shard_map/psum | solution.py:238
  1068.4 162.6 %all-reduce.9.cloned.1.call-done = f32[19968]{0:T(1024)} async-done(((f32[19968]{0:T(1024)}), f32[19968]{0:T(1024)}) %all-reduce.9.cloned.1.call-update) | async-done | bytes 79888 | tf_op jit(solution)/shard_map/psum | solution.py:234
  1244.6 302.0 %all-reduce.13.cloned.1.call-done = (bf16[768,3072]{1,0:T(8,128)(2,1)}, bf16[768,3072]{1,0:T(8,128)(2,1)}, bf16[3072,768]{1,0:T(8,128)(2,1)}, bf16[3072,768]{1,0:T(8,128)(2,1)}) async-done(((bf16[768,3072]{1,0:T(8,128)(2,1)}, bf16[768,3072]{1,0:T(8,128)(2,1)}, bf16[3072,768]{1,0:T(8,128)(2,1)}, bf16[3072,768]{1,0:T(8,128)(2,1)}), (bf16[768,3072]{1,0:T(8,128)(2,1)}, bf16[768,3072]{1,0:T(8,128)(2,1)}, ...) | async-done | bytes 18874384 | tf_op jit(solution)/shard_map/psum | solution.py:244
  (622 shorter events, 576.6 us)
Async XLA Ops:
  25.7 25.5 %collective-permute-start.2 = (bf16[6,180,768]{2,1,0:T(8,128)(2,1)}, bf16[6,180,768]{2,1,0:T(8,128)(2,1)S(1)}, u32[]{:S(2)}, u32[]{:S(2)}) collective-permute-start(bf16[6,180,768]{2,1,0:T(8,128)(2,1)} %bitcast.654), channel_id=1, source_target_pairs={{0,8},{24,16},{1,9},{25,17},{2,10},{26,18},{3,11},{27,19},{4,12},{... | collective-permute-start | bytes 4976648 | tf_op jit(solution)/shard_map/ppermute | solution.py:165
  73.1 46.2 %all-to-all-start = ((bf16[16,72,768]{2,1,0:T(8,128)(2,1)}), bf16[16,72,768]{2,1,0:T(8,128)(2,1)}, u32[]{:S(2)}, u32[]{:S(2)}) async-start(bf16[16,72,768]{2,1,0:T(8,128)(2,1)} %reshape.865), calls=%async_computation | async-start | bytes 3538944 | tf_op jit(solution)/shard_map/all_to_all | solution.py:89
  97.0 3.3 collective-permute-start.1
  97.6 138.6 %collective-permute-start.9 = (bf16[768,3072]{1,0:T(8,128)(2,1)}, bf16[768,3072]{1,0:T(8,128)(2,1)}, u32[]{:S(2)}, u32[]{:S(2)}) collective-permute-start(bf16[768,3072]{1,0:T(8,128)(2,1)} %bitcast.683), channel_id=1, source_target_pairs={{0,16},{16,0},{1,17},{17,1},{2,18},{18,2},{3,19},{19,3},{4,20},{20... | collective-permute-start | bytes 14155784 | tf_op jit(solution)/shard_map/ppermute | solution.py:158
  182.1 28.6 %all-to-all-start.1 = ((bf16[16,72,768]{2,1,0:T(8,128)(2,1)}), bf16[16,72,768]{2,1,0:T(8,128)(2,1)}, u32[]{:S(2)}, u32[]{:S(2)}) async-start(bf16[16,72,768]{2,1,0:T(8,128)(2,1)} %reshape.870), calls=%async_computation.1 | async-start | bytes 3538944 | tf_op jit(solution)/shard_map/all_to_all | solution.py:98
  189.5 87.0 %collective-permute-start.11 = (bf16[3072,768]{1,0:T(8,128)(2,1)}, bf16[3072,768]{1,0:T(8,128)(2,1)}, u32[]{:S(2)}, u32[]{:S(2)}) collective-permute-start(bf16[3072,768]{1,0:T(8,128)(2,1)} %bitcast.684), channel_id=1, source_target_pairs={{0,16},{16,0},{1,17},{17,1},{2,18},{18,2},{3,19},{19,3},{4,20},{20... | collective-permute-start | bytes 14155784 | tf_op jit(solution)/shard_map/ppermute | solution.py:158
  315.6 28.9 %all-to-all-start.2 = ((bf16[16,72,768]{2,1,0:T(8,128)(2,1)}), bf16[16,72,768]{2,1,0:T(8,128)(2,1)S(1)}, u32[]{:S(2)}, u32[]{:S(2)}) async-start(bf16[16,72,768]{2,1,0:T(8,128)(2,1)} %reshape.876), calls=%async_computation.2 | async-start | bytes 3538944 | tf_op jit(solution)/shard_map/all_to_all | solution.py:89
  399.6 48.7 %all-to-all-start.3 = ((bf16[16,72,768]{2,1,0:T(8,128)(2,1)}), bf16[16,72,768]{2,1,0:T(8,128)(2,1)}, u32[]{:S(2)}, u32[]{:S(2)}) async-start(bf16[16,72,768]{2,1,0:T(8,128)(2,1)} %reshape.881), calls=%async_computation.3 | async-start | bytes 3538944 | tf_op jit(solution)/shard_map/all_to_all | solution.py:98
  405.8 39.1 %collective-permute-start.17 = (bf16[6,180,768]{2,1,0:T(8,128)(2,1)S(1)}, bf16[6,180,768]{2,1,0:T(8,128)(2,1)S(1)}, u32[]{:S(2)}, u32[]{:S(2)}) collective-permute-start(bf16[6,180,768]{2,1,0:T(8,128)(2,1)S(1)} %bitcast.673), channel_id=1, source_target_pairs={{0,8},{24,16},{1,9},{25,17},{2,10},{26,18},{3,11},{27,19},{4,12},{... | collective-permute-start | bytes 4976648 | tf_op jit(solution)/shard_map/ppermute | solution.py:165
  637.0 27.6 %all-to-all-start.5 = ((bf16[16,72,768]{2,1,0:T(8,128)(2,1)}), bf16[16,72,768]{2,1,0:T(8,128)(2,1)}, u32[]{:S(2)}, u32[]{:S(2)}) async-start(bf16[16,72,768]{2,1,0:T(8,128)(2,1)} %reshape.894), calls=%async_computation.5 | async-start | bytes 3538944 | tf_op jit(solution)/shard_map/all_to_all | solution.py:98
  746.9 30.0 %all-to-all-start.6 = ((bf16[16,72,768]{2,1,0:T(8,128)(2,1)}), bf16[16,72,768]{2,1,0:T(8,128)(2,1)}, u32[]{:S(2)}, u32[]{:S(2)}) async-start(bf16[16,72,768]{2,1,0:T(8,128)(2,1)} %reshape.900), calls=%async_computation.6 | async-start | bytes 3538944 | tf_op jit(solution)/shard_map/all_to_all | solution.py:89
  837.2 28.3 %all-to-all-start.7 = ((bf16[16,72,768]{2,1,0:T(8,128)(2,1)}), bf16[16,72,768]{2,1,0:T(8,128)(2,1)}, u32[]{:S(2)}, u32[]{:S(2)}) async-start(bf16[16,72,768]{2,1,0:T(8,128)(2,1)} %reshape.905), calls=%async_computation.7 | async-start | bytes 3538944 | tf_op jit(solution)/shard_map/all_to_all | solution.py:98
  842.7 206.4 %all-reduce.11.cloned.1.call-start = ((), (), s32[]{:S(2)}) async-start(), calls=%async_computation.9 | async-start | bytes 3145728 | tf_op jit(solution)/shard_map/psum | solution.py:238
  864.0 367.0 %all-reduce.9.cloned.1.call-start = ((), (), s32[]{:S(2)}) async-start(), calls=%async_computation.8 | async-start | bytes 163840 | tf_op jit(solution)/shard_map/psum | solution.py:234
  885.8 660.8 %all-reduce.13.cloned.1.call-start = ((), (), s32[]{:S(2)}) async-start(), calls=%async_computation.10 | async-start | bytes 37748736 | tf_op jit(solution)/shard_map/psum | solution.py:244
  897.2 39.1 %collective-permute-start.13 = (bf16[6,180,768]{2,1,0:T(8,128)(2,1)}, bf16[6,180,768]{2,1,0:T(8,128)(2,1)}, u32[]{:S(2)}, u32[]{:S(2)}) collective-permute-start(bf16[6,180,768]{2,1,0:T(8,128)(2,1)} %multiply_convert_fusion.5), channel_id=1, source_target_pairs={{0,0},{16,8},{1,1},{17,9},{2,2},{18,10},{3,3},{19,11},{4,4},{20,12... | collective-permute-start | bytes 4976648 | tf_op jit(solution)/shard_map/ppermute | solution.py:172
  931.6 4.8 collective-permute-start.14
  933.1 124.4 %collective-permute-start.15 = (bf16[6,180,768]{2,1,0:T(8,128)(2,1)}, bf16[6,180,768]{2,1,0:T(8,128)(2,1)}, u32[]{:S(2)}, u32[]{:S(2)}) collective-permute-start(bf16[6,180,768]{2,1,0:T(8,128)(2,1)} %multiply_convert_fusion.5), channel_id=1, source_target_pairs={{8,0},{24,8},{9,1},{25,9},{10,2},{26,10},{11,3},{27,11},{12,4},{28... | collective-permute-start | bytes 4976648 | tf_op jit(solution)/shard_map/ppermute | solution.py:172
  934.4 123.1 %collective-permute-start.16 = (bf16[6,180,768]{2,1,0:T(8,128)(2,1)}, bf16[6,180,768]{2,1,0:T(8,128)(2,1)}, u32[]{:S(2)}, u32[]{:S(2)}) collective-permute-start(bf16[6,180,768]{2,1,0:T(8,128)(2,1)} %multiply_convert_fusion.4), channel_id=1, source_target_pairs={{8,16},{24,24},{9,17},{25,25},{10,18},{26,26},{11,19},{27,27},{12,... | collective-permute-start | bytes 4976648 | tf_op jit(solution)/shard_map/ppermute | solution.py:173
  939.3 298.9 %collective-permute-start.19 = (bf16[6,180,768]{2,1,0:T(8,128)(2,1)S(1)}, bf16[6,180,768]{2,1,0:T(8,128)(2,1)}, u32[]{:S(2)}, u32[]{:S(2)}) collective-permute-start(bf16[6,180,768]{2,1,0:T(8,128)(2,1)S(1)} %copy-done.27), channel_id=1, source_target_pairs={{0,16},{16,24},{1,17},{17,25},{2,18},{18,26},{3,19},{19,27},{4,20}... | collective-permute-start | bytes 4976648 | tf_op jit(solution)/shard_map/ppermute | solution.py:173
  1050.6 16.3 %collective-permute-start.22 = (f32[2,2,4,96,96]{4,3,2,1,0:T(8,128)S(1)}, f32[2,2,4,96,96]{4,3,2,1,0:T(8,128)S(1)}, u32[]{:S(2)}, u32[]{:S(2)}) collective-permute-start(f32[2,2,4,96,96]{4,3,2,1,0:T(8,128)S(1)} %get-tuple-element.117), channel_id=1, source_target_pairs={{0,16},{16,0},{1,17},{17,1},{2,18},{18,2},{3,19},{19,3},{4,20},{20... | collective-permute-start | bytes 1769480 | tf_op jit(solution)/shard_map/ppermute | solution.py:239
  1055.3 182.9 %collective-permute-start.18 = (bf16[6,180,768]{2,1,0:T(8,128)(2,1)}, bf16[6,180,768]{2,1,0:T(8,128)(2,1)S(1)}, u32[]{:S(2)}, u32[]{:S(2)}) collective-permute-start(bf16[6,180,768]{2,1,0:T(8,128)(2,1)} %add_convert_fusion.2), channel_id=1, source_target_pairs={{0,0},{16,8},{1,1},{17,9},{2,2},{18,10},{3,3},{19,11},{4,4},{20,12... | collective-permute-start | bytes 4976648 | tf_op jit(solution)/shard_map/ppermute | solution.py:172
  1059.1 179.2 %collective-permute-start.21 = (bf16[6,180,768]{2,1,0:T(8,128)(2,1)S(1)}, bf16[6,180,768]{2,1,0:T(8,128)(2,1)}, u32[]{:S(2)}, u32[]{:S(2)}) collective-permute-start(bf16[6,180,768]{2,1,0:T(8,128)(2,1)S(1)} %copy-done.27), channel_id=1, source_target_pairs={{8,16},{24,24},{9,17},{25,25},{10,18},{26,26},{11,19},{27,27},{12,... | collective-permute-start | bytes 4976648 | tf_op jit(solution)/shard_map/ppermute | solution.py:173
  1061.0 177.3 %collective-permute-start.20 = (bf16[6,180,768]{2,1,0:T(8,128)(2,1)}, bf16[6,180,768]{2,1,0:T(8,128)(2,1)}, u32[]{:S(2)}, u32[]{:S(2)}) collective-permute-start(bf16[6,180,768]{2,1,0:T(8,128)(2,1)} %add_convert_fusion.2), channel_id=1, source_target_pairs={{8,0},{24,8},{9,1},{25,9},{10,2},{26,10},{11,3},{27,11},{12,4},{28... | collective-permute-start | bytes 4976648 | tf_op jit(solution)/shard_map/ppermute | solution.py:172
  (166 other events, 3606.1 us)
Sparse Core Ops, SparseCore 0:
  864.1 185.0 all-reduce.10
  1055.6 175.3 all-reduce.8
  1239.2 307.3 all-reduce.12

commit v2 on v1

v2 whole, which is shorter than its diff:
```python
import functools
import math

import jax
import jax.numpy as jnp
import numpy as np
from jax import lax
from jax.experimental import pallas as pl
from jax.experimental.pallas import tpu as pltpu
from jax.sharding import Mesh, PartitionSpec as P

BLOCKS = 8
LAT = 90
EPSILON = 1e-05
SHRINK = 0.01
SOFTNESS = 0.1
ROWS_AXES = ("section", "lane")
ALL = ("section", "half", "lane")
SLAB = ("half", "lane")
F32 = jnp.float32
BF16 = jnp.bfloat16
VMEM_BYTES = 56 * 1024 * 1024


def split_table(table):
    high = np.asarray(table, np.float32).astype(jnp.bfloat16)
    low = (np.asarray(table, np.float64) - high.astype(np.float64)).astype(jnp.bfloat16)
    return np.concatenate([high, low], 0)


def longitude_tables(longitudes, padded):
    column = np.arange(longitudes)[:, None]
    frequency = np.arange(padded)[None, :]
    angle = (column * frequency % longitudes) * (2.0 * math.pi / longitudes)
    usable = (frequency <= longitudes // 2) / math.sqrt(longitudes)
    forward = np.concatenate([np.cos(angle) * usable, -np.sin(angle) * usable], 1)
    doubled = np.where((frequency == 0) | (frequency == longitudes // 2), 1.0, 2.0)
    inverse = forward * np.concatenate([doubled, doubled], 1)
    return (forward, inverse)


def latitude_table(rows, fields):
    index = np.arange(LAT)
    angle = (index[:, None] * index[None, :] % LAT) * (2.0 * math.pi / LAT)
    parts = []
    for wave in (np.cos(angle), np.sin(angle)):
        whole = np.zeros((rows, rows))
        for field in range(fields):
            span = slice(field * LAT, (field + 1) * LAT)
            whole[span, span] = wave / math.sqrt(LAT)
        parts.append(whole)
    return np.concatenate(parts, 0)


def dot(left, right):
    return jnp.dot(left, right, preferred_element_type=F32)


def dot_transposed(left, right):
    return lax.dot_general(left, right, (((1,), (1,)), ((), ())), preferred_element_type=F32)


def table_times_low(table_ref, low):
    count = table_ref.shape[0] // 2
    return dot(table_ref[:count, :], low) + dot(table_ref[count:, :], low)


def table_times(table_ref, value):
    count = table_ref.shape[0] // 2
    high = value.astype(BF16)
    rest = (value - high.astype(F32)).astype(BF16)
    return dot(table_ref[:count, :], high) + dot(table_ref[:count, :], rest) + dot(table_ref[count:, :], high)


def gelu_pair(value):
    size = jnp.abs(value) * math.sqrt(0.5)
    inverse = 1.0 / (1.0 + 0.3275911 * size)
    wave = jnp.exp(-0.5 * value * value)
    series = inverse * (0.254829592 + inverse * (-0.284496736 + inverse * (1.421413741 + inverse * (-1.453152027 + inverse * 1.061405429))))
    tail = 0.5 * series * wave
    share = jnp.where(value > 0, 1.0 - tail, tail)
    return value * share, share + value * wave * (1.0 / math.sqrt(2.0 * math.pi))


def centered(value):
    center = value - jnp.mean(value, axis=-1, keepdims=True)
    inverse = lax.rsqrt(jnp.mean(center * center, axis=-1, keepdims=True) + EPSILON)
    return center * inverse, inverse


def norm_back(grad, gain, unit, inverse):
    scaled = grad * gain
    return (scaled - jnp.mean(scaled, axis=-1, keepdims=True) - unit * jnp.mean(scaled * unit, axis=-1, keepdims=True)) * inverse


def scatter_modes(sent, spectrum, row, rows, lanes, per):
    width = spectrum.shape[1]
    half = width // 2
    modes = lanes * per
    for part in range(2):
        for lane in range(lanes):
            base = ((part * lanes + lane) * rows + row) * per
            for wave in range(2):
                piece = spectrum[wave * modes + lane * per : wave * modes + (lane + 1) * per, part * half : (part + 1) * half]
                sent[base : base + per, wave * half : (wave + 1) * half] = piece


def gather_modes(spectrum, back, row, rows, lanes, per):
    width = spectrum.shape[1]
    half = width // 2
    modes = lanes * per
    for part in range(2):
        for lane in range(lanes):
            base = ((part * lanes + lane) * rows + row) * per
            for wave in range(2):
                piece = back[base : base + per, wave * half : (wave + 1) * half]
                spectrum[wave * modes + lane * per : wave * modes + (lane + 1) * per, part * half : (part + 1) * half] = piece


def front_kernel(x_ref, gain_ref, shift_ref, table_ref, sent_ref, x32, sent32, *, rows, lanes, per):
    x32[...] = x_ref[...].astype(F32)
    longs = x_ref.shape[0] // rows
    for row in range(rows):
        unit, _ = centered(x32[row * longs : (row + 1) * longs, :])
        spectrum = table_times(table_ref, unit * gain_ref[...] + shift_ref[...])
        scatter_modes(sent32, spectrum, row, rows, lanes, per)
    sent_ref[...] = sent32[...].astype(BF16)


def middle_kernel(back_ref, x_ref, gain_ref, shift_ref, gain_two_ref, shift_two_ref, table_ref, mixed_ref, norm_ref, x32, back32, spectrum, norm32, *, rows, lanes, per):
    x32[...] = x_ref[...].astype(F32)
    back32[...] = back_ref[...].astype(F32)
    longs = x_ref.shape[0] // rows
    for row in range(rows):
        span = slice(row * longs, (row + 1) * longs)
        gather_modes(spectrum, back32, row, rows, lanes, per)
        value = x32[span, :]
        unit, _ = centered(value)
        mixed = table_times_low(table_ref, spectrum[...].astype(BF16)) + (unit * gain_ref[...] + shift_ref[...]) + value
        mixed_ref[span, :] = mixed
        unit, _ = centered(mixed)
        norm32[span, :] = unit * gain_two_ref[...] + shift_two_ref[...]
    norm_ref[...] = norm32[...].astype(BF16)


def latitude_forward(table_ref, value, count):
    half = value.shape[1] // 2
    both = table_times_low(table_ref, value)
    cosine, sine = both[:count, :], both[count:, :]
    return cosine[:, :half] + sine[:, half:], cosine[:, half:] - sine[:, :half]


def latitude_inverse(table_ref, value, count):
    half = value.shape[1] // 2
    both = table_times(table_ref, value)
    cosine, sine = both[:count, :], both[count:, :]
    return cosine[:, :half] - sine[:, half:], cosine[:, half:] + sine[:, :half]


def strided_fill(apart, got_ref):
    total, width = got_ref.shape
    for tile in range(width // 128):
        apart[tile * total : (tile + 1) * total, :] = got_ref[:, tile * 128 : (tile + 1) * 128].astype(F32)


def strided_take(apart, mode, per, total, width):
    spans = [pl.ds(tile * total + mode, total // per, stride=per) for tile in range(width // 128)]
    return jnp.concatenate([apart[span, :] for span in spans], 1).astype(BF16)


def strided_put(apart, mode, per, total, first, value):
    for tile in range(value.shape[1] // 128):
        span = pl.ds((first + tile) * total + mode, total // per, stride=per)
        apart[span, :] = value[:, tile * 128 : (tile + 1) * 128]


def strided_send(sent_ref, apart):
    total, width = sent_ref.shape
    for tile in range(width // 128):
        sent_ref[:, tile * 128 : (tile + 1) * 128] = apart[tile * total : (tile + 1) * total, :].astype(BF16)


def chunk_of(total):
    return total // 3 if total % 48 == 0 else total


def spectral_kernel(got_ref, table_ref, one_ref, bias_one_ref, two_ref, bias_two_ref, sent_ref, low_ref, active_ref, slope_ref, factor_ref, got32, shrunk, *, per):
    total, width = got_ref.shape
    count, half = total // per, width // 2
    strided_fill(got32, got_ref)
    for mode in range(per):
        real, imag = latitude_forward(table_ref, strided_take(got32, mode, per, total, width), count)
        span = slice(mode * count, (mode + 1) * count)
        low_ref[span, :half] = real.astype(BF16)
        low_ref[span, half:] = imag.astype(BF16)
    chunk = chunk_of(total)

    @pl.loop(0, total // chunk)
    def _(step):
        span = pl.ds(pl.multiple_of(step * chunk, chunk), chunk)
        first = dot(low_ref[span, :], one_ref[...]) + bias_one_ref[...]
        active, slope = gelu_pair(first)
        active = active.astype(BF16)
        active_ref[span, :] = active
        slope_ref[span, :] = slope.astype(BF16)
        second = dot(active, two_ref[...]) + bias_two_ref[...]
        bend = jnp.tanh(second * (1.0 / SOFTNESS))
        shrunk[span, :] = second - SHRINK * bend
        factor_ref[span, :] = (1.0 - SHRINK / SOFTNESS * (1.0 - bend * bend)).astype(BF16)

    for mode in range(per):
        real, imag = latitude_inverse(table_ref, shrunk[mode * count : (mode + 1) * count, :], count)
        strided_put(got32, mode, per, total, 0, real)
        strided_put(got32, mode, per, total, half // 128, imag)
    strided_send(sent_ref, got32)


def spectral_back_kernel(got_ref, table_ref, one_ref, two_ref, slope_ref, factor_ref, sent_ref, second_ref, first_ref, got32, grad, *, per):
    total, width = got_ref.shape
    count, half = total // per, width // 2
    strided_fill(got32, got_ref)
    for mode in range(per):
        real, imag = latitude_forward(table_ref, strided_take(got32, mode, per, total, width), count)
        span = slice(mode * count, (mode + 1) * count)
        second_ref[span, :half] = (real * factor_ref[span, :half].astype(F32)).astype(BF16)
        second_ref[span, half:] = (imag * factor_ref[span, half:].astype(F32)).astype(BF16)
    chunk = chunk_of(total)

    @pl.loop(0, total // chunk)
    def _(step):
        span = pl.ds(pl.multiple_of(step * chunk, chunk), chunk)
        grad_active = dot_transposed(second_ref[span, :], two_ref[...])
        first = (grad_active * slope_ref[span, :].astype(F32)).astype(BF16)
        first_ref[span, :] = first
        grad[span, :] = dot_transposed(first, one_ref[...])

    for mode in range(per):
        real, imag = latitude_inverse(table_ref, grad[mode * count : (mode + 1) * count, :], count)
        strided_put(got32, mode, per, total, 0, real)
        strided_put(got32, mode, per, total, half // 128, imag)
    strided_send(sent_ref, got32)


def dense_kernel(live_ref, norm_ref, in_ref, in_bias_ref, out_ref, out_bias_ref, mixed_ref, result_ref, active_ref, slope_ref, total):
    step = pl.program_id(0)
    hidden = dot(norm_ref[...], in_ref[...]) + in_bias_ref[...]
    active, slope = gelu_pair(hidden)
    active = active.astype(BF16)
    active_ref[...] = active
    slope_ref[...] = slope.astype(BF16)
    part = dot(active, out_ref[...])

    @pl.when(step == 0)
    def _():
        total[...] = part + mixed_ref[...] + out_bias_ref[...]

    @pl.when(step > 0)
    def _():
        total[...] += part

    @pl.when(step == pl.num_programs(0) - 1)
    def _():
        index = lax.broadcasted_iota(jnp.int32, total.shape, 0)
        result_ref[...] = jnp.where(index < live_ref[0], total[...], 0.0).astype(BF16)


def dense_back_kernel(grad_ref, out_ref, slope_ref, in_ref, hidden_ref, bias_ref, norm_ref):
    step = pl.program_id(0)
    grad_active = dot_transposed(grad_ref[...], out_ref[...])
    hidden = (grad_active * slope_ref[...].astype(F32)).astype(BF16)
    hidden_ref[...] = hidden
    bias_ref[...] = jnp.sum(hidden.astype(F32), axis=0, keepdims=True)
    part = dot_transposed(hidden, in_ref[...])

    @pl.when(step == 0)
    def _():
        norm_ref[...] = part

    @pl.when(step > 0)
    def _():
        norm_ref[...] += part


def middle_back_kernel(norm_ref, mixed_ref, grad_ref, gain_two_ref, table_ref, sent_ref, grad_mixed_ref, small_ref, grad32, sent32, *, rows, lanes, per):
    grad32[...] = grad_ref[...].astype(F32)
    longs = mixed_ref.shape[0] // rows
    gain_grad = shift_grad = bias_grad = 0.0
    for row in range(rows):
        span = slice(row * longs, (row + 1) * longs)
        unit, inverse = centered(mixed_ref[span, :])
        grad_norm = norm_ref[span, :]
        grad_out = grad32[span, :]
        grad_mixed = norm_back(grad_norm, gain_two_ref[...], unit, inverse) + grad_out
        gain_grad += jnp.sum(grad_norm * unit, axis=0, keepdims=True)
        shift_grad += jnp.sum(grad_norm, axis=0, keepdims=True)
        bias_grad += jnp.sum(grad_out, axis=0, keepdims=True)
        grad_mixed_ref[span, :] = grad_mixed
        scatter_modes(sent32, table_times(table_ref, grad_mixed), row, rows, lanes, per)
    small_ref[0:1, :] = gain_grad
    small_ref[1:2, :] = shift_grad
    small_ref[2:3, :] = bias_grad
    sent_ref[...] = sent32[...].astype(BF16)


def front_back_kernel(back_ref, grad_mixed_ref, x_ref, gain_ref, table_ref, grad_ref, small_ref, x32, back32, spectrum, *, rows, lanes, per):
    x32[...] = x_ref[...].astype(F32)
    back32[...] = back_ref[...].astype(F32)
    longs = x_ref.shape[0] // rows
    gain_grad = shift_grad = 0.0
    for row in range(rows):
        span = slice(row * longs, (row + 1) * longs)
        gather_modes(spectrum, back32, row, rows, lanes, per)
        grad_mixed = grad_mixed_ref[span, :]
        grad_normed = table_times_low(table_ref, spectrum[...].astype(BF16)) + grad_mixed
        unit, inverse = centered(x32[span, :])
        gain_grad += jnp.sum(grad_normed * unit, axis=0, keepdims=True)
        shift_grad += jnp.sum(grad_normed, axis=0, keepdims=True)
        x32[span, :] = norm_back(grad_normed, gain_ref[...], unit, inverse) + grad_mixed
    small_ref[0:1, :] = gain_grad
    small_ref[1:2, :] = shift_grad
    grad_ref[...] = x32[...].astype(BF16)


def call(body, outs, scratch, *args, flops=0, **named):
    bytes_moved = sum(a.size * a.dtype.itemsize for a in args) + sum(math.prod(s) * np.dtype(d).itemsize for s, d in outs)
    return pl.pallas_call(
        functools.partial(body, **named),
        out_shape=[jax.ShapeDtypeStruct(s, d) for s, d in outs],
        in_specs=[pl.BlockSpec(memory_space=pltpu.VMEM)] * len(args),
        out_specs=[pl.BlockSpec(memory_space=pltpu.VMEM)] * len(outs),
        scratch_shapes=[pltpu.VMEM(s, F32) for s in scratch],
        compiler_params=pltpu.CompilerParams(vmem_limit_bytes=VMEM_BYTES),
        cost_estimate=pl.CostEstimate(flops=flops, bytes_accessed=bytes_moved, transcendentals=0),
    )(*args)


def front(x, gain, shift, lay):
    tokens, width = x.shape
    moved = (lay["modes"], width)
    return call(front_kernel, [(moved, BF16)], [(tokens, width), moved], x, gain, shift, lay["to_modes"], flops=lay["cost"], **lay["sizes"])[0]


def middle(back, x, gain, shift, gain_two, shift_two, lay):
    tokens, width = x.shape
    scratch = [(tokens, width), (lay["modes"], width), (lay["waves"], width), (tokens, width)]
    outs = [((tokens, width), F32), ((tokens, width), BF16)]
    return call(middle_kernel, outs, scratch, back, x, gain, shift, gain_two, shift_two, lay["from_modes"], flops=lay["cost"], **lay["sizes"])


def apart(shape):
    return (shape[0] * shape[1] // 128, 128)


def spectral(got, w, lay):
    shape = got.shape
    return call(spectral_kernel, [(shape, BF16)] * 5, [apart(shape), shape], got, lay["latitude"], w[2], w[3], w[4], w[5], flops=4 * lay["cost"], per=lay["sizes"]["per"])


def spectral_back(got, w, slope, factor, lay):
    shape = got.shape
    return call(spectral_back_kernel, [(shape, BF16)] * 3, [apart(shape), shape], got, lay["latitude"], w[2], w[4], slope, factor, flops=4 * lay["cost"], per=lay["sizes"]["per"])


def dense(norm, mixed, w, live):
    tokens, width = norm.shape
    hidden = w[8].shape[1]
    tile = 512
    whole = lambda shape: pl.BlockSpec(shape, lambda j: (0, 0))
    across = lambda count: pl.BlockSpec((count, tile), lambda j: (0, j))
    return pl.pallas_call(
        dense_kernel,
        grid=(hidden // tile,),
        out_shape=[
            jax.ShapeDtypeStruct((tokens, width), BF16),
            jax.ShapeDtypeStruct((tokens, hidden), BF16),
            jax.ShapeDtypeStruct((tokens, hidden), BF16),
        ],
        in_specs=[
            pl.BlockSpec(memory_space=pltpu.SMEM),
            whole((tokens, width)),
            across(width),
            across(1),
            pl.BlockSpec((tile, width), lambda j: (j, 0)),
            whole((1, width)),
            whole((tokens, width)),
        ],
        out_specs=[whole((tokens, width)), across(tokens), across(tokens)],
        scratch_shapes=[pltpu.VMEM((tokens, width), F32)],
        compiler_params=pltpu.CompilerParams(vmem_limit_bytes=VMEM_BYTES, dimension_semantics=("arbitrary",)),
        cost_estimate=pl.CostEstimate(flops=4 * tokens * width * hidden, bytes_accessed=30 << 20, transcendentals=tokens * hidden),
    )(live, norm, w[8], w[9], w[10], w[11], mixed)


def dense_back(grad, w, slope):
    tokens, width = grad.shape
    hidden = w[8].shape[1]
    tile = 512
    whole = lambda shape: pl.BlockSpec(shape, lambda j: (0, 0))
    across = lambda count: pl.BlockSpec((count, tile), lambda j: (0, j))
    return pl.pallas_call(
        dense_back_kernel,
        grid=(hidden // tile,),
        out_shape=[
            jax.ShapeDtypeStruct((tokens, hidden), BF16),
            jax.ShapeDtypeStruct((1, hidden), F32),
            jax.ShapeDtypeStruct((tokens, width), F32),
        ],
        in_specs=[whole((tokens, width)), pl.BlockSpec((tile, width), lambda j: (j, 0)), across(tokens), across(width)],
        out_specs=[across(tokens), across(1), whole((tokens, width))],
        compiler_params=pltpu.CompilerParams(vmem_limit_bytes=VMEM_BYTES, dimension_semantics=("arbitrary",)),
        cost_estimate=pl.CostEstimate(flops=4 * tokens * width * hidden, bytes_accessed=30 << 20, transcendentals=0),
    )(grad, w[10], slope, w[8])


def middle_back(grad_norm, mixed, grad, gain_two, lay):
    tokens, width = mixed.shape
    moved = (lay["modes"], width)
    outs = [(moved, BF16), ((tokens, width), F32), ((3, width), F32)]
    return call(middle_back_kernel, outs, [(tokens, width), moved], grad_norm, mixed, grad, gain_two, lay["to_modes_grad"], flops=lay["cost"], **lay["sizes"])


def front_back(back, grad_mixed, x, gain, lay):
    tokens, width = x.shape
    scratch = [(tokens, width), (lay["modes"], width), (lay["waves"], width)]
    return call(front_back_kernel, [((tokens, width), BF16), ((2, width), F32)], scratch, back, grad_mixed, x, gain, lay["from_modes_grad"], flops=lay["cost"], **lay["sizes"])


def exchange(item):
    count = lax.axis_size("lane") * 2
    pieces = item.reshape(count, item.shape[0] // count, item.shape[1])
    return lax.all_to_all(pieces, ROWS_AXES, 0, 0, tiled=True).reshape(item.shape)


def swap(item, axis, bit):
    return lax.ppermute(item, axis, [(i, i ^ bit) for i in range(lax.axis_size(axis))])


def shed(item, axis, bit):
    set_bit = (lax.axis_index(axis) & bit) > 0
    count = item.shape[0] // 2
    lower, upper = item[:count], item[count:]
    got = swap(jnp.where(set_bit, lower, upper), axis, bit)
    return (jnp.where(set_bit, upper, lower).astype(F32) + got.astype(F32)).astype(BF16)


def double(item, axis, bit):
    set_bit = (lax.axis_index(axis) & bit) > 0
    got = swap(item, axis, bit)
    return jnp.concatenate([jnp.where(set_bit, got, item), jnp.where(set_bit, item, got)], 0)


def lane_bits(turn):
    bits = [1 << i for i in range(lax.axis_size("lane").bit_length() - 1)]
    return [("lane", b) for b in bits[-turn:] + bits[:-turn]] if turn else [("lane", b) for b in bits]


def add_up(item, turn):
    route = [("section", 1)] + lane_bits(turn) + [("half", 1)]
    for axis, bit in route:
        item = shed(item, axis, bit)
    for axis, bit in route[:0:-1]:
        item = double(item, axis, bit)
    return item


def add_small(item):
    slabs = lax.axis_size("lane") * lax.axis_size("half")
    size = item.shape[0]
    each = -(-size // (slabs * 1024)) * 1024
    pieces = jnp.pad(item, (0, slabs * each - size)).astype(BF16).reshape(slabs, each // 128, 128)
    got = lax.all_to_all(pieces, SLAB, 0, 0, tiled=True)
    total = jnp.sum(got.astype(F32), axis=0).astype(BF16)
    spread = jnp.broadcast_to(total[None], pieces.shape)
    return lax.all_to_all(spread, SLAB, 0, 0, tiled=True).reshape(-1)[:size].astype(F32)


def both_layers(item, core):
    other = lax.ppermute(item, "section", [(0, 1), (1, 0)])
    return (jnp.where(core == 0, item, other), jnp.where(core == 0, other, item))


def fetch(pair, core, half):
    own = lax.dynamic_index_in_dim(pair, half, 0, keepdims=False)
    give = lax.dynamic_index_in_dim(pair, 1 - half, 0, keepdims=False)
    got = lax.ppermute(give, ("section", "half"), [(0, 1), (3, 2)])
    got = jnp.where(core == half, own, got)
    return got.reshape(-1, got.shape[-1])


def deliver(layer_zero, layer_one, core, shape):
    parts = []
    for micro in range(2):
        first = lax.ppermute(layer_zero, ("section", "half"), [(micro, 0), (2 + micro, 1)])
        second = lax.ppermute(layer_one, ("section", "half"), [(micro, 2), (2 + micro, 3)])
        parts.append(jnp.where(core == 0, first, second).reshape(shape))
    return jnp.stack(parts)[None]


def block_diagonal(weight):
    _, blocks, size, _ = weight.shape
    same = jnp.eye(blocks, dtype=weight.dtype)
    real, imag = (jnp.einsum("bij,bc->bicj", w, same).reshape(blocks * size, blocks * size) for w in (weight[0], weight[1]))
    return jnp.concatenate([jnp.concatenate([real, imag], 1), jnp.concatenate([-imag, real], 1)], 0)


def block_grads(left, right):
    width = left.shape[1]
    blocks = BLOCKS // 2
    size = width // 2 // blocks
    outer = lax.dot_general(left, right, (((0,), (0,)), ((), ())), preferred_element_type=F32)

    def pick(i, j, b):
        top, side = (i * blocks + b) * size, (j * blocks + b) * size
        return outer[top : top + size, side : side + size]

    real = [pick(0, 0, b) + pick(1, 1, b) for b in range(blocks)]
    imag = [pick(0, 1, b) - pick(1, 0, b) for b in range(blocks)]
    return jnp.stack(real + imag).reshape(2, blocks, size, size)


def layer_forward(x, w, live, lay):
    got = exchange(front(x, w[0], w[1], lay))
    sent, low, active, slope, factor = spectral(got, w, lay)
    mixed, norm = middle(exchange(sent), x, w[0], w[1], w[6], w[7], lay)
    result, activated, bend = dense(norm, mixed, w, live)
    return result, (x, low, active, slope, factor, mixed, norm, activated, bend)


def layer_backward(saved, grad, w, lay):
    x, low, active, slope, factor, mixed, norm, activated, bend = saved
    grad_hidden, grad_in_bias, grad_norm = dense_back(grad, w, bend)
    sent, grad_mixed, small_two = middle_back(grad_norm, mixed, grad, w[6], lay)
    got = exchange(sent)
    across = (((0,), (0,)), ((), ()))
    grad_in = lax.dot_general(norm, grad_hidden, across, preferred_element_type=F32).astype(BF16)
    grad_out = lax.dot_general(activated, grad, across, preferred_element_type=F32).astype(BF16)
    dense_grads = (add_up(grad_in, 0), add_up(grad_out, 1))
    sent, grad_second, grad_first = spectral_back(got, w, slope, factor, lay)
    got = exchange(sent)
    grad_one, grad_two = block_grads(low, grad_first), block_grads(active, grad_second)
    bias_one = jnp.sum(grad_first.astype(F32), axis=0)
    bias_two = jnp.sum(grad_second.astype(F32), axis=0)
    grad_x, small_one = front_back(got, grad_mixed, x, w[0], lay)
    late = add_small(small_one.reshape(-1))
    early = (grad_one, grad_two, bias_one, bias_two, small_two, grad_in_bias)
    shapes = [a.shape for a in early]
    merged = add_small(jnp.concatenate([a.reshape(-1) for a in early]))
    pieces = []
    for shape in shapes:
        size = math.prod(shape)
        pieces.append(merged[:size].reshape(shape))
        merged = merged[size:]
    return grad_x, dense_grads, (*pieces, late.reshape(small_one.shape))


def shards(tokens, cotangent, *params):
    core = lax.axis_index("section")
    half = lax.axis_index("half")
    lane = lax.axis_index("lane")
    lanes = lax.axis_size("lane")
    _, rows, longitudes, width = tokens.shape
    total_rows = rows * lanes * 2
    fields = total_rows // LAT
    live = fields * LAT
    per = -(-(longitudes // 2 + 1) // lanes)
    forward_table, inverse_table = longitude_tables(longitudes, per * lanes)
    lay = {
        "to_modes": jnp.asarray(split_table(forward_table.T)),
        "from_modes": jnp.asarray(split_table(inverse_table)),
        "to_modes_grad": jnp.asarray(split_table(inverse_table.T)),
        "from_modes_grad": jnp.asarray(split_table(forward_table)),
        "latitude": jnp.asarray(split_table(latitude_table(total_rows, fields))),
        "modes": 2 * lanes * rows * per,
        "waves": 2 * lanes * per,
        "cost": 1 << 30,
        "sizes": {"rows": rows, "lanes": lanes, "per": per},
    }
    first_row = (core * lanes + lane) * rows
    live_tokens = (jnp.clip(live - first_row, 0, rows) * longitudes).astype(jnp.int32)
    blocks = BLOCKS // 2
    x = fetch(tokens, core, half)
    grad = fetch(cotangent, core, half)
    grad = jnp.where(jnp.arange(grad.shape[0], dtype=jnp.int32)[:, None] < live_tokens, grad, jnp.zeros_like(grad))
    pairs = [both_layers(item[0], core) for item in params]
    layers = []
    for level in range(2):
        w = [pair[level] for pair in pairs]
        for at in (2, 4):
            w[at] = block_diagonal(lax.dynamic_slice_in_dim(w[at], core * blocks, blocks, 1))
        for at in (3, 5):
            w[at] = lax.dynamic_slice_in_dim(w[at], core * blocks, blocks, 1).astype(F32).reshape(1, -1)
        for at in (0, 1, 6, 7, 9, 11):
            w[at] = w[at].astype(F32).reshape(1, -1)
        layers.append(w)
    live_arg = live_tokens.reshape(1)
    out_one, saved_one = layer_forward(x, layers[0], live_arg, lay)
    out_two, saved_two = layer_forward(out_one, layers[1], live_arg, lay)
    grad_two, dense_two, rest_two = layer_backward(saved_two, grad, layers[1], lay)
    grad_one, dense_one, rest_one = layer_backward(saved_one, grad_two, layers[0], lay)
    shape = tokens.shape[1:]
    outputs = deliver(out_one, out_two, core, shape)
    input_grads = deliver(grad_one, grad_two, core, shape)
    dense_outs = []
    for first, second in zip(dense_one, dense_two):
        got_first = lax.ppermute(first, "section", [(1, 0)])
        got_second = lax.ppermute(second, "section", [(0, 1)])
        upper = jnp.where(core == 0, first, got_second)
        lower = jnp.where(core == 0, got_first, second)
        dense_outs.append(jnp.concatenate([upper, lower], 0).astype(F32)[None])
    size = width // BLOCKS
    rest = []
    for first, second in zip(rest_one, rest_two):
        other = lax.ppermute(jnp.where(core == 0, second, first), "section", [(0, 1), (1, 0)])
        rest.append((jnp.where(core == 0, first, second), other))

    def joined(pair, axis):
        own, other = pair
        return jnp.where(core == 0, jnp.concatenate([own, other], axis), jnp.concatenate([other, own], axis))

    spectral_one, spectral_two = (joined(rest[i], 1)[None] for i in (0, 1))
    biases = []
    for i in (2, 3):
        biases.append(joined([a.reshape(2, blocks, size) for a in rest[i]], 1)[None])
    small_two, in_bias, small_one = (a + b for a, b in rest[4:])
    return (
        outputs, input_grads, small_one[0:1], small_one[1:2], spectral_one, biases[0], spectral_two, biases[1],
        small_two[0:1], small_two[1:2], dense_outs[0], in_bias, dense_outs[1], small_two[2:3],
    )


def solution(mesh):
    devices = mesh.devices
    slabs = devices.shape[1]
    wide = Mesh(devices.reshape(2, 2, slabs // 2), ALL)
    rows = P(None, ("half", "lane"))
    own = P("section")
    return jax.shard_map(
        shards,
        mesh=wide,
        in_specs=(rows, rows) + (own,) * 12,
        out_specs=(P("section", None, ("half", "lane")),) * 2 + (own,) * 12,
        check_vma=False,
    )
```

time: 1580 us -> 1050 us (0.66)
  waiting for transfers between devices: 685 us -> 227 us
  matrix products: 329 us -> 51.7 us
  Pallas kernels: 0 us -> 214 us
  local copies, waits for them, and re-layouts: 296 us -> 129 us
  other arithmetic: 96 us -> 200 us
  starting transfers between devices: 110 us -> 210 us
  blocking collectives: 33 us -> 0 us
    psum x3 -> x0, waiting for transfers between devices: 564 us -> none  [the longest x1 302 us: shards(): a = lax.psum(dense_one[at].astype(BF16), ALL)]
    dot_general x40 -> x8, matrix products: 329 us -> 51.7 us  [the longest x2 19.5 us: layer_backward(): lax.dot_general(norm, grad_hidden, across, preferred_element_type=F32)]
    pallas_call x0 -> x16, Pallas kernels: none -> 214 us  [the longest x12 119 us: call(): pl.pallas_call(functools.partial(body, **named), out_shape=[jax.ShapeDtyp...]
    reshape x42 -> x30, local copies, waits for them, and re-layouts: 155 us -> 30 us  [the longest x8 16.2 us: block_diagonal(): jnp.einsum('bij,bc->bicj', w, same).reshape(blocks * size, blocks * size)]
    ppermute x1 -> x47, waiting for transfers between devices: 0.01 us -> 110 us  [the longest x36 109 us: swap(): lax.ppermute(item, axis, [(i, i ^ bit) for i in range(lax.axis_size(axis))])]
    ppermute x1 -> x47, starting transfers between devices: 0.07 us -> 59.8 us  [the longest x36 49.4 us: swap(): lax.ppermute(item, axis, [(i, i ^ bit) for i in range(lax.axis_size(axis))])]
    all_to_all x7 -> x16, starting transfers between devices: 59 us -> 106 us  [the longest x8 65.6 us: exchange(): lax.all_to_all(pieces, ROWS_AXES, 0, 0, tiled=True).reshape(item.shape)]
    select_n x6 -> x52, other arithmetic: 4.6 us -> 48.5 us  [the longest x20 15 us: shed(): got = swap(jnp.where(set_bit, lower, upper), axis, bit)]
  transfers between devices with their start and end apart: 33 -> 85, of which waited for: 15 -> 32; matrix products, arithmetic and copies ran while one was open for 17% -> 32% of each run, Pallas kernels for 0% -> 15%
where the time goes in v2:
time: 1050 us; the launch traced here: 1030 us
  waiting for transfers between devices  227 us (22%)
  Pallas kernels  214 us (20%)
  starting transfers between devices  210 us (20%)
  other arithmetic  200 us (19%)
  local copies, waits for them, and re-layouts  129 us (12%)
  matrix products  51.7 us (5%)
    pallas_call x12, Pallas kernels, call(): pl.pallas_call(functools.partial(body, **named), out_shape=[jax.ShapeDtyp...  119 us
    ppermute x36, waiting for transfers between devices, swap(): lax.ppermute(item, axis, [(i, i ^ bit) for i in range(lax.axis_size(axis))])  109 us
    all_to_all x8, starting transfers between devices, exchange(): lax.all_to_all(pieces, ROWS_AXES, 0, 0, tiled=True).reshape(item.shape)  65.6 us
    pallas_call x2, Pallas kernels, dense(): pl.pallas_call(dense_kernel, grid=(hidden // tile,), out_shape=[jax.Shape...  56.5 us
    ppermute x36, starting transfers between devices, swap(): lax.ppermute(item, axis, [(i, i ^ bit) for i in range(lax.axis_size(axis))])  49.4 us
    ppermute x2, waiting for transfers between devices, fetch(): got = lax.ppermute(give, ('section', 'half'), [(0, 1), (3, 2)])  46.4 us
    pallas_call x2, Pallas kernels, dense_back(): pl.pallas_call(dense_back_kernel, grid=(hidden // tile,), out_shape=[jax....  38.2 us
    unnamed x130, local copies, waits for them, and re-layouts  30.9 us
  transfers between devices with their start and end apart: 85, of which 32 were waited for; matrix products, arithmetic and copies ran while one was open for 32% of the time, Pallas kernels for 15%

profile of v2, /device:TPU:0, one launch (start us, length us, event | category | flops | bytes accessed | tf_op | source)
XLA Modules:
  0.0 1034.1 jit_solution(12452895383028813247)
XLA Ops:
  0.7 17.0 %constant_dynamic-slice_fusion.1 = (bf16[1,6,180,768]{3,0,2,1:T(2,128)(2,1)}, bf16[1,6,180,768]{3,0,2,1:T(2,128)(2,1)S(1)}, bf16[1,6,180,768]{3,0,2,1:T(2,128)(2,1)S(1)}, bf16[1,6,180,768]{3,0,2,1:T(2,128)(2,1)}) fusion(bf16[2,6,180,768]{3,0,2,1:T(2,128)(2,1)} %param.20, s32[]{:T(128)S(6)} %select_n.697, s32[]{:T(128)S(6)} %select_n.698, ...), kind=kLoop, calls=%fused_computation.299 | loop fusion | bytes 13271048 | tf_op jit(solution)/shard_map/jit(dynamic_index_in_dim)/dynamic_slice | solution.py:483
  28.7 16.0 %collective-permute-done = bf16[6,180,768]{2,1,0:T(8,128)(2,1)} collective-permute-done((bf16[6,180,768]{2,1,0:T(8,128)(2,1)}, bf16[6,180,768]{2,1,0:T(8,128)(2,1)}, u32[]{:S(2)}, u32[]{:S(2)}) %collective-permute-start) | collective-permute-done | bytes 1658912 | tf_op jit(solution)/shard_map/ppermute | solution.py:485
  56.8 23.2 %all-to-all-start = ((bf16[16,72,768]{2,1,0:T(8,128)(2,1)}), bf16[16,72,768]{2,1,0:T(8,128)(2,1)}, u32[]{:S(2)}, u32[]{:S(2)}) async-start(bf16[16,72,768]{2,1,0:T(8,128)(2,1)} %bitcast.255), calls=%async_computation | async-start | bytes 3538944 | tf_op jit(solution)/shard_map/all_to_all | solution.py:431
  116.8 14.9 %shard_map.291 = (bf16[1152,768]{1,0:T(8,128)(2,1)}, bf16[1152,768]{1,0:T(8,128)(2,1)}, bf16[1152,768]{1,0:T(8,128)(2,1)}, bf16[1152,768]{1,0:T(8,128)(2,1)}, bf16[1152,768]{1,0:T(8,128)(2,1)}) custom-call(bf16[1152,768]{1,0:T(8,128)(2,1)} %bitcast.4.got_ref, bf16[384,96]{1,0:T(8,128)(2,1)} %constant.65.clone.table_ref, ...), custom_call_target="tpu_custom_call" | custom-call | flops 4294967296 | bytes 13056000 | tf_op jit(solution)/shard_map/pallas_call | solution.py:326
  167.7 28.3 %shard_map.293 = (bf16[1080,768]{1,0:T(8,128)(2,1)}, bf16[1080,3072]{1,0:T(8,128)(2,1)}, bf16[1080,3072]{1,0:T(8,128)(2,1)}) custom-call(s32[1]{0:T(128)} %bitcast.live_ref, bf16[1080,768]{1,0:T(8,128)(2,1)} %get-tuple-element.57.norm_ref, bf16[768,3072]{1,0:T(8,128)(2,1)} %get-tuple-element.101.in_ref, f32[1,3072]{1,0:T(1,128)} %bitcast.273, ...), custom_call_target="tpu_custom_call" | custom-call | flops 10192158720 | bytes 31457280 | tf_op jit(solution)/shard_map/pallas_call | solution.py:370
  229.5 14.9 %shard_map.295 = (bf16[1152,768]{1,0:T(8,128)(2,1)}, bf16[1152,768]{1,0:T(8,128)(2,1)}, bf16[1152,768]{1,0:T(8,128)(2,1)}, bf16[1152,768]{1,0:T(8,128)(2,1)}, bf16[1152,768]{1,0:T(8,128)(2,1)}) custom-call(bf16[1152,768]{1,0:T(8,128)(2,1)} %bitcast.23.got_ref, bf16[384,96]{1,0:T(8,128)(2,1)} %constant.65.clone.table_ref, ...), custom_call_target="tpu_custom_call" | custom-call | flops 4294967296 | bytes 13056000 | tf_op jit(solution)/shard_map/pallas_call | solution.py:326
  259.0 30.4 %collective-permute-done.17 = bf16[6,180,768]{2,1,0:T(8,128)(2,1)S(1)} collective-permute-done((bf16[6,180,768]{2,1,0:T(8,128)(2,1)}, bf16[6,180,768]{2,1,0:T(8,128)(2,1)S(1)}, u32[]{:S(2)}, u32[]{:S(2)}) %collective-permute-start.17) | collective-permute-done | bytes 1658912 | tf_op jit(solution)/shard_map/ppermute | solution.py:485
  293.5 14.0 %collective-permute-start.13 = (bf16[1080,768]{1,0:T(8,128)(2,1)}, bf16[1080,768]{1,0:T(8,128)(2,1)}, u32[]{:S(2)}, u32[]{:S(2)}) collective-permute-start(bf16[1080,768]{1,0:T(8,128)(2,1)} %get-tuple-element.59.x_ref), channel_id=1, source_target_pairs={{0,0},{16,8},{1,1},{17,9},{2,2},{18,10},{3,3},{19,11},{4,4},{20,12... | collective-permute-start | bytes 4976648 | tf_op jit(solution)/shard_map/ppermute | solution.py:493
  316.6 28.2 %shard_map.297 = (bf16[1080,768]{1,0:T(8,128)(2,1)}, bf16[1080,3072]{1,0:T(8,128)(2,1)}, bf16[1080,3072]{1,0:T(8,128)(2,1)}) custom-call(s32[1]{0:T(128)} %bitcast.live_ref, bf16[1080,768]{1,0:T(8,128)(2,1)} %get-tuple-element.61.norm_ref, bf16[768,3072]{1,0:T(8,128)(2,1)} %get-tuple-element.100.in_ref, f32[1,3072]{1,0:T(1,128)} %bitcast.271, ...), custom_call_target="tpu_custom_call" | custom-call | flops 10192158720 | bytes 31457280 | tf_op jit(solution)/shard_map/pallas_call | solution.py:370
  349.4 19.1 %shard_map.298 = (bf16[1080,3072]{1,0:T(8,128)(2,1)}, f32[1,3072]{1,0:T(1,128)}, f32[1080,768]{1,0:T(8,128)}) custom-call(bf16[1080,768]{1,0:T(8,128)(2,1)} %broadcast_select_fusion.8.grad_ref, bf16[3072,768]{1,0:T(8,128)(2,1)} %get-tuple-element.98.out_ref, bf16[1080,3072]{1,0:T(8,128)(2,1)} %get-tuple-element.64.slope_ref, ...), custom_call_target="tpu_custom_call" | custom-call | flops 10192158720 | bytes 31457280 | tf_op jit(solution)/shard_map/pallas_call | solution.py:400
  378.3 11.2 %all-to-all-start.4 = ((bf16[16,72,768]{2,1,0:T(8,128)(2,1)}), bf16[16,72,768]{2,1,0:T(8,128)(2,1)}, u32[]{:S(2)}, u32[]{:S(2)}) async-start(bf16[16,72,768]{2,1,0:T(8,128)(2,1)} %bitcast.257), calls=%async_computation.4 | async-start | bytes 3538944 | tf_op jit(solution)/shard_map/all_to_all | solution.py:431
  438.6 13.8 %shard_map.300 = (bf16[1152,768]{1,0:T(8,128)(2,1)}, bf16[1152,768]{1,0:T(8,128)(2,1)}, bf16[1152,768]{1,0:T(8,128)(2,1)}) custom-call(bf16[1152,768]{1,0:T(8,128)(2,1)} %bitcast.39.got_ref, bf16[384,96]{1,0:T(8,128)(2,1)} %constant.65.clone.table_ref, bf16[768,768]{1,0:T(8,128)(2,1)} %maximum_maximum_fusion.2.one_ref, ...), custom_call_target="tpu_custom_call" | custom-call | flops 4294967296 | bytes 13049856 | tf_op jit(solution)/shard_map/pallas_call | solution.py:326
  537.7 10.0 collective-permute-done.62
  585.9 17.2 %collective-permute-done.44 = bf16[96,3072]{1,0:T(8,128)(2,1)} collective-permute-done((bf16[96,3072]{1,0:T(8,128)(2,1)}, bf16[96,3072]{1,0:T(8,128)(2,1)}, u32[]{:S(2)}, u32[]{:S(2)}) %collective-permute-start.44) | collective-permute-done | bytes 589856 | tf_op jit(solution)/shard_map/ppermute | solution.py:435
  628.4 19.2 %shard_map.302 = (bf16[1080,3072]{1,0:T(8,128)(2,1)}, f32[1,3072]{1,0:T(1,128)}, f32[1080,768]{1,0:T(8,128)}) custom-call(bf16[1080,768]{1,0:T(8,128)(2,1)} %get-tuple-element.71.grad_ref, bf16[3072,768]{1,0:T(8,128)(2,1)} %get-tuple-element.99.out_ref, bf16[1080,3072]{1,0:T(8,128)(2,1)} %get-tuple-element.72.slope_ref, ...), custom_call_target="tpu_custom_call" | custom-call | flops 10192158720 | bytes 31457280 | tf_op jit(solution)/shard_map/pallas_call | solution.py:400
  647.6 10.0 convolution_convert_fusion.3
  666.1 9.9 shard_map.303
  706.7 13.8 %shard_map.304 = (bf16[1152,768]{1,0:T(8,128)(2,1)}, bf16[1152,768]{1,0:T(8,128)(2,1)}, bf16[1152,768]{1,0:T(8,128)(2,1)}) custom-call(bf16[1152,768]{1,0:T(8,128)(2,1)} %bitcast.43.got_ref, bf16[384,96]{1,0:T(8,128)(2,1)} %constant.65.clone.table_ref, bf16[768,768]{1,0:T(8,128)(2,1)} %maximum_maximum_fusion.one_ref, ...), custom_call_target="tpu_custom_call" | custom-call | flops 4294967296 | bytes 13049856 | tf_op jit(solution)/shard_map/pallas_call | solution.py:326
  831.9 10.4 %collective-permute-done.34 = bf16[48,3072]{1,0:T(8,128)(2,1)S(1)} collective-permute-done((bf16[48,3072]{1,0:T(8,128)(2,1)S(1)}, bf16[48,3072]{1,0:T(8,128)(2,1)S(1)}, u32[]{:S(2)}, u32[]{:S(2)}) %collective-permute-start.34) | collective-permute-done | bytes 294944 | tf_op jit(solution)/shard_map/ppermute | solution.py:435
  846.1 11.7 %collective-permute-done.35 = bf16[96,3072]{1,0:T(8,128)(2,1)S(1)} collective-permute-done((bf16[96,3072]{1,0:T(8,128)(2,1)S(1)}, bf16[96,3072]{1,0:T(8,128)(2,1)S(1)}, u32[]{:S(2)}, u32[]{:S(2)}) %collective-permute-start.35) | collective-permute-done | bytes 589856 | tf_op jit(solution)/shard_map/ppermute | solution.py:435
  921.4 19.9 %collective-permute-done.57 = bf16[768,768]{1,0:T(8,128)(2,1)} collective-permute-done((bf16[768,768]{1,0:T(8,128)(2,1)}, bf16[768,768]{1,0:T(8,128)(2,1)}, u32[]{:S(2)}, u32[]{:S(2)}) %collective-permute-start.57) | collective-permute-done | bytes 1179680 | tf_op jit(solution)/shard_map/ppermute | solution.py:435
  965.5 30.0 %collective-permute-done.20 = bf16[1080,768]{1,0:T(8,128)(2,1)} collective-permute-done((bf16[1080,768]{1,0:T(8,128)(2,1)}, bf16[1080,768]{1,0:T(8,128)(2,1)}, u32[]{:S(2)}, u32[]{:S(2)}) %collective-permute-start.20) | collective-permute-done | bytes 1658912 | tf_op jit(solution)/shard_map/ppermute | solution.py:493
  998.3 10.0 stack_reshape.19
  1008.3 10.6 %maximum_bitcast_fusion.1 = bf16[1,2,6,180,768]{4,1,3,2,0:T(2,128)(2,1)} fusion(bf16[1,6,180,768]{3,0,2,1:T(2,128)(2,1)} %stack_reshape.19, bf16[1,6,180,768]{3,0,2,1:T(2,128)(2,1)S(1)} %stack_reshape.18), kind=kLoop, calls=%fused_computation.15 | loop fusion | flops 6635520 | bytes 6635520 | tf_op jit(solution)/shard_map/broadcast_in_dim | solution.py:496
  (539 shorter events, 628.0 us)
Async XLA Ops:
  56.8 60.0 %all-to-all-start = ((bf16[16,72,768]{2,1,0:T(8,128)(2,1)}), bf16[16,72,768]{2,1,0:T(8,128)(2,1)}, u32[]{:S(2)}, u32[]{:S(2)}) async-start(bf16[16,72,768]{2,1,0:T(8,128)(2,1)} %bitcast.255), calls=%async_computation | async-start | bytes 3538944 | tf_op jit(solution)/shard_map/all_to_all | solution.py:431
  80.0 63.4 %collective-permute-start.9 = (bf16[768,3072]{1,0:T(8,128)(2,1)}, bf16[768,3072]{1,0:T(8,128)(2,1)}, u32[]{:S(2)}, u32[]{:S(2)}) collective-permute-start(bf16[768,3072]{1,0:T(8,128)(2,1)} %bitcast.251), channel_id=1, source_target_pairs={{0,16},{16,0},{1,17},{17,1},{2,18},{18,2},{3,19},{19,3},{4,20},{20... | collective-permute-start | bytes 14155784 | tf_op jit(solution)/shard_map/ppermute | solution.py:478
  80.6 70.9 %collective-permute-start.11 = (bf16[3072,768]{1,0:T(8,128)(2,1)}, bf16[3072,768]{1,0:T(8,128)(2,1)}, u32[]{:S(2)}, u32[]{:S(2)}) collective-permute-start(bf16[3072,768]{1,0:T(8,128)(2,1)} %bitcast.252), channel_id=1, source_target_pairs={{0,16},{16,0},{1,17},{17,1},{2,18},{18,2},{3,19},{19,3},{4,20},{20... | collective-permute-start | bytes 14155784 | tf_op jit(solution)/shard_map/ppermute | solution.py:478
  244.4 64.7 %all-to-all-start.3 = ((bf16[16,72,768]{2,1,0:T(8,128)(2,1)}), bf16[16,72,768]{2,1,0:T(8,128)(2,1)}, u32[]{:S(2)}, u32[]{:S(2)}) async-start(bf16[16,72,768]{2,1,0:T(8,128)(2,1)} %bitcast.258), calls=%async_computation.3 | async-start | bytes 3538944 | tf_op jit(solution)/shard_map/all_to_all | solution.py:431
  293.5 120.4 %collective-permute-start.13 = (bf16[1080,768]{1,0:T(8,128)(2,1)}, bf16[1080,768]{1,0:T(8,128)(2,1)}, u32[]{:S(2)}, u32[]{:S(2)}) collective-permute-start(bf16[1080,768]{1,0:T(8,128)(2,1)} %get-tuple-element.59.x_ref), channel_id=1, source_target_pairs={{0,0},{16,8},{1,1},{17,9},{2,2},{18,10},{3,3},{19,11},{4,4},{20,12... | collective-permute-start | bytes 4976648 | tf_op jit(solution)/shard_map/ppermute | solution.py:493
  307.5 112.2 %collective-permute-start.15 = (bf16[1080,768]{1,0:T(8,128)(2,1)}, bf16[1080,768]{1,0:T(8,128)(2,1)S(1)}, u32[]{:S(2)}, u32[]{:S(2)}) collective-permute-start(bf16[1080,768]{1,0:T(8,128)(2,1)} %get-tuple-element.59.x_ref), channel_id=1, source_target_pairs={{8,0},{24,8},{9,1},{25,9},{10,2},{26,10},{11,3},{27,11},{12,4},{28... | collective-permute-start | bytes 4976648 | tf_op jit(solution)/shard_map/ppermute | solution.py:493
  344.8 69.2 %collective-permute-start.14 = (bf16[1080,768]{1,0:T(8,128)(2,1)}, bf16[1080,768]{1,0:T(8,128)(2,1)}, u32[]{:S(2)}, u32[]{:S(2)}) collective-permute-start(bf16[1080,768]{1,0:T(8,128)(2,1)} %get-tuple-element.63), channel_id=1, source_target_pairs={{0,16},{16,24},{1,17},{17,25},{2,18},{18,26},{3,19},{19,27},{4,20}... | collective-permute-start | bytes 4976648 | tf_op jit(solution)/shard_map/ppermute | solution.py:494
  347.3 72.4 %collective-permute-start.16 = (bf16[1080,768]{1,0:T(8,128)(2,1)}, bf16[1080,768]{1,0:T(8,128)(2,1)}, u32[]{:S(2)}, u32[]{:S(2)}) collective-permute-start(bf16[1080,768]{1,0:T(8,128)(2,1)} %get-tuple-element.63), channel_id=1, source_target_pairs={{8,16},{24,24},{9,17},{25,25},{10,18},{26,26},{11,19},{27,27},{12,... | collective-permute-start | bytes 4976648 | tf_op jit(solution)/shard_map/ppermute | solution.py:494
  378.3 60.3 %all-to-all-start.4 = ((bf16[16,72,768]{2,1,0:T(8,128)(2,1)}), bf16[16,72,768]{2,1,0:T(8,128)(2,1)}, u32[]{:S(2)}, u32[]{:S(2)}) async-start(bf16[16,72,768]{2,1,0:T(8,128)(2,1)} %bitcast.257), calls=%async_computation.4 | async-start | bytes 3538944 | tf_op jit(solution)/shard_map/all_to_all | solution.py:431
  428.2 68.5 %collective-permute-start.59 = (bf16[768,768]{1,0:T(8,128)(2,1)S(1)}, bf16[768,768]{1,0:T(8,128)(2,1)}, u32[]{:S(2)}, u32[]{:S(2)}) collective-permute-start(bf16[768,768]{1,0:T(8,128)(2,1)S(1)} %broadcast_select_fusion.15), channel_id=1, source_target_pairs={{0,4},{1,5},{2,6},{3,7},{4,0},{5,1},{6,2},{7,3},{8,12},{9,13},{10,... | collective-permute-start | bytes 3538952 | tf_op jit(solution)/shard_map/ppermute | solution.py:435
  437.1 63.6 %collective-permute-start.38 = (bf16[192,3072]{1,0:T(8,128)(2,1)}, bf16[192,3072]{1,0:T(8,128)(2,1)}, u32[]{:S(2)}, u32[]{:S(2)}) collective-permute-start(bf16[192,3072]{1,0:T(8,128)(2,1)} %broadcast_select_fusion.21), channel_id=1, source_target_pairs={{0,1},{1,0},{2,3},{3,2},{4,5},{5,4},{6,7},{7,6},{8,9},{9,8},{10,11... | collective-permute-start | bytes 3538952 | tf_op jit(solution)/shard_map/ppermute | solution.py:435
  516.3 56.2 %all-to-all-start.15 = ((bf16[16,80,128]{2,1,0:T(8,128)(2,1)}), bf16[16,80,128]{2,1,0:T(8,128)(2,1)}, u32[]{:S(2)}, u32[]{:S(2)}) async-start(bf16[16,80,128]{2,1,0:T(8,128)(2,1)} %broadcast_in_dim.29), calls=%async_computation.15 | async-start | bytes 655360 | tf_op jit(solution)/shard_map/all_to_all | solution.py:474
  582.0 100.5 %collective-permute-start.66 = (bf16[768,768]{1,0:T(8,128)(2,1)}, bf16[768,768]{1,0:T(8,128)(2,1)}, u32[]{:S(2)}, u32[]{:S(2)}) collective-permute-start(bf16[768,768]{1,0:T(8,128)(2,1)} %pad_maximum_fusion.7), channel_id=1, source_target_pairs={{0,4},{1,5},{2,6},{3,7},{4,0},{5,1},{6,2},{7,3},{8,12},{9,13},{10,... | collective-permute-start | bytes 3538952 | tf_op jit(solution)/shard_map/ppermute | solution.py:435
  605.8 84.9 %collective-permute-start.45 = (bf16[192,3072]{1,0:T(8,128)(2,1)}, bf16[192,3072]{1,0:T(8,128)(2,1)}, u32[]{:S(2)}, u32[]{:S(2)}) collective-permute-start(bf16[192,3072]{1,0:T(8,128)(2,1)} %pad_maximum_fusion.5), channel_id=1, source_target_pairs={{0,1},{1,0},{2,3},{3,2},{4,5},{5,4},{6,7},{7,6},{8,9},{9,8},{10,11... | collective-permute-start | bytes 3538952 | tf_op jit(solution)/shard_map/ppermute | solution.py:435
  628.4 65.3 %collective-permute-start.49 = (bf16[1536,768]{1,0:T(8,128)(2,1)}, bf16[1536,768]{1,0:T(8,128)(2,1)}, u32[]{:S(2)}, u32[]{:S(2)}) collective-permute-start(bf16[1536,768]{1,0:T(8,128)(2,1)} %broadcast_select_fusion.5), channel_id=1, source_target_pairs={{0,16},{16,0},{1,17},{17,1},{2,18},{18,2},{3,19},{19,3},{4,20},{20... | collective-permute-start | bytes 7077896 | tf_op jit(solution)/shard_map/ppermute | solution.py:435
  686.8 258.3 %collective-permute-start.67 = (bf16[1536,768]{1,0:T(8,128)(2,1)}, bf16[1536,768]{1,0:T(8,128)(2,1)}, u32[]{:S(2)}, u32[]{:S(2)}) collective-permute-start(bf16[1536,768]{1,0:T(8,128)(2,1)} %pad_maximum_fusion.3), channel_id=1, source_target_pairs={{0,16},{1,17},{2,18},{3,19},{4,20},{5,21},{6,22},{7,23},{8,24},{9,... | collective-permute-start | bytes 7077896 | tf_op jit(solution)/shard_map/ppermute | solution.py:606
  698.1 63.6 %collective-permute-start.50 = (bf16[768,768]{1,0:T(8,128)(2,1)}, bf16[768,768]{1,0:T(8,128)(2,1)}, u32[]{:S(2)}, u32[]{:S(2)}) collective-permute-start(bf16[768,768]{1,0:T(8,128)(2,1)} %broadcast_select_fusion.18), channel_id=1, source_target_pairs={{0,4},{1,5},{2,6},{3,7},{4,0},{5,1},{6,2},{7,3},{8,12},{9,13},{10,... | collective-permute-start | bytes 3538952 | tf_op jit(solution)/shard_map/ppermute | solution.py:435
  705.2 61.2 %collective-permute-start.29 = (bf16[192,3072]{1,0:T(8,128)(2,1)}, bf16[192,3072]{1,0:T(8,128)(2,1)}, u32[]{:S(2)}, u32[]{:S(2)}) collective-permute-start(bf16[192,3072]{1,0:T(8,128)(2,1)} %broadcast_select_fusion.24), channel_id=1, source_target_pairs={{0,1},{1,0},{2,3},{3,2},{4,5},{5,4},{6,7},{7,6},{8,9},{9,8},{10,11... | collective-permute-start | bytes 3538952 | tf_op jit(solution)/shard_map/ppermute | solution.py:435
  772.2 177.2 %collective-permute-start.46 = (bf16[384,3072]{1,0:T(8,128)(2,1)}, bf16[384,3072]{1,0:T(8,128)(2,1)}, u32[]{:S(2)}, u32[]{:S(2)}) collective-permute-start(bf16[384,3072]{1,0:T(8,128)(2,1)} %pad_maximum_fusion.1), channel_id=1, source_target_pairs={{0,16},{1,17},{2,18},{3,19},{4,20},{5,21},{6,22},{7,23},{8,24},{9,... | collective-permute-start | bytes 7077896 | tf_op jit(solution)/shard_map/ppermute | solution.py:606
  798.6 60.6 %all-to-all-start.7 = ((bf16[16,72,768]{2,1,0:T(8,128)(2,1)}), bf16[16,72,768]{2,1,0:T(8,128)(2,1)S(1)}, u32[]{:S(2)}, u32[]{:S(2)}) async-start(bf16[16,72,768]{2,1,0:T(8,128)(2,1)} %bitcast.253), calls=%async_computation.7 | async-start | bytes 3538944 | tf_op jit(solution)/shard_map/all_to_all | solution.py:431
  859.1 58.6 %collective-permute-start.36 = (bf16[192,3072]{1,0:T(8,128)(2,1)}, bf16[192,3072]{1,0:T(8,128)(2,1)}, u32[]{:S(2)}, u32[]{:S(2)}) collective-permute-start(bf16[192,3072]{1,0:T(8,128)(2,1)} %pad_maximum_fusion.4), channel_id=1, source_target_pairs={{0,1},{1,0},{2,3},{3,2},{4,5},{5,4},{6,7},{7,6},{8,9},{9,8},{10,11... | collective-permute-start | bytes 3538952 | tf_op jit(solution)/shard_map/ppermute | solution.py:435
  945.1 50.4 %collective-permute-start.20 = (bf16[1080,768]{1,0:T(8,128)(2,1)}, bf16[1080,768]{1,0:T(8,128)(2,1)}, u32[]{:S(2)}, u32[]{:S(2)}) collective-permute-start(bf16[1080,768]{1,0:T(8,128)(2,1)} %get-tuple-element.79), channel_id=1, source_target_pairs={{8,0},{24,8},{9,1},{25,9},{10,2},{26,10},{11,3},{27,11},{12,4},{28... | collective-permute-start | bytes 4976648 | tf_op jit(solution)/shard_map/ppermute | solution.py:493
  949.4 69.5 %collective-permute-start.68 = (bf16[1536,768]{1,0:T(8,128)(2,1)}, bf16[1536,768]{1,0:T(8,128)(2,1)}, u32[]{:S(2)}, u32[]{:S(2)}) collective-permute-start(bf16[1536,768]{1,0:T(8,128)(2,1)} %get-tuple-element.107), channel_id=1, source_target_pairs={{16,0},{17,1},{18,2},{19,3},{20,4},{21,5},{22,6},{23,7},{24,8},{25... | collective-permute-start | bytes 7077896 | tf_op jit(solution)/shard_map/ppermute | solution.py:605
  954.3 71.6 %collective-permute-start.47 = (bf16[384,3072]{1,0:T(8,128)(2,1)}, bf16[384,3072]{1,0:T(8,128)(2,1)}, u32[]{:S(2)}, u32[]{:S(2)}) collective-permute-start(bf16[384,3072]{1,0:T(8,128)(2,1)} %get-tuple-element.113), channel_id=1, source_target_pairs={{16,0},{17,1},{18,2},{19,3},{20,4},{21,5},{22,6},{23,7},{24,8},{25... | collective-permute-start | bytes 7077896 | tf_op jit(solution)/shard_map/ppermute | solution.py:605
  (120 other events, 1583.8 us)

commit v3 on v2

v3 whole, which is shorter than its diff:
```python
import functools
import math

import jax
import jax.numpy as jnp
import numpy as np
from jax import lax
from jax.experimental import pallas as pl
from jax.experimental.pallas import tpu as pltpu
from jax.sharding import Mesh, PartitionSpec as P

BLOCKS = 8
LAT = 90
EPSILON = 1e-05
SHRINK = 0.01
SOFTNESS = 0.1
ROWS_AXES = ("section", "lane")
ALL = ("section", "half", "lane")
SLAB = ("half", "lane")
F32 = jnp.float32
BF16 = jnp.bfloat16
VMEM_BYTES = 56 * 1024 * 1024
GAIN_ONE, SHIFT_ONE, GAIN_TWO, SHIFT_TWO, OUT_BIAS, IN_BIAS, BIAS_ONE, BIAS_TWO = 0, 1, 2, 3, 4, 5, 9, 10
G_GAIN_TWO, G_SHIFT_TWO, G_OUT_BIAS, G_IN_BIAS, G_BIAS_ONE, G_BIAS_TWO, G_GAIN_ONE, G_SHIFT_ONE, G_ROWS = 0, 1, 2, 3, 7, 8, 9, 10, 16


def split_table(table):
    high = np.asarray(table, np.float32).astype(jnp.bfloat16)
    low = (np.asarray(table, np.float64) - high.astype(np.float64)).astype(jnp.bfloat16)
    return np.concatenate([high, low], 0)


def longitude_tables(longitudes, padded):
    column = np.arange(longitudes)[:, None]
    frequency = np.arange(padded)[None, :]
    angle = (column * frequency % longitudes) * (2.0 * math.pi / longitudes)
    usable = (frequency <= longitudes // 2) / math.sqrt(longitudes)
    forward = np.concatenate([np.cos(angle) * usable, -np.sin(angle) * usable], 1)
    doubled = np.where((frequency == 0) | (frequency == longitudes // 2), 1.0, 2.0)
    inverse = forward * np.concatenate([doubled, doubled], 1)
    return (forward, inverse)


def latitude_table(rows, fields):
    index = np.arange(LAT)
    angle = (index[:, None] * index[None, :] % LAT) * (2.0 * math.pi / LAT)
    parts = []
    for wave in (np.cos(angle), np.sin(angle)):
        whole = np.zeros((rows, rows))
        for field in range(fields):
            span = slice(field * LAT, (field + 1) * LAT)
            whole[span, span] = wave / math.sqrt(LAT)
        parts.append(whole)
    return np.concatenate(parts, 0)


def dot(left, right):
    return jnp.dot(left, right, preferred_element_type=F32)


def dot_transposed(left, right):
    return lax.dot_general(left, right, (((1,), (1,)), ((), ())), preferred_element_type=F32)


def table_times_low(table_ref, low):
    count = table_ref.shape[0] // 2
    return dot(table_ref[:count, :], low) + dot(table_ref[count:, :], low)


def table_times(table_ref, value):
    count = table_ref.shape[0] // 2
    high = value.astype(BF16)
    rest = (value - high.astype(F32)).astype(BF16)
    return dot(table_ref[:count, :], high) + dot(table_ref[:count, :], rest) + dot(table_ref[count:, :], high)


def gelu_pair(value):
    size = jnp.abs(value) * math.sqrt(0.5)
    inverse = 1.0 / (1.0 + 0.3275911 * size)
    wave = jnp.exp(-0.5 * value * value)
    series = inverse * (0.254829592 + inverse * (-0.284496736 + inverse * (1.421413741 + inverse * (-1.453152027 + inverse * 1.061405429))))
    tail = 0.5 * series * wave
    share = jnp.where(value > 0, 1.0 - tail, tail)
    return value * share, share + value * wave * (1.0 / math.sqrt(2.0 * math.pi))


def row_of(vec_ref, at):
    return vec_ref[at : at + 1, :]


def centered(value):
    center = value - jnp.mean(value, axis=-1, keepdims=True)
    inverse = lax.rsqrt(jnp.mean(center * center, axis=-1, keepdims=True) + EPSILON)
    return center * inverse, inverse


def norm_back(grad, gain, unit, inverse):
    scaled = grad * gain
    return (scaled - jnp.mean(scaled, axis=-1, keepdims=True) - unit * jnp.mean(scaled * unit, axis=-1, keepdims=True)) * inverse


def scatter_modes(sent, spectrum, row, rows, lanes, per):
    width = spectrum.shape[1]
    half = width // 2
    modes = lanes * per
    for part in range(2):
        for lane in range(lanes):
            base = ((part * lanes + lane) * rows + row) * per
            for wave in range(2):
                piece = spectrum[wave * modes + lane * per : wave * modes + (lane + 1) * per, part * half : (part + 1) * half]
                sent[base : base + per, wave * half : (wave + 1) * half] = piece


def gather_modes(spectrum, back, row, rows, lanes, per):
    width = spectrum.shape[1]
    half = width // 2
    modes = lanes * per
    for part in range(2):
        for lane in range(lanes):
            base = ((part * lanes + lane) * rows + row) * per
            for wave in range(2):
                piece = back[base : base + per, wave * half : (wave + 1) * half]
                spectrum[wave * modes + lane * per : wave * modes + (lane + 1) * per, part * half : (part + 1) * half] = piece


def front_kernel(x_ref, vec_ref, table_ref, sent_ref, sent32, *, rows, lanes, per):
    for row in range(rows):
        unit, _ = centered(x_ref[row].astype(F32))
        spectrum = table_times(table_ref, unit * row_of(vec_ref, GAIN_ONE) + row_of(vec_ref, SHIFT_ONE))
        scatter_modes(sent32, spectrum, row, rows, lanes, per)
    sent_ref[...] = sent32[...].astype(BF16)


def middle_kernel(back_ref, x_ref, vec_ref, table_ref, mixed_ref, norm_ref, back32, spectrum, norm32, *, rows, lanes, per):
    back32[...] = back_ref[...].astype(F32)
    longs = x_ref.shape[1]
    for row in range(rows):
        span = slice(row * longs, (row + 1) * longs)
        gather_modes(spectrum, back32, row, rows, lanes, per)
        value = x_ref[row].astype(F32)
        unit, _ = centered(value)
        mixed = table_times_low(table_ref, spectrum[...].astype(BF16)) + (unit * row_of(vec_ref, GAIN_ONE) + row_of(vec_ref, SHIFT_ONE)) + value
        mixed_ref[span, :] = mixed
        unit, _ = centered(mixed)
        norm32[span, :] = unit * row_of(vec_ref, GAIN_TWO) + row_of(vec_ref, SHIFT_TWO)
    norm_ref[...] = norm32[...].astype(BF16)


def latitude_forward(table_ref, value, count):
    half = value.shape[1] // 2
    both = table_times_low(table_ref, value)
    cosine, sine = both[:count, :], both[count:, :]
    return cosine[:, :half] + sine[:, half:], cosine[:, half:] - sine[:, :half]


def latitude_inverse(table_ref, value, count):
    half = value.shape[1] // 2
    both = table_times(table_ref, value)
    cosine, sine = both[:count, :], both[count:, :]
    return cosine[:, :half] - sine[:, half:], cosine[:, half:] + sine[:, :half]


def strided_fill(apart, got_ref):
    total, width = got_ref.shape
    for tile in range(width // 128):
        apart[tile * total : (tile + 1) * total, :] = got_ref[:, tile * 128 : (tile + 1) * 128].astype(F32)


def strided_take(apart, mode, per, total, width):
    spans = [pl.ds(tile * total + mode, total // per, stride=per) for tile in range(width // 128)]
    return jnp.concatenate([apart[span, :] for span in spans], 1).astype(BF16)


def strided_put(apart, mode, per, total, first, value):
    for tile in range(value.shape[1] // 128):
        span = pl.ds((first + tile) * total + mode, total // per, stride=per)
        apart[span, :] = value[:, tile * 128 : (tile + 1) * 128]


def strided_send(sent_ref, apart):
    total, width = sent_ref.shape
    for tile in range(width // 128):
        sent_ref[:, tile * 128 : (tile + 1) * 128] = apart[tile * total : (tile + 1) * total, :].astype(BF16)


def chunk_of(total):
    return total // 3 if total % 48 == 0 else total


def spectral_kernel(got_ref, table_ref, one_ref, two_ref, vec_ref, sent_ref, low_ref, active_ref, slope_ref, factor_ref, got32, shrunk, *, per):
    total, width = got_ref.shape
    count, half = total // per, width // 2
    strided_fill(got32, got_ref)
    for mode in range(per):
        real, imag = latitude_forward(table_ref, strided_take(got32, mode, per, total, width), count)
        span = slice(mode * count, (mode + 1) * count)
        low_ref[span, :half] = real.astype(BF16)
        low_ref[span, half:] = imag.astype(BF16)
    chunk = chunk_of(total)

    @pl.loop(0, total // chunk)
    def _(step):
        span = pl.ds(pl.multiple_of(step * chunk, chunk), chunk)
        first = dot(low_ref[span, :], one_ref[...]) + row_of(vec_ref, BIAS_ONE)
        active, slope = gelu_pair(first)
        active = active.astype(BF16)
        active_ref[span, :] = active
        slope_ref[span, :] = slope.astype(BF16)
        second = dot(active, two_ref[...]) + row_of(vec_ref, BIAS_TWO)
        bend = jnp.tanh(second * (1.0 / SOFTNESS))
        shrunk[span, :] = second - SHRINK * bend
        factor_ref[span, :] = (1.0 - SHRINK / SOFTNESS * (1.0 - bend * bend)).astype(BF16)

    for mode in range(per):
        real, imag = latitude_inverse(table_ref, shrunk[mode * count : (mode + 1) * count, :], count)
        strided_put(got32, mode, per, total, 0, real)
        strided_put(got32, mode, per, total, half // 128, imag)
    strided_send(sent_ref, got32)


def spectral_back_kernel(got_ref, table_ref, one_ref, two_ref, slope_ref, factor_ref, sent_ref, second_ref, first_ref, got32, grad, *, per):
    total, width = got_ref.shape
    count, half = total // per, width // 2
    strided_fill(got32, got_ref)
    for mode in range(per):
        real, imag = latitude_forward(table_ref, strided_take(got32, mode, per, total, width), count)
        span = slice(mode * count, (mode + 1) * count)
        second_ref[span, :half] = (real * factor_ref[span, :half].astype(F32)).astype(BF16)
        second_ref[span, half:] = (imag * factor_ref[span, half:].astype(F32)).astype(BF16)
    chunk = chunk_of(total)

    @pl.loop(0, total // chunk)
    def _(step):
        span = pl.ds(pl.multiple_of(step * chunk, chunk), chunk)
        grad_active = dot_transposed(second_ref[span, :], two_ref[...])
        first = (grad_active * slope_ref[span, :].astype(F32)).astype(BF16)
        first_ref[span, :] = first
        grad[span, :] = dot_transposed(first, one_ref[...])

    for mode in range(per):
        real, imag = latitude_inverse(table_ref, grad[mode * count : (mode + 1) * count, :], count)
        strided_put(got32, mode, per, total, 0, real)
        strided_put(got32, mode, per, total, half // 128, imag)
    strided_send(sent_ref, got32)


def choose(place_ref, level, own_ref, other_ref, chosen):
    @pl.when(place_ref[0] == level)
    def _():
        chosen[...] = own_ref[...]

    @pl.when(place_ref[0] != level)
    def _():
        chosen[...] = other_ref[...]


def dense_kernel(place_ref, norm_ref, in_ref, in_other_ref, out_ref, out_other_ref, vec_ref, mixed_ref, result_ref, active_ref, slope_ref, total, in_kept, out_kept, *, level):
    step = pl.program_id(0)
    choose(place_ref, level, in_ref, in_other_ref, in_kept)
    choose(place_ref, level, out_ref, out_other_ref, out_kept)
    hidden = dot(norm_ref[...], in_kept[...]) + vec_ref[pl.ds(IN_BIAS + step, 1), :]
    active, slope = gelu_pair(hidden)
    active = active.astype(BF16)
    active_ref[...] = active
    slope_ref[...] = slope.astype(BF16)
    part = dot(active, out_kept[...])

    @pl.when(step == 0)
    def _():
        total[...] = part + mixed_ref[...] + row_of(vec_ref, OUT_BIAS)

    @pl.when(step > 0)
    def _():
        total[...] += part

    @pl.when(step == pl.num_programs(0) - 1)
    def _():
        rows, longs, _ = result_ref.shape
        for row in range(rows):
            value = total[row * longs : (row + 1) * longs, :]
            result_ref[row] = jnp.where(row < place_ref[1], value, 0.0).astype(BF16)


def dense_back_kernel(place_ref, grad_ref, out_ref, out_other_ref, slope_ref, in_ref, in_other_ref, hidden_ref, bias_ref, norm_ref, in_kept, out_kept, *, level):
    step = pl.program_id(0)
    choose(place_ref, level, in_ref, in_other_ref, in_kept)
    choose(place_ref, level, out_ref, out_other_ref, out_kept)
    grad_active = dot_transposed(grad_ref[...], out_kept[...])
    hidden = (grad_active * slope_ref[...].astype(F32)).astype(BF16)
    hidden_ref[...] = hidden
    bias_ref[pl.ds(step, 1), :] = jnp.sum(hidden.astype(F32), axis=0, keepdims=True)
    part = dot_transposed(hidden, in_kept[...])

    @pl.when(step == 0)
    def _():
        norm_ref[...] = part

    @pl.when(step > 0)
    def _():
        norm_ref[...] += part


def middle_back_kernel(norm_ref, mixed_ref, grad_ref, vec_ref, table_ref, sent_ref, grad_mixed_ref, small_ref, grad32, sent32, *, rows, lanes, per):
    grad32[...] = grad_ref[...].astype(F32)
    longs = mixed_ref.shape[0] // rows
    gain_grad = shift_grad = bias_grad = 0.0
    for row in range(rows):
        span = slice(row * longs, (row + 1) * longs)
        unit, inverse = centered(mixed_ref[span, :])
        grad_norm = norm_ref[span, :]
        grad_out = grad32[span, :]
        grad_mixed = norm_back(grad_norm, row_of(vec_ref, GAIN_TWO), unit, inverse) + grad_out
        gain_grad += jnp.sum(grad_norm * unit, axis=0, keepdims=True)
        shift_grad += jnp.sum(grad_norm, axis=0, keepdims=True)
        bias_grad += jnp.sum(grad_out, axis=0, keepdims=True)
        grad_mixed_ref[span, :] = grad_mixed
        scatter_modes(sent32, table_times(table_ref, grad_mixed), row, rows, lanes, per)
    small_ref[0:1, :] = gain_grad
    small_ref[1:2, :] = shift_grad
    small_ref[2:3, :] = bias_grad
    sent_ref[...] = sent32[...].astype(BF16)


def front_back_kernel(back_ref, grad_mixed_ref, x_ref, vec_ref, table_ref, known_ref, grad_ref, flat_ref, small_ref, back32, spectrum, flat32, *, rows, lanes, per):
    back32[...] = back_ref[...].astype(F32)
    longs = x_ref.shape[1]
    gain_grad = shift_grad = 0.0
    for row in range(rows):
        span = slice(row * longs, (row + 1) * longs)
        gather_modes(spectrum, back32, row, rows, lanes, per)
        grad_mixed = grad_mixed_ref[span, :]
        grad_normed = table_times_low(table_ref, spectrum[...].astype(BF16)) + grad_mixed
        unit, inverse = centered(x_ref[row].astype(F32))
        gain_grad += jnp.sum(grad_normed * unit, axis=0, keepdims=True)
        shift_grad += jnp.sum(grad_normed, axis=0, keepdims=True)
        grad = norm_back(grad_normed, row_of(vec_ref, GAIN_ONE), unit, inverse) + grad_mixed
        flat32[span, :] = grad
        grad_ref[row] = grad.astype(BF16)
    known = known_ref[...]
    index = lax.broadcasted_iota(jnp.int32, known.shape, 0)
    known = jnp.where(index == G_GAIN_ONE, gain_grad, jnp.where(index == G_SHIFT_ONE, shift_grad, known))
    for tile in range(known.shape[1] // 128):
        small_ref[tile * G_ROWS : (tile + 1) * G_ROWS, :] = known[:, tile * 128 : (tile + 1) * 128].astype(BF16)
    flat_ref[...] = flat32[...].astype(BF16)


def spectral_grad_kernel(low_ref, first_ref, active_ref, second_ref, small_ref, in_bias_ref, blocks_ref, known_ref, outer, *, blocks):
    half = outer.shape[0] // 2
    size = half // blocks
    blocks_ref[...] = jnp.zeros_like(blocks_ref)
    for which, (left, right) in enumerate(((low_ref, first_ref), (active_ref, second_ref))):
        outer[...] = lax.dot_general(left[...], right[...], (((0,), (0,)), ((), ())), preferred_element_type=F32)
        for block in range(blocks):
            up, down = slice(block * size, (block + 1) * size), slice(half + block * size, half + (block + 1) * size)
            at = (which * 2 * blocks + block) * size
            blocks_ref[at : at + size, :size] = (outer[up, up] + outer[down, down]).astype(BF16)
            at += blocks * size
            blocks_ref[at : at + size, :size] = (outer[up, down] - outer[down, up]).astype(BF16)
    known_ref[...] = jnp.zeros_like(known_ref)
    known_ref[G_GAIN_TWO : G_OUT_BIAS + 1, :] = small_ref[...]
    known_ref[G_IN_BIAS : G_IN_BIAS + 4, :] = in_bias_ref[...]
    known_ref[G_BIAS_ONE : G_BIAS_ONE + 1, :] = jnp.sum(first_ref[...].astype(F32), axis=0, keepdims=True)
    known_ref[G_BIAS_TWO : G_BIAS_TWO + 1, :] = jnp.sum(second_ref[...].astype(F32), axis=0, keepdims=True)


def matrices_kernel(place_ref, own_one_ref, own_two_ref, other_one_ref, other_two_ref, one_a_ref, two_a_ref, one_b_ref, two_b_ref, whole, *, blocks):
    core = place_ref[0]
    size = own_one_ref.shape[-1]
    half = blocks * size

    def build(source, target):
        whole[...] = jnp.zeros_like(whole)
        for block in range(blocks):
            real = source[0, core * blocks + block].astype(F32)
            imag = source[1, core * blocks + block].astype(F32)
            up, down = slice(block * size, (block + 1) * size), slice(half + block * size, half + (block + 1) * size)
            whole[up, up] = real
            whole[up, down] = imag
            whole[down, up] = -imag
            whole[down, down] = real
        target[...] = whole[...].astype(BF16)

    for level, targets in enumerate(((one_a_ref, two_a_ref), (one_b_ref, two_b_ref))):

        @pl.when(core == level)
        def _(targets=targets):
            build(own_one_ref, targets[0])
            build(own_two_ref, targets[1])

        @pl.when(core != level)
        def _(targets=targets):
            build(other_one_ref, targets[0])
            build(other_two_ref, targets[1])


def first_shed_kernel(place_ref, in_ref, in_got_ref, out_ref, out_got_ref, *targets):
    step = pl.program_id(0)
    for core, (mine, got) in enumerate(((out_ref, out_got_ref), (in_ref, in_got_ref))):

        @pl.when(place_ref[0] == core)
        def _(mine=mine, got=got):
            total = (mine[...].astype(F32) + got[...].astype(F32)).astype(BF16)
            for route in range(len(targets) // 2):
                keeps = (step // 2) % 2 == place_ref[2 + route]

                @pl.when((step // 4 == route) & keeps)
                def _(route=route, total=total):
                    targets[2 * route + 1][...] = total

                @pl.when((step // 4 == route) & jnp.logical_not(keeps))
                def _(route=route, total=total):
                    targets[2 * route][...] = total


def shed_kernel(bits_ref, *refs):
    count = len(refs) // 4
    kept, got, sends, keeps = (refs[i * count : (i + 1) * count] for i in range(4))
    for at in range(count):
        half = sends[at].shape[0]
        for target, bit in ((keeps[at], bits_ref[at]), (sends[at], 1 - bits_ref[at])):
            span = pl.ds(pl.multiple_of(bit * half, half), half)
            target[...] = (kept[at][span, :].astype(F32) + got[at][span, :].astype(F32)).astype(BF16)


def stack_kernel(*refs):
    *sources, target = refs
    count = len(sources) // 2
    rows = sources[0].shape[0]
    for at in range(count):
        target[at * rows : (at + 1) * rows, :] = (sources[at][...].astype(F32) + sources[count + at][...].astype(F32)).astype(BF16)


def add_kernel(place_ref, one_ref, one_got_ref, two_ref, two_got_ref, mine_ref, give_ref):
    for core, (first, second) in enumerate(((mine_ref, give_ref), (give_ref, mine_ref))):

        @pl.when(place_ref[0] == core)
        def _(first=first, second=second):
            first[...] = (one_ref[...].astype(F32) + one_got_ref[...].astype(F32)).astype(BF16)
            second[...] = (two_ref[...].astype(F32) + two_got_ref[...].astype(F32)).astype(BF16)


def pack_kernel(place_ref, mine_ref, got_ref, *targets):
    for core, (first, second) in enumerate(((mine_ref, got_ref), (got_ref, mine_ref))):

        @pl.when(place_ref[0] == core)
        def _(first=first, second=second):
            for at, target in enumerate(targets):
                rows = target.shape[1]
                target[0] = first[at * rows : (at + 1) * rows, :]
                target[1] = second[at * rows : (at + 1) * rows, :]


def double_kernel(bits_ref, *refs):
    count = len(refs) // 3
    own, got, targets = (refs[i * count : (i + 1) * count] for i in range(3))
    for at in range(count):
        rows = own[at].shape[1]
        for source, bit in ((own[at], bits_ref[at]), (got[at], 1 - bits_ref[at])):
            targets[at][:, pl.ds(pl.multiple_of(bit * rows, rows), rows), :] = source[...]


def finish_kernel(place_ref, *refs, routes):
    sources, (in_grad_ref, out_grad_ref) = refs[:routes], refs[-2:]
    part, step = pl.program_id(0), pl.program_id(1)
    rows = out_grad_ref.shape[0]
    per_half = sources[0].shape[1] // rows
    span = pl.ds(pl.multiple_of((step % per_half) * rows, rows), rows)
    for route in range(routes):
        for which, target in enumerate((out_grad_ref, in_grad_ref)):

            @pl.when((step // per_half == route) & (part == which))
            def _(target=target, source=sources[route]):
                target[...] = source[0, span, :].astype(F32)


def small_sum_kernel(got_ref, spread_ref):
    total = jnp.sum(got_ref[...].astype(F32), axis=0).astype(BF16)
    for at in range(spread_ref.shape[0]):
        spread_ref[at] = total


def small_finish_kernel(place_ref, own_ref, other_ref, one_ref, two_ref, bias_one_ref, bias_two_ref, gain_one_ref, shift_one_ref, gain_two_ref, shift_two_ref, in_bias_ref, out_bias_ref, vec, vec_other, *, blocks):
    core = place_ref[0]
    size = one_ref.shape[-1]
    matrix_rows = 4 * blocks * size
    tiles = vec.shape[1] // 128
    for which, target in enumerate((one_ref, two_ref)):
        for wave in range(2):
            for block in range(blocks):
                at = core * matrix_rows + ((which * 2 + wave) * blocks + block) * size
                span = pl.ds(pl.multiple_of(at, 32), size)
                target[wave, core * blocks + block] = own_ref[span, :].astype(F32)[:, :size]
                target[wave, (1 - core) * blocks + block] = other_ref[span, :].astype(F32)[:, :size]
    for source, target in ((own_ref, vec), (other_ref, vec_other)):
        for tile in range(tiles):
            at = 2 * matrix_rows + (core * tiles + tile) * G_ROWS
            target[:, tile * 128 : (tile + 1) * 128] = source[pl.ds(pl.multiple_of(at, G_ROWS), G_ROWS), :].astype(F32)
    half = vec.shape[1] // 2
    for row, target in ((G_BIAS_ONE, bias_one_ref), (G_BIAS_TWO, bias_two_ref)):
        for wave in range(2):
            for source, place in ((vec, core), (vec_other, 1 - core)):
                target[wave : wave + 1, pl.ds(pl.multiple_of(place * half, 128), half)] = source[row : row + 1, wave * half : (wave + 1) * half]
    total = vec[...] + vec_other[...]
    for row, target in ((G_GAIN_ONE, gain_one_ref), (G_SHIFT_ONE, shift_one_ref), (G_GAIN_TWO, gain_two_ref), (G_SHIFT_TWO, shift_two_ref), (G_OUT_BIAS, out_bias_ref)):
        target[...] = total[row : row + 1, :]
    in_bias_ref[...] = total[G_IN_BIAS : G_IN_BIAS + 4, :]


def call(body, outs, scratch, *args, flops=0, scalars=0, **named):
    bytes_moved = sum(a.size * a.dtype.itemsize for a in args) + sum(math.prod(s) * np.dtype(d).itemsize for s, d in outs)
    return pl.pallas_call(
        functools.partial(body, **named),
        out_shape=[jax.ShapeDtypeStruct(s, d) for s, d in outs],
        in_specs=[pl.BlockSpec(memory_space=pltpu.SMEM if i < scalars else pltpu.VMEM) for i in range(len(args))],
        out_specs=[pl.BlockSpec(memory_space=pltpu.VMEM)] * len(outs),
        scratch_shapes=[pltpu.VMEM(s, F32) for s in scratch],
        compiler_params=pltpu.CompilerParams(vmem_limit_bytes=VMEM_BYTES),
        cost_estimate=pl.CostEstimate(flops=flops, bytes_accessed=bytes_moved if flops else bytes_moved // 8, transcendentals=0),
    )(*args)


def front(x, vec, lay):
    moved = (lay["modes"], x.shape[2])
    return call(front_kernel, [(moved, BF16)], [moved], x, vec, lay["to_modes"], flops=lay["cost"], **lay["sizes"])[0]


def middle(back, x, vec, lay):
    tokens, width = x.shape[0] * x.shape[1], x.shape[2]
    scratch = [(lay["modes"], width), (lay["waves"], width), (tokens, width)]
    outs = [((tokens, width), F32), ((tokens, width), BF16)]
    return call(middle_kernel, outs, scratch, back, x, vec, lay["from_modes"], flops=lay["cost"], **lay["sizes"])


def apart(shape):
    return (shape[0] * shape[1] // 128, 128)


def spectral(got, one, two, vec, lay):
    shape = got.shape
    return call(spectral_kernel, [(shape, BF16)] * 5, [apart(shape), shape], got, lay["latitude"], one, two, vec, flops=4 * lay["cost"], per=lay["sizes"]["per"])


def spectral_back(got, one, two, slope, factor, lay):
    shape = got.shape
    return call(spectral_back_kernel, [(shape, BF16)] * 3, [apart(shape), shape], got, lay["latitude"], one, two, slope, factor, flops=4 * lay["cost"], per=lay["sizes"]["per"])


def spectral_grads(low, first, active, second, small, in_bias):
    width = low.shape[1]
    blocks = BLOCKS // 2
    outs = [((4 * width // 2, 128), BF16), ((G_ROWS, width), F32)]
    return call(spectral_grad_kernel, outs, [(width, width)], low, first, active, second, small, in_bias, flops=4 * low.shape[0] * width * width, blocks=blocks)


def matrices(place, own, other):
    _, blocks, size, _ = own[0].shape
    shape = (blocks * size, blocks * size)
    return call(matrices_kernel, [(shape, BF16)] * 4, [shape], place, *own, *other, scalars=1, blocks=blocks // 2)


def dense_specs(tokens, width, tile, level):
    whole = lambda shape: pl.BlockSpec(shape, lambda j, c: (0,) * len(shape))
    across = lambda count: pl.BlockSpec((count, tile), lambda j, c: (0, j))
    pick = lambda own: (lambda j, c: jnp.where((c[0] == level) == own, j, 0))
    wide = [pl.BlockSpec((width, tile), lambda j, c, own=own: (0, pick(own)(j, c))) for own in (True, False)]
    tall = [pl.BlockSpec((tile, width), lambda j, c, own=own: (pick(own)(j, c), 0)) for own in (True, False)]
    return whole, across, wide, tall


def dense(place, norm, mixed, pairs, vec, shape, level):
    tokens, width = norm.shape
    hidden = pairs[0][0].shape[1]
    tile = width
    whole, across, wide, tall = dense_specs(tokens, width, tile, level)
    return pl.pallas_call(
        functools.partial(dense_kernel, level=level),
        grid_spec=pltpu.PrefetchScalarGridSpec(
            num_scalar_prefetch=1,
            grid=(hidden // tile,),
            in_specs=[whole((tokens, width)), *wide, *tall, whole(vec.shape), whole((tokens, width))],
            out_specs=[whole(shape), across(tokens), across(tokens)],
            scratch_shapes=[pltpu.VMEM((tokens, width), F32), pltpu.VMEM((width, tile), BF16), pltpu.VMEM((tile, width), BF16)],
        ),
        out_shape=[
            jax.ShapeDtypeStruct(shape, BF16),
            jax.ShapeDtypeStruct((tokens, hidden), BF16),
            jax.ShapeDtypeStruct((tokens, hidden), BF16),
        ],
        compiler_params=pltpu.CompilerParams(vmem_limit_bytes=VMEM_BYTES),
        cost_estimate=pl.CostEstimate(flops=4 * tokens * width * hidden, bytes_accessed=30 << 20, transcendentals=tokens * hidden),
    )(place, norm, *pairs[0], *pairs[1], vec, mixed)


def dense_back(place, grad, pairs, slope, level):
    tokens, width = grad.shape
    hidden = pairs[0][0].shape[1]
    tile = width
    whole, across, wide, tall = dense_specs(tokens, width, tile, level)
    return pl.pallas_call(
        functools.partial(dense_back_kernel, level=level),
        grid_spec=pltpu.PrefetchScalarGridSpec(
            num_scalar_prefetch=1,
            grid=(hidden // tile,),
            in_specs=[whole((tokens, width)), *tall, across(tokens), *wide],
            out_specs=[across(tokens), whole((hidden // tile, tile)), whole((tokens, width))],
            scratch_shapes=[pltpu.VMEM((width, tile), BF16), pltpu.VMEM((tile, width), BF16)],
        ),
        out_shape=[
            jax.ShapeDtypeStruct((tokens, hidden), BF16),
            jax.ShapeDtypeStruct((hidden // tile, tile), F32),
            jax.ShapeDtypeStruct((tokens, width), F32),
        ],
        compiler_params=pltpu.CompilerParams(vmem_limit_bytes=VMEM_BYTES),
        cost_estimate=pl.CostEstimate(flops=4 * tokens * width * hidden, bytes_accessed=30 << 20, transcendentals=0),
    )(place, grad, *pairs[1], slope, *pairs[0])


def middle_back(grad_norm, mixed, grad, vec, lay):
    tokens, width = mixed.shape
    moved = (lay["modes"], width)
    outs = [(moved, BF16), ((tokens, width), F32), ((3, width), F32)]
    return call(middle_back_kernel, outs, [(tokens, width), moved], grad_norm, mixed, grad, vec, lay["to_modes_grad"], flops=lay["cost"], **lay["sizes"])


def front_back(back, grad_mixed, x, vec, known, lay):
    tokens, width = grad_mixed.shape
    scratch = [(lay["modes"], width), (lay["waves"], width), (tokens, width)]
    outs = [(x.shape, BF16), ((tokens, width), BF16), ((G_ROWS * width // 128, 128), BF16)]
    return call(front_back_kernel, outs, scratch, back, grad_mixed, x, vec, lay["from_modes_grad"], known, flops=lay["cost"], **lay["sizes"])


def first_shed(place, grad_in, grad_in_got, grad_out, grad_out_got):
    width, hidden = grad_in.shape
    rows = hidden // ROUTES // 4
    tall = width // rows
    wide = pl.BlockSpec((rows, width), lambda j, c: (jnp.where(c[0] == 1, j % tall, 0), jnp.where(c[0] == 1, j // tall, 0)))
    high = pl.BlockSpec((rows, width), lambda j, c: (jnp.where(c[0] == 0, j, 0), 0))

    def target(route, keep):
        def index(j, c):
            step = jnp.clip(j - 4 * route, 0, 3)
            upper = (c[2 + route] == 1) == keep
            return (jnp.where(upper, jnp.maximum(step - 2, 0), jnp.minimum(step, 1)), 0)

        return pl.BlockSpec((rows, width), index)

    outs = pl.pallas_call(
        first_shed_kernel,
        grid_spec=pltpu.PrefetchScalarGridSpec(
            num_scalar_prefetch=1,
            grid=(4 * ROUTES,),
            in_specs=[wide, wide, high, high],
            out_specs=[target(route, keep) for route in range(ROUTES) for keep in (False, True)],
        ),
        out_shape=[jax.ShapeDtypeStruct((2 * rows, width), BF16)] * (2 * ROUTES),
        compiler_params=pltpu.CompilerParams(vmem_limit_bytes=VMEM_BYTES),
        cost_estimate=pl.CostEstimate(flops=0, bytes_accessed=width * hidden, transcendentals=0),
    )(place, grad_in, grad_in_got, grad_out, grad_out_got)
    return outs[::2], outs[1::2]


def shed(bits, kept, got):
    rows, width = kept[0].shape
    outs = call(shed_kernel, [((rows // 2, width), BF16)] * (2 * len(kept)), [], bits, *kept, *got, scalars=1)
    return outs[: len(kept)], outs[len(kept) :]


def double(bits, own, got):
    _, rows, width = own[0].shape
    return call(double_kernel, [((2, 2 * rows, width), BF16)] * len(own), [], bits, *own, *got, scalars=1)


def finish(place, pieces, shape, other_side, kept=()):
    width, hidden = shape
    half = pieces[0].shape[1]
    rows = hidden // ROUTES // 4
    tall = width // rows
    per_half = half // rows
    steps = ROUTES * per_half

    def block(j, c):
        route = j // per_half
        side = sum(jnp.where(route == r, c[2 + r], 0) for r in range(ROUTES))
        side = 1 - side if other_side else side
        return (2 * route + side) * per_half + j % per_half

    def wide(p, j, c):
        at = block(jnp.where(p == 1, j, 0), c)
        return at % tall, at // tall

    piece = pl.BlockSpec((1, half, width), lambda p, j, c: (p, 0, 0))
    inputs = [piece] * ROUTES + [pl.BlockSpec(memory_space=pl.ANY)] * len(kept)
    return pl.pallas_call(
        functools.partial(finish_kernel, routes=ROUTES),
        grid_spec=pltpu.PrefetchScalarGridSpec(
            num_scalar_prefetch=1,
            grid=(2, steps),
            in_specs=inputs,
            out_specs=[
                pl.BlockSpec((rows, width), wide),
                pl.BlockSpec((rows, width), lambda p, j, c: (block(jnp.where(p == 0, j, steps - 1), c), 0)),
            ],
        ),
        out_shape=[jax.ShapeDtypeStruct((width, hidden), F32), jax.ShapeDtypeStruct((hidden, width), F32)],
        input_output_aliases={1 + ROUTES + i: i for i in range(len(kept))},
        compiler_params=pltpu.CompilerParams(vmem_limit_bytes=VMEM_BYTES),
        cost_estimate=pl.CostEstimate(flops=0, bytes_accessed=6 * width * hidden, transcendentals=0),
    )(place, *pieces, *kept)


def deliver(core, layer_zero, layer_one):
    return jnp.stack([jnp.where(core == 0, a, b) for a, b in zip(layer_zero, layer_one)])[None]


def after(item, *earlier):
    return lax.optimization_barrier((item, *earlier))[0]


def exchange(item):
    count = lax.axis_size("lane") * 2
    pieces = item.reshape(count, item.shape[0] // count, item.shape[1])
    return lax.all_to_all(pieces, ROWS_AXES, 0, 0, tiled=True).reshape(item.shape)


ROUTES = 3


def routes_of():
    bits = [1 << i for i in range(lax.axis_size("lane").bit_length() - 1)]
    turns = [route * len(bits) // ROUTES for route in range(ROUTES)]
    return [bits[turn:] + bits[:turn] for turn in turns]


def swap(item, bit):
    return lax.ppermute(item, "lane", [(i, i ^ bit) for i in range(lax.axis_size("lane"))])


def swap_all(items, at):
    return [swap(item, route[at]) for item, route in zip(items, routes_of())]


def stack(kept, got):
    rows, width = kept[0].shape
    return call(stack_kernel, [((ROUTES * rows, width), BF16)], [], *kept, *got)[0]


def across_halves(item):
    return lax.ppermute(item, "half", [(0, 1), (1, 0)])


def pack(place, one, one_got, two, two_got):
    rows, width = one.shape
    mine, give = call(add_kernel, [(one.shape, BF16)] * 2, [], place, one, one_got, two, two_got, scalars=1)
    got = lax.ppermute(give, "section", [(0, 1), (1, 0)])
    return mine, call(pack_kernel, [((2, rows // ROUTES, width), BF16)] * ROUTES, [], place, mine, got, scalars=1)


def small_sums(parts, core):
    slabs = lax.axis_size("lane") * lax.axis_size("half")
    count = sum(a.shape[0] for a in parts)
    each = -(-count // (slabs * 8)) * 8
    parts = [*parts, jnp.zeros((slabs * each - count, 128), BF16)]
    pieces = jnp.concatenate(parts, 0).reshape(slabs, each, 128)
    got = lax.all_to_all(pieces, SLAB, 0, 0, tiled=True)
    spread = call(small_sum_kernel, [(got.shape, BF16)], [], got)[0]
    total = lax.all_to_all(spread, SLAB, 0, 0, tiled=True).reshape(slabs * each, 128)
    return total, lax.ppermute(total, "section", [(0, 1), (1, 0)])


def fetch(pair, core, half):
    first = lax.ppermute(pair[1], ("section", "half"), [(0, 1)])
    second = lax.ppermute(pair[0], ("section", "half"), [(3, 2)])
    own = jnp.where(half == 0, pair[0], pair[1])
    return jnp.where(core == half, own, jnp.where(core == 0, first, second))


def send_out(item, level):
    return [lax.ppermute(item, ("section", "half"), [(micro, 2 * level), (2 + micro, 2 * level + 1)]) for micro in range(2)]


ACROSS = (((0,), (0,)), ((), ()))


def exchanged(items):
    return [(item, lax.ppermute(item, "section", [(0, 1), (1, 0)])) for item in items]


def shards(tokens, cotangent, *params):
    core = lax.axis_index("section")
    half = lax.axis_index("half")
    lane = lax.axis_index("lane")
    lanes = lax.axis_size("lane")
    _, rows, longitudes, width = tokens.shape
    total_rows = rows * lanes * 2
    fields = total_rows // LAT
    live = fields * LAT
    per = -(-(longitudes // 2 + 1) // lanes)
    forward_table, inverse_table = longitude_tables(longitudes, per * lanes)
    lay = {
        "to_modes": jnp.asarray(split_table(forward_table.T)),
        "from_modes": jnp.asarray(split_table(inverse_table)),
        "to_modes_grad": jnp.asarray(split_table(inverse_table.T)),
        "from_modes_grad": jnp.asarray(split_table(forward_table)),
        "latitude": jnp.asarray(split_table(latitude_table(total_rows, fields))),
        "modes": 2 * lanes * rows * per,
        "waves": 2 * lanes * per,
        "cost": 1 << 30,
        "sizes": {"rows": rows, "lanes": lanes, "per": per},
    }
    first_row = (core * lanes + lane) * rows
    live_rows = jnp.clip(live - first_row, 0, rows).astype(jnp.int32)
    blocks = BLOCKS // 2
    size = width // BLOCKS
    routes = routes_of()
    levels = len(routes[0])
    bits = [jnp.stack([((lane & route[at]) > 0).astype(jnp.int32) for route in routes]) for at in range(levels)]
    place = jnp.concatenate([jnp.stack([core.astype(jnp.int32), live_rows]), bits[0]])
    params = [item[0] for item in params]
    gain_one, shift_one, spectral_one, bias_one, spectral_two, bias_two, gain_two, shift_two, dense_in, in_bias, dense_out, out_bias = params
    x = fetch(tokens, core, half)
    vectors = [gain_one, shift_one, gain_two, shift_two, out_bias, in_bias, bias_one, bias_two]
    vectors = jnp.concatenate([a.reshape(-1, width) for a in vectors], 0)
    vectors, other = exchanged([vectors])[0]
    vectors = jnp.stack([jnp.where(core == 0, vectors, other), jnp.where(core == 0, other, vectors)]).astype(F32)
    mine = lax.dynamic_slice_in_dim(vectors[:, BIAS_ONE:], core * (width // 2), width // 2, 2).reshape(2, 2, width)
    vectors = jnp.concatenate([vectors[:, :BIAS_ONE], mine], 1)
    vec_one, vec_two = vectors[0], vectors[1]
    spectra = exchanged([spectral_one, spectral_two])
    one_a, two_a, one_b, two_b = matrices(place, [a for a, _ in spectra], [b for _, b in spectra])
    shape = x.shape

    got = exchange(front(x, vec_one, lay))
    dense_in, dense_out = after((dense_in, dense_out), got)
    pairs = exchanged([dense_in, dense_out])
    sent, low_one, active_one, slope_one, factor_one = spectral(got, one_a, two_a, vec_one, lay)
    got = exchange(sent)
    grad = fetch(after(cotangent, got), core, half)
    mixed_one, norm_one = middle(got, x, vec_one, lay)
    out_one, activated_one, bend_one = dense(place, norm_one, mixed_one, pairs, vec_one, shape, 0)
    grad = jnp.where(jnp.arange(rows, dtype=jnp.int32)[:, None, None] < live_rows, grad, jnp.zeros_like(grad))
    got = exchange(front(after(out_one, grad), vec_two, lay))
    grad = grad.reshape(-1, width)
    sent, low_two, active_two, slope_two, factor_two = spectral(got, one_b, two_b, vec_two, lay)
    got = exchange(sent)
    delivered_one = send_out(after(out_one, got), 0)
    mixed_two, norm_two = middle(got, out_one, vec_two, lay)
    out_two, activated_two, bend_two = dense(place, norm_two, mixed_two, pairs, vec_two, shape, 1)
    grad_hidden, in_bias_two, grad_norm = dense_back(place, after(grad, *delivered_one), pairs, bend_two, 1)
    sent, grad_mixed, small_two = middle_back(grad_norm, mixed_two, grad, vec_two, lay)
    got = exchange(sent)
    delivered_two = send_out(out_two, 1)
    norm_two, activated_two = after((norm_two, activated_two), sent)
    sums_two = (
        lax.dot_general(norm_two, grad_hidden, ACROSS, preferred_element_type=F32).astype(BF16),
        lax.dot_general(activated_two, grad, ACROSS, preferred_element_type=F32).astype(BF16),
    )
    from_two = (lax.ppermute(sums_two[0], "section", [(0, 1)]), lax.ppermute(sums_two[1], "section", [(1, 0)]))
    sent, grad_second, grad_first = spectral_back(after(got, *delivered_two, *sums_two), one_b, two_b, slope_two, factor_two, lay)
    got = exchange(sent)
    blocks_two, known = spectral_grads(low_two, grad_first, active_two, grad_second, small_two, in_bias_two)
    sums_two, from_two = after((sums_two, from_two), sent)
    sends_two, keeps_two = first_shed(place, sums_two[0], from_two[0], sums_two[1], from_two[1])
    gots_two = swap_all(sends_two, 0)
    activations = deliver(core, delivered_one, delivered_two)
    grad_x_two, grad, small_two = front_back(after(got, activations, *sends_two), grad_mixed, out_one, vec_two, known, lay)
    grads_two = send_out(grad_x_two, 1)
    grad_hidden, in_bias_one, grad_norm = dense_back(place, grad, pairs, bend_one, 0)
    sends_two, keeps_two = shed(bits[1], keeps_two, after(gots_two, grad_norm))
    gots_two = swap_all(sends_two, 1)
    sent, grad_mixed, small_one = middle_back(after(grad_norm, *sends_two), mixed_one, grad, vec_one, lay)
    got = exchange(sent)
    norm_one, activated_one = after((norm_one, activated_one), sent)
    norm_one = after(norm_one, *grads_two)
    grad_out = lax.dot_general(activated_one, grad, ACROSS, preferred_element_type=F32).astype(BF16)
    grad_out_got = lax.ppermute(grad_out, "section", [(1, 0)])
    grad_in = lax.dot_general(norm_one, grad_hidden, ACROSS, preferred_element_type=F32).astype(BF16)
    grad_in_got = lax.ppermute(grad_in, "section", [(0, 1)])
    for at in range(2, levels):
        sends_two, keeps_two = shed(bits[at], keeps_two, gots_two)
        gots_two = swap_all(sends_two, at)
    got = after(got, grad_in, grad_out, *sends_two)
    sent, grad_second, grad_first = spectral_back(got, one_a, two_a, slope_one, factor_one, lay)
    stacked_two = stack(keeps_two, after(gots_two, sent))
    halved_two = across_halves(stacked_two)
    grad_in, grad_in_got, grad_out, grad_out_got = after((grad_in, grad_in_got, grad_out, grad_out_got), sent)
    sends, keeps = first_shed(place, grad_in, grad_in_got, grad_out, grad_out_got)
    gots = swap_all(sends, 0)
    got = exchange(sent)
    blocks_one, known = spectral_grads(low_one, grad_first, active_one, grad_second, small_one, in_bias_one)
    grad_x_one, _, small_one = front_back(after(got, *sends), grad_mixed, x, vec_one, known, lay)
    gots = after(gots, grad_x_one)
    for at in range(1, levels):
        sends, keeps = shed(bits[at], keeps, gots)
        gots = swap_all(sends, at)
    stacked = stack(keeps, gots)
    mine, own = pack(place, stacked, across_halves(stacked), stacked_two, after(halved_two, stacked))
    grads_one = send_out(after(grad_x_one, mine), 0)
    for at in reversed(range(levels)):
        gots = swap_all(own, at)
        if at > 0:
            own = double(bits[at], own, gots)
    total, other = small_sums(after([blocks_one, blocks_two, small_one, small_two], mine), core)
    row = ((1, width), F32)
    outs = [((2, BLOCKS, size, size), F32)] * 2 + [((2, width), F32)] * 2 + [row] * 4 + [((4, width), F32), row]
    one, two, bias_one, bias_two, gain_one, shift_one, gain_two, shift_two, in_bias, out_bias = call(
        small_finish_kernel, outs, [(G_ROWS, width)] * 2, place, total, other, scalars=1, blocks=blocks
    )
    dense_grads = finish(place, own, dense_in.shape, False)
    grad_in, grad_out = finish(place, gots, dense_in.shape, True, dense_grads)
    return (
        activations, deliver(core, grads_one, grads_two),
        gain_one, shift_one, one[None], bias_one.reshape(1, 2, BLOCKS, size), two[None], bias_two.reshape(1, 2, BLOCKS, size),
        gain_two, shift_two, grad_in[None], in_bias.reshape(1, -1), grad_out[None], out_bias,
    )


def solution(mesh):
    devices = mesh.devices
    slabs = devices.shape[1]
    wide = Mesh(devices.reshape(2, 2, slabs // 2), ALL)
    rows = P(None, ("half", "lane"))
    own = P("section")
    return jax.shard_map(
        shards,
        mesh=wide,
        in_specs=(rows, rows) + (own,) * 12,
        out_specs=(P("section", None, ("half", "lane")),) * 2 + (own,) * 12,
        check_vma=False,
    )
```

time: 1050 us -> 831 us (0.79)
  other arithmetic: 200 us -> 13.7 us
  Pallas kernels: 214 us -> 320 us
  local copies, waits for them, and re-layouts: 129 us -> 40.7 us
  blocking collectives: 0 us -> 86.2 us
  waiting for transfers between devices: 227 us -> 143 us
  starting transfers between devices: 210 us -> 171 us
    all_to_all x0 -> x3, blocking collectives: none -> 86.2 us  [exchange(): lax.all_to_all(pieces, ROWS_AXES, 0, 0, tiled=True).reshape(item.shape)]
    ppermute x69 -> x52, waiting for transfers between devices: 201 us -> 129 us  [the longest x27 69.7 us: swap(): lax.ppermute(item, 'lane', [(i, i ^ bit) for i in range(lax.axis_size('la...]
    select_n x55 -> x2, other arithmetic: 65.8 us -> 4.62 us  [the longest x1 4.19 us: fetch(): return jnp.where(core == half, own, jnp.where(core == 0, first, second))]
    pallas_call x12 -> x27, Pallas kernels: 119 us -> 175 us  [call(): pl.pallas_call(functools.partial(body, **named), out_shape=[jax.ShapeDtyp...]
    pallas_call x4 -> x8, Pallas kernels: 94.7 us -> 145 us  [the longest x2 60.2 us: dense(): pl.pallas_call(functools.partial(dense_kernel, level=level), grid_spec=pl...]
    convert_element_type x24 -> x1, other arithmetic: 39.8 us -> 0.02 us  [shards(): jnp.stack([jnp.where(core == 0, vectors, other), jnp.where(core == 0, oth...]
    another operation x8 -> x3, local copies, waits for them, and re-layouts: 34.2 us -> 0.18 us  [shards(): vectors = jnp.concatenate([a.reshape(-1, width) for a in vectors], 0)]
    concatenate x22 -> x0, other arithmetic: 30.5 us -> none  [the longest x4 11.5 us: shards(): dense_outs.append(jnp.concatenate([upper, lower], 0).astype(F32)[None])]
  transfers between devices with their start and end apart: 85 -> 59, of which waited for: 32 -> 20; matrix products, arithmetic and copies ran while one was open for 32% -> 8% of each run, Pallas kernels for 15% -> 35%
where the time goes in v3:
time: 831 us; the launch traced here: 821 us
  Pallas kernels  320 us (39%)
  starting transfers between devices  171 us (21%)
  waiting for transfers between devices  143 us (17%)
  blocking collectives  86.2 us (10%)
  matrix products  44.3 us (5%)
  local copies, waits for them, and re-layouts  40.7 us (5%)
  other arithmetic  13.7 us (2%)
    pallas_call x27, Pallas kernels, call(): pl.pallas_call(functools.partial(body, **named), out_shape=[jax.ShapeDtyp...  175 us
    all_to_all x3, blocking collectives, exchange(): lax.all_to_all(pieces, ROWS_AXES, 0, 0, tiled=True).reshape(item.shape)  86.2 us
    ppermute x27, waiting for transfers between devices, swap(): lax.ppermute(item, 'lane', [(i, i ^ bit) for i in range(lax.axis_size('la...  69.7 us
    pallas_call x2, Pallas kernels, dense(): pl.pallas_call(functools.partial(dense_kernel, level=level), grid_spec=pl...  60.2 us
    all_to_all x5, starting transfers between devices, exchange(): lax.all_to_all(pieces, ROWS_AXES, 0, 0, tiled=True).reshape(item.shape)  43.9 us
    ppermute x2, waiting for transfers between devices, across_halves(): return lax.ppermute(item, 'half', [(0, 1), (1, 0)])  42 us
    pallas_call x2, Pallas kernels, dense_back(): pl.pallas_call(functools.partial(dense_back_kernel, level=level), grid_sp...  41.2 us
    ppermute x27, starting transfers between devices, swap(): lax.ppermute(item, 'lane', [(i, i ^ bit) for i in range(lax.axis_size('la...  33.9 us
  transfers between devices with their start and end apart: 59, of which 20 were waited for; matrix products, arithmetic and copies ran while one was open for 8% of the time, Pallas kernels for 35%

profile of v3, /device:TPU:0, one launch (start us, length us, event | category | flops | bytes accessed | tf_op | source)
XLA Modules:
  0.0 820.9 jit_solution(15529140484304317092)
XLA Ops:
  24.4 12.5 %collective-permute-done = bf16[6,180,768]{2,1,0:T(8,128)(2,1)} collective-permute-done((bf16[6,180,768]{2,1,0:T(8,128)(2,1)}, bf16[6,180,768]{2,1,0:T(8,128)(2,1)}, u32[]{:S(2)}, u32[]{:S(2)}) %collective-permute-start) | collective-permute-done | bytes 1658912 | tf_op jit(solution)/shard_map/ppermute | solution.py:771
  46.2 24.5 %all-to-all-start = ((bf16[16,72,768]{2,1,0:T(8,128)(2,1)}), bf16[16,72,768]{2,1,0:T(8,128)(2,1)S(1)}, u32[]{:S(2)}, u32[]{:S(2)}) async-start(bf16[16,72,768]{2,1,0:T(8,128)(2,1)} %bitcast.90), calls=%async_computation | async-start | bytes 3538944 | tf_op jit(solution)/shard_map/all_to_all | solution.py:722
  79.2 14.3 %all-to-all-done = bf16[16,72,768]{2,1,0:T(8,128)(2,1)S(1)} async-done(((bf16[16,72,768]{2,1,0:T(8,128)(2,1)}), bf16[16,72,768]{2,1,0:T(8,128)(2,1)S(1)}, u32[]{:S(2)}, u32[]{:S(2)}) %all-to-all-start) | async-done | bytes 1769504 | tf_op jit(solution)/shard_map/all_to_all | solution.py:722
  94.7 14.8 %shard_map.292 = (bf16[1152,768]{1,0:T(8,128)(2,1)}, bf16[1152,768]{1,0:T(8,128)(2,1)}, bf16[1152,768]{1,0:T(8,128)(2,1)}, bf16[1152,768]{1,0:T(8,128)(2,1)}, bf16[1152,768]{1,0:T(8,128)(2,1)}) custom-call(bf16[1152,768]{1,0:T(8,128)(2,1)} %bitcast.88, bf16[384,96]{1,0:T(8,128)(2,1)} %constant.48.clone.table_ref, ...), custom_call_target="tpu_custom_call" | custom-call | flops 4294967296 | bytes 13083648 | tf_op jit(solution)/shard_map/pallas_call | solution.py:511
  109.5 29.6 %all_to_all.50 = bf16[16,72,768]{2,1,0:T(8,128)(2,1)} all-to-all(bf16[16,72,768]{2,1,0:T(8,128)(2,1)} %bitcast.98), channel_id=1, replica_groups=mesh['section'=2,'half'=2,'lane'=8] {'section','lane'}, dimensions={0} | all-to-all | bytes 3538944 | tf_op jit(solution)/shard_map/all_to_all | solution.py:722
  154.1 29.9 %shard_map.294 = (bf16[6,180,768]{2,1,0:T(8,128)(2,1)}, bf16[1080,3072]{1,0:T(8,128)(2,1)}, bf16[1080,3072]{1,0:T(8,128)(2,1)}) custom-call(s32[5]{0:T(128)} %concatenate.12.place_ref, bf16[1080,768]{1,0:T(8,128)(2,1)} %get-tuple-element.227.norm_ref, bf16[768,3072]{1,0:T(8,128)(2,1)} %bitcast.109, bf16[768,3072]{1,0:T(8,128)(2,1)} %collective-permute-done.5.in_other_ref, ...), custom_call_target="tpu_custom_call" | custom-call | flops 10192158720 | bytes 31457280 | tf_op jit(solution)/shard_map/pallas_call | solution.py:575
  189.6 28.4 %all_to_all.51 = bf16[16,72,768]{2,1,0:T(8,128)(2,1)} all-to-all(bf16[16,72,768]{2,1,0:T(8,128)(2,1)} %bitcast.100), channel_id=1, replica_groups=mesh['section'=2,'half'=2,'lane'=8] {'section','lane'}, dimensions={0} | all-to-all | bytes 3538944 | tf_op jit(solution)/shard_map/all_to_all | solution.py:722
  218.0 14.8 %shard_map.296 = (bf16[1152,768]{1,0:T(8,128)(2,1)}, bf16[1152,768]{1,0:T(8,128)(2,1)}, bf16[1152,768]{1,0:T(8,128)(2,1)}, bf16[1152,768]{1,0:T(8,128)(2,1)}, bf16[1152,768]{1,0:T(8,128)(2,1)}) custom-call(bf16[1152,768]{1,0:T(8,128)(2,1)} %bitcast.97, bf16[384,96]{1,0:T(8,128)(2,1)} %constant.48.clone.table_ref, ...), custom_call_target="tpu_custom_call" | custom-call | flops 4294967296 | bytes 13083648 | tf_op jit(solution)/shard_map/pallas_call | solution.py:511
  232.8 28.3 %all_to_all.52 = bf16[16,72,768]{2,1,0:T(8,128)(2,1)} all-to-all(bf16[16,72,768]{2,1,0:T(8,128)(2,1)} %bitcast.99), channel_id=1, replica_groups=mesh['section'=2,'half'=2,'lane'=8] {'section','lane'}, dimensions={0} | all-to-all | bytes 3538944 | tf_op jit(solution)/shard_map/all_to_all | solution.py:722
  273.7 30.3 %shard_map.298 = (bf16[6,180,768]{2,1,0:T(8,128)(2,1)}, bf16[1080,3072]{1,0:T(8,128)(2,1)}, bf16[1080,3072]{1,0:T(8,128)(2,1)}) custom-call(s32[5]{0:T(128)} %concatenate.12.place_ref, bf16[1080,768]{1,0:T(8,128)(2,1)} %get-tuple-element.187.norm_ref, bf16[768,3072]{1,0:T(8,128)(2,1)} %bitcast.110, bf16[768,3072]{1,0:T(8,128)(2,1)} %collective-permute-done.5.in_other_ref, ...), custom_call_target="tpu_custom_call" | custom-call | flops 10192158720 | bytes 31457280 | tf_op jit(solution)/shard_map/pallas_call | solution.py:575
  313.7 20.6 %shard_map.299 = (bf16[1080,3072]{1,0:T(8,128)(2,1)}, f32[4,768]{1,0:T(4,128)}, f32[1080,768]{1,0:T(8,128)}) custom-call(s32[5]{0:T(128)} %concatenate.12.place_ref, bf16[1080,768]{1,0:T(8,128)(2,1)} %reshape.111.grad_ref, bf16[3072,768]{1,0:T(8,128)(2,1)} %bitcast.116, bf16[3072,768]{1,0:T(8,128)(2,1)} %collective-permute-done.6.out_other_ref, ...), custom_call_target="tpu_custom_call" | custom-call | flops 10192158720 | bytes 31457280 | tf_op jit(solution)/shard_map/pallas_call | solution.py:599
  348.0 11.5 %convolution_convert_fusion.2.out_ref = bf16[3072,768]{1,0:T(8,128)(2,1)} fusion(bf16[1080,3072]{1,0:T(8,128)(2,1)} %get-tuple-element.189, bf16[1080,768]{1,0:T(8,128)(2,1)S(1)} %copy-done.1), kind=kOutput, calls=%fused_computation.2 | convolution fusion | flops 5098438656 | bytes 13012992 | tf_op jit(solution)/shard_map/dot_general | solution.py:855
  361.1 11.0 %convolution_convert_fusion.3.in_ref = bf16[768,3072]{1,0:T(8,128)(2,1)} fusion(bf16[1080,768]{1,0:T(8,128)(2,1)S(1)} %copy-done.49, bf16[1080,3072]{1,0:T(8,128)(2,1)} %get-tuple-element.188), kind=kOutput, calls=%fused_computation.3 | convolution fusion | flops 5098438656 | bytes 13012992 | tf_op jit(solution)/shard_map/dot_general | solution.py:854
  380.7 13.6 %shard_map.301 = (bf16[1152,768]{1,0:T(8,128)(2,1)}, bf16[1152,768]{1,0:T(8,128)(2,1)}, bf16[1152,768]{1,0:T(8,128)(2,1)}) custom-call(bf16[1152,768]{1,0:T(8,128)(2,1)} %bitcast.93, bf16[384,96]{1,0:T(8,128)(2,1)} %constant.48.clone.table_ref, bf16[768,768]{1,0:T(8,128)(2,1)} %get-tuple-element.175.one_ref, bf16[768,768]{1,0:T(8,128)(2,1)} %get-tuple-element.176.two_ref, ...), custom_call_target="tpu_custom_call" | custom-call | flops 4294967296 | bytes 13049856 | tf_op jit(solution)/shard_map/pallas_call | solution.py:511
  411.5 12.2 %shard_map.302 = (bf16[512,768]{1,0:T(8,128)(2,1)}, bf16[512,768]{1,0:T(8,128)(2,1)}, bf16[512,768]{1,0:T(8,128)(2,1)}, bf16[512,768]{1,0:T(8,128)(2,1)}, bf16[5...) custom-call(s32[5]{0:T(128)} %concatenate.12.place_ref, bf16[768,3072]{1,0:T(8,128)(2,1)} %convolution_convert_fusion.3.in_ref, ...), custom_call_target="tpu_custom_call" | custom-call | bytes 2359296 | tf_op jit(solution)/shard_map/pallas_call | solution.py:647
  441.6 20.7 %shard_map.305 = (bf16[1080,3072]{1,0:T(8,128)(2,1)}, f32[4,768]{1,0:T(4,128)}, f32[1080,768]{1,0:T(8,128)}) custom-call(s32[5]{0:T(128)} %concatenate.12.place_ref, bf16[1080,768]{1,0:T(8,128)(2,1)} %get-tuple-element.210.grad_ref, bf16[3072,768]{1,0:T(8,128)(2,1)} %bitcast.117, bf16[3072,768]{1,0:T(8,128)(2,1)} %collective-permute-done.6.out_other_ref, ...), custom_call_target="tpu_custom_call" | custom-call | flops 10192158720 | bytes 31457280 | tf_op jit(solution)/shard_map/pallas_call | solution.py:599
  493.7 11.1 %convolution_convert_fusion.1.in_ref = bf16[768,3072]{1,0:T(8,128)(2,1)} fusion(bf16[1080,768]{1,0:T(8,128)(2,1)S(1)} %copy-done.48, bf16[1080,3072]{1,0:T(8,128)(2,1)} %get-tuple-element.228), kind=kOutput, calls=%fused_computation.1 | convolution fusion | flops 5098438656 | bytes 13012992 | tf_op jit(solution)/shard_map/dot_general | solution.py:876
  527.0 13.5 %shard_map.309 = (bf16[1152,768]{1,0:T(8,128)(2,1)}, bf16[1152,768]{1,0:T(8,128)(2,1)}, bf16[1152,768]{1,0:T(8,128)(2,1)}) custom-call(bf16[1152,768]{1,0:T(8,128)(2,1)} %bitcast.33.got_ref, bf16[384,96]{1,0:T(8,128)(2,1)} %constant.48.clone.table_ref, bf16[768,768]{1,0:T(8,128)(2,1)} %get-tuple-element.165.one_ref, ...), custom_call_target="tpu_custom_call" | custom-call | flops 4294967296 | bytes 13049856 | tf_op jit(solution)/shard_map/pallas_call | solution.py:511
  545.3 12.2 %shard_map.310 = (bf16[512,768]{1,0:T(8,128)(2,1)}, bf16[512,768]{1,0:T(8,128)(2,1)}, bf16[512,768]{1,0:T(8,128)(2,1)}, bf16[512,768]{1,0:T(8,128)(2,1)}, bf16[5...) custom-call(s32[5]{0:T(128)} %concatenate.12.place_ref, bf16[768,3072]{1,0:T(8,128)(2,1)} %convolution_convert_fusion.1.in_ref, ...), custom_call_target="tpu_custom_call" | custom-call | bytes 2359296 | tf_op jit(solution)/shard_map/pallas_call | solution.py:647
  614.6 12.6 %collective-permute-start.38 = (bf16[384,768]{1,0:T(8,128)(2,1)}, bf16[384,768]{1,0:T(8,128)(2,1)S(1)}, u32[]{:S(2)}, u32[]{:S(2)}) collective-permute-start(bf16[384,768]{1,0:T(8,128)(2,1)} %shard_map.316.two_ref), channel_id=1, source_target_pairs={{0,8},{8,0},{1,9},{9,1},{2,10},{10,2},{3,11},{11,3},{4,12},{12,4},... | collective-permute-start | bytes 1769480 | tf_op jit(solution)/shard_map/ppermute | solution.py:748
  632.5 30.9 %collective-permute-done.38.two_got_ref = bf16[384,768]{1,0:T(8,128)(2,1)S(1)} collective-permute-done((bf16[384,768]{1,0:T(8,128)(2,1)}, bf16[384,768]{1,0:T(8,128)(2,1)S(1)}, u32[]{:S(2)}, u32[]{:S(2)}) %collective-permute-start.38) | collective-permute-done | bytes 589856 | tf_op jit(solution)/shard_map/ppermute | solution.py:748
  695.1 14.3 %collective-permute-start.39 = (bf16[6,180,768]{2,1,0:T(8,128)(2,1)}, bf16[6,180,768]{2,1,0:T(8,128)(2,1)}, u32[]{:S(2)}, u32[]{:S(2)}) collective-permute-start(bf16[6,180,768]{2,1,0:T(8,128)(2,1)} %get-tuple-element.283), channel_id=1, source_target_pairs={{0,0},{16,8},{1,1},{17,9},{2,2},{18,10},{3,3},{19,11},{4,4},{20,12... | collective-permute-start | bytes 4976648 | tf_op jit(solution)/shard_map/ppermute | solution.py:778
  725.0 15.8 %collective-permute-done.46.refs_3_ = bf16[2,256,768]{2,1,0:T(8,128)(2,1)S(1)} collective-permute-done((bf16[2,256,768]{2,1,0:T(8,128)(2,1)}, bf16[2,256,768]{2,1,0:T(8,128)(2,1)S(1)}, u32[]{:S(2)}, u32[]{:S(2)}) %collective-permute-start.46) | collective-permute-done | bytes 786464 | tf_op jit(solution)/shard_map/ppermute | solution.py:735
  740.9 16.9 %collective-permute-done.47.refs_4_ = bf16[2,256,768]{2,1,0:T(8,128)(2,1)S(1)} collective-permute-done((bf16[2,256,768]{2,1,0:T(8,128)(2,1)}, bf16[2,256,768]{2,1,0:T(8,128)(2,1)S(1)}, u32[]{:S(2)}, u32[]{:S(2)}) %collective-permute-start.47) | collective-permute-done | bytes 786464 | tf_op jit(solution)/shard_map/ppermute | solution.py:735
  (274 shorter events, 375.1 us)
Async XLA Ops:
  46.2 47.2 %all-to-all-start = ((bf16[16,72,768]{2,1,0:T(8,128)(2,1)}), bf16[16,72,768]{2,1,0:T(8,128)(2,1)S(1)}, u32[]{:S(2)}, u32[]{:S(2)}) async-start(bf16[16,72,768]{2,1,0:T(8,128)(2,1)} %bitcast.90), calls=%async_computation | async-start | bytes 3538944 | tf_op jit(solution)/shard_map/all_to_all | solution.py:722
  93.5 60.6 %collective-permute-start.5 = (bf16[768,3072]{1,0:T(8,128)(2,1)}, bf16[768,3072]{1,0:T(8,128)(2,1)}, u32[]{:S(2)}, u32[]{:S(2)}) collective-permute-start(bf16[768,3072]{1,0:T(8,128)(2,1)} %bitcast.108), channel_id=1, source_target_pairs={{0,16},{16,0},{1,17},{17,1},{2,18},{18,2},{3,19},{19,3},{4,20},{20... | collective-permute-start | bytes 14155784 | tf_op jit(solution)/shard_map/ppermute | solution.py:785
  93.7 60.4 %collective-permute-start.6 = (bf16[3072,768]{1,0:T(8,128)(2,1)}, bf16[3072,768]{1,0:T(8,128)(2,1)}, u32[]{:S(2)}, u32[]{:S(2)}) collective-permute-start(bf16[3072,768]{1,0:T(8,128)(2,1)} %bitcast.113), channel_id=1, source_target_pairs={{0,16},{16,0},{1,17},{17,1},{2,18},{18,2},{3,19},{19,3},{4,20},{20... | collective-permute-start | bytes 14155784 | tf_op jit(solution)/shard_map/ppermute | solution.py:785
  140.9 43.1 %collective-permute-start.7 = (bf16[6,180,768]{2,1,0:T(8,128)(2,1)}, bf16[6,180,768]{2,1,0:T(8,128)(2,1)S(1)}, u32[]{:S(2)}, u32[]{:S(2)}) collective-permute-start(bf16[6,180,768]{2,1,0:T(8,128)(2,1)} %get-tuple-element.331), channel_id=1, source_target_pairs={{0,8},{1,9},{2,10},{3,11},{4,12},{5,13},{6,14},{7,15}} | collective-permute-start | bytes 4976648 | tf_op jit(solution)/shard_map/ppermute | solution.py:771
  144.8 39.3 %collective-permute-start.8 = (bf16[6,180,768]{2,1,0:T(8,128)(2,1)S(1)}, bf16[6,180,768]{2,1,0:T(8,128)(2,1)}, u32[]{:S(2)}, u32[]{:S(2)}) collective-permute-start(bf16[6,180,768]{2,1,0:T(8,128)(2,1)S(1)} %get-tuple-element.330), channel_id=1, source_target_pairs={{24,16},{25,17},{26,18},{27,19},{28,20},{29,21},{30,22},{31,23}} | collective-permute-start | bytes 4976648 | tf_op jit(solution)/shard_map/ppermute | solution.py:772
  261.0 52.7 %collective-permute-start.11 = (bf16[6,180,768]{2,1,0:T(8,128)(2,1)S(1)}, bf16[6,180,768]{2,1,0:T(8,128)(2,1)}, u32[]{:S(2)}, u32[]{:S(2)}) collective-permute-start(bf16[6,180,768]{2,1,0:T(8,128)(2,1)S(1)} %copy-done.6), channel_id=1, source_target_pairs={{8,0},{24,8},{9,1},{25,9},{10,2},{26,10},{11,3},{27,11},{12,4},{28... | collective-permute-start | bytes 4976648 | tf_op jit(solution)/shard_map/ppermute | solution.py:778
  262.3 51.4 %collective-permute-start.9 = (bf16[6,180,768]{2,1,0:T(8,128)(2,1)S(1)}, bf16[6,180,768]{2,1,0:T(8,128)(2,1)}, u32[]{:S(2)}, u32[]{:S(2)}) collective-permute-start(bf16[6,180,768]{2,1,0:T(8,128)(2,1)S(1)} %copy-done.6), channel_id=1, source_target_pairs={{0,0},{16,8},{1,1},{17,9},{2,2},{18,10},{3,3},{19,11},{4,4},{20,12... | collective-permute-start | bytes 4976648 | tf_op jit(solution)/shard_map/ppermute | solution.py:778
  304.0 75.5 %collective-permute-start.10 = (bf16[6,180,768]{2,1,0:T(8,128)(2,1)}, bf16[6,180,768]{2,1,0:T(8,128)(2,1)}, u32[]{:S(2)}, u32[]{:S(2)}) collective-permute-start(bf16[6,180,768]{2,1,0:T(8,128)(2,1)} %get-tuple-element.181), channel_id=1, source_target_pairs={{0,16},{16,24},{1,17},{17,25},{2,18},{18,26},{3,19},{19,27},{4,20}... | collective-permute-start | bytes 4976648 | tf_op jit(solution)/shard_map/ppermute | solution.py:778
  311.7 67.8 %collective-permute-start.12 = (bf16[6,180,768]{2,1,0:T(8,128)(2,1)}, bf16[6,180,768]{2,1,0:T(8,128)(2,1)}, u32[]{:S(2)}, u32[]{:S(2)}) collective-permute-start(bf16[6,180,768]{2,1,0:T(8,128)(2,1)} %get-tuple-element.181), channel_id=1, source_target_pairs={{8,16},{24,24},{9,17},{25,25},{10,18},{26,26},{11,19},{27,27},{12,... | collective-permute-start | bytes 4976648 | tf_op jit(solution)/shard_map/ppermute | solution.py:778
  359.5 52.0 %collective-permute-start.14 = (bf16[3072,768]{1,0:T(8,128)(2,1)}, bf16[3072,768]{1,0:T(8,128)(2,1)}, u32[]{:S(2)}, u32[]{:S(2)}) collective-permute-start(bf16[3072,768]{1,0:T(8,128)(2,1)} %convolution_convert_fusion.2.out_ref), channel_id=1, source_target_pairs={{16,0},{17,1},{18,2},{19,3},{20,4},{21,5},{22,6},{23,7},{24,8},{25... | collective-permute-start | bytes 14155784 | tf_op jit(solution)/shard_map/ppermute | solution.py:857
  372.1 39.4 %collective-permute-start.13 = (bf16[768,3072]{1,0:T(8,128)(2,1)}, bf16[768,3072]{1,0:T(8,128)(2,1)}, u32[]{:S(2)}, u32[]{:S(2)}) collective-permute-start(bf16[768,3072]{1,0:T(8,128)(2,1)} %convolution_convert_fusion.3.in_ref), channel_id=1, source_target_pairs={{0,16},{1,17},{2,18},{3,19},{4,20},{5,21},{6,22},{7,23},{8,24},{9,... | collective-permute-start | bytes 14155784 | tf_op jit(solution)/shard_map/ppermute | solution.py:857
  423.7 38.6 %collective-permute-start.15 = (bf16[512,768]{1,0:T(8,128)(2,1)}, bf16[512,768]{1,0:T(8,128)(2,1)}, u32[]{:S(2)}, u32[]{:S(2)}) collective-permute-start(bf16[512,768]{1,0:T(8,128)(2,1)} %get-tuple-element.198), channel_id=1, source_target_pairs={{0,1},{1,0},{2,3},{3,2},{4,5},{5,4},{6,7},{7,6},{8,9},{9,8},{10,11... | collective-permute-start | bytes 2359304 | tf_op jit(solution)/shard_map/ppermute | solution.py:735
  437.1 56.5 %collective-permute-start.18 = (bf16[6,180,768]{2,1,0:T(8,128)(2,1)}, bf16[6,180,768]{2,1,0:T(8,128)(2,1)}, u32[]{:S(2)}, u32[]{:S(2)}) collective-permute-start(bf16[6,180,768]{2,1,0:T(8,128)(2,1)} %get-tuple-element.226), channel_id=1, source_target_pairs={{0,16},{16,24},{1,17},{17,25},{2,18},{18,26},{3,19},{19,27},{4,20}... | collective-permute-start | bytes 4976648 | tf_op jit(solution)/shard_map/ppermute | solution.py:778
  439.6 54.0 %collective-permute-start.19 = (bf16[6,180,768]{2,1,0:T(8,128)(2,1)}, bf16[6,180,768]{2,1,0:T(8,128)(2,1)}, u32[]{:S(2)}, u32[]{:S(2)}) collective-permute-start(bf16[6,180,768]{2,1,0:T(8,128)(2,1)} %get-tuple-element.226), channel_id=1, source_target_pairs={{8,16},{24,24},{9,17},{25,25},{10,18},{26,26},{11,19},{27,27},{12,... | collective-permute-start | bytes 4976648 | tf_op jit(solution)/shard_map/ppermute | solution.py:778
  476.3 50.7 %all-to-all-start.6 = ((bf16[16,72,768]{2,1,0:T(8,128)(2,1)}), bf16[16,72,768]{2,1,0:T(8,128)(2,1)}, u32[]{:S(2)}, u32[]{:S(2)}) async-start(bf16[16,72,768]{2,1,0:T(8,128)(2,1)} %bitcast.89), calls=%async_computation.6 | async-start | bytes 3538944 | tf_op jit(solution)/shard_map/all_to_all | solution.py:722
  492.1 53.2 %collective-permute-start.24 = (bf16[3072,768]{1,0:T(8,128)(2,1)}, bf16[3072,768]{1,0:T(8,128)(2,1)}, u32[]{:S(2)}, u32[]{:S(2)}) collective-permute-start(bf16[3072,768]{1,0:T(8,128)(2,1)} %convolution_convert_fusion.out_ref), channel_id=1, source_target_pairs={{16,0},{17,1},{18,2},{19,3},{20,4},{21,5},{22,6},{23,7},{24,8},{25... | collective-permute-start | bytes 14155784 | tf_op jit(solution)/shard_map/ppermute | solution.py:875
  504.8 40.5 %collective-permute-start.23 = (bf16[768,3072]{1,0:T(8,128)(2,1)}, bf16[768,3072]{1,0:T(8,128)(2,1)}, u32[]{:S(2)}, u32[]{:S(2)}) collective-permute-start(bf16[768,3072]{1,0:T(8,128)(2,1)} %convolution_convert_fusion.1.in_ref), channel_id=1, source_target_pairs={{0,16},{1,17},{2,18},{3,19},{4,20},{5,21},{6,22},{7,23},{8,24},{9,... | collective-permute-start | bytes 14155784 | tf_op jit(solution)/shard_map/ppermute | solution.py:877
  614.6 48.8 %collective-permute-start.38 = (bf16[384,768]{1,0:T(8,128)(2,1)}, bf16[384,768]{1,0:T(8,128)(2,1)S(1)}, u32[]{:S(2)}, u32[]{:S(2)}) collective-permute-start(bf16[384,768]{1,0:T(8,128)(2,1)} %shard_map.316.two_ref), channel_id=1, source_target_pairs={{0,8},{8,0},{1,9},{9,1},{2,10},{10,2},{3,11},{11,3},{4,12},{12,4},... | collective-permute-start | bytes 1769480 | tf_op jit(solution)/shard_map/ppermute | solution.py:748
  630.3 44.1 %collective-permute-start.34 = (bf16[384,768]{1,0:T(8,128)(2,1)}, bf16[384,768]{1,0:T(8,128)(2,1)S(1)}, u32[]{:S(2)}, u32[]{:S(2)}) collective-permute-start(bf16[384,768]{1,0:T(8,128)(2,1)} %shard_map.315.one_ref), channel_id=1, source_target_pairs={{0,8},{8,0},{1,9},{9,1},{2,10},{10,2},{3,11},{11,3},{4,12},{12,4},... | collective-permute-start | bytes 1769480 | tf_op jit(solution)/shard_map/ppermute | solution.py:748
  695.1 76.3 %collective-permute-start.39 = (bf16[6,180,768]{2,1,0:T(8,128)(2,1)}, bf16[6,180,768]{2,1,0:T(8,128)(2,1)}, u32[]{:S(2)}, u32[]{:S(2)}) collective-permute-start(bf16[6,180,768]{2,1,0:T(8,128)(2,1)} %get-tuple-element.283), channel_id=1, source_target_pairs={{0,0},{16,8},{1,1},{17,9},{2,2},{18,10},{3,3},{19,11},{4,4},{20,12... | collective-permute-start | bytes 4976648 | tf_op jit(solution)/shard_map/ppermute | solution.py:778
  711.6 59.8 %all-to-all-start.9 = ((bf16[16,208,128]{2,1,0:T(8,128)(2,1)}), bf16[16,208,128]{2,1,0:T(8,128)(2,1)}, u32[]{:S(2)}, u32[]{:S(2)}) async-start(bf16[16,208,128]{2,1,0:T(8,128)(2,1)} %shard_map.318), calls=%async_computation.9 | async-start | bytes 1703936 | tf_op jit(solution)/shard_map/all_to_all | solution.py:766
  720.8 37.0 %collective-permute-start.47 = (bf16[2,256,768]{2,1,0:T(8,128)(2,1)}, bf16[2,256,768]{2,1,0:T(8,128)(2,1)S(1)}, u32[]{:S(2)}, u32[]{:S(2)}) collective-permute-start(bf16[2,256,768]{2,1,0:T(8,128)(2,1)} %get-tuple-element.305.refs_1_), channel_id=1, source_target_pairs={{0,4},{1,5},{2,6},{3,7},{4,0},{5,1},{6,2},{7,3},{8,12},{9,13},{10,... | collective-permute-start | bytes 2359304 | tf_op jit(solution)/shard_map/ppermute | solution.py:735
  723.8 49.3 %collective-permute-start.40 = (bf16[6,180,768]{2,1,0:T(8,128)(2,1)}, bf16[6,180,768]{2,1,0:T(8,128)(2,1)}, u32[]{:S(2)}, u32[]{:S(2)}) collective-permute-start(bf16[6,180,768]{2,1,0:T(8,128)(2,1)} %get-tuple-element.283), channel_id=1, source_target_pairs={{8,0},{24,8},{9,1},{25,9},{10,2},{26,10},{11,3},{27,11},{12,4},{28... | collective-permute-start | bytes 4976648 | tf_op jit(solution)/shard_map/ppermute | solution.py:778
  771.5 41.7 %collective-permute-start.41 = (bf16[3328,128]{1,0:T(8,128)(2,1)}, bf16[3328,128]{1,0:T(8,128)(2,1)S(1)}, u32[]{:S(2)}, u32[]{:S(2)}) collective-permute-start(bf16[3328,128]{1,0:T(8,128)(2,1)} %bitcast.40.own_ref), channel_id=1, source_target_pairs={{0,16},{16,0},{1,17},{17,1},{2,18},{18,2},{3,19},{19,3},{4,20},{20... | collective-permute-start | bytes 2555912 | tf_op jit(solution)/shard_map/ppermute | solution.py:767
  (85 other events, 1226.8 us)

commit v4 on v3

--- a/solution.py
+++ b/solution.py
@@ -708,12 +708,19 @@
     )(place, *pieces, *kept)
 
 
-def deliver(core, layer_zero, layer_one):
-    return jnp.stack([jnp.where(core == 0, a, b) for a, b in zip(layer_zero, layer_one)])[None]
+def deliver(core, half, layer_zero, layer_one):
+    first, second = (list(parts[:2]) for parts in (layer_zero, layer_one))
+    for level, (parts, whole) in enumerate(((first, layer_zero), (second, layer_one))):
+        parts[level] = jnp.where(half == level, whole[2], parts[level])
+    return jnp.stack([jnp.where(core == 0, a, b) for a, b in zip(first, second)])[None]
 
 
 def after(item, *earlier):
     return lax.optimization_barrier((item, *earlier))[0]
+
+
+def together(*items):
+    return lax.optimization_barrier(items)
 
 
 def exchange(item):
@@ -755,13 +762,13 @@
     return mine, call(pack_kernel, [((2, rows // ROUTES, width), BF16)] * ROUTES, [], place, mine, got, scalars=1)
 
 
-def small_sums(parts, core):
+def small_sums(parts, earlier):
     slabs = lax.axis_size("lane") * lax.axis_size("half")
     count = sum(a.shape[0] for a in parts)
     each = -(-count // (slabs * 8)) * 8
     parts = [*parts, jnp.zeros((slabs * each - count, 128), BF16)]
     pieces = jnp.concatenate(parts, 0).reshape(slabs, each, 128)
-    got = lax.all_to_all(pieces, SLAB, 0, 0, tiled=True)
+    got = after(lax.all_to_all(pieces, SLAB, 0, 0, tiled=True), *earlier)
     spread = call(small_sum_kernel, [(got.shape, BF16)], [], got)[0]
     total = lax.all_to_all(spread, SLAB, 0, 0, tiled=True).reshape(slabs * each, 128)
     return total, lax.ppermute(total, "section", [(0, 1), (1, 0)])
@@ -775,7 +782,8 @@
 
 
 def send_out(item, level):
-    return [lax.ppermute(item, ("section", "half"), [(micro, 2 * level), (2 + micro, 2 * level + 1)]) for micro in range(2)]
+    pairs = lambda micro: [(2 * side + micro, 2 * level + side) for side in range(2)]
+    return [lax.ppermute(item, ("section", "half"), [p for p in pairs(micro) if p[0] != p[1]]) for micro in range(2)] + [item]
 
 
 ACROSS = (((0,), (0,)), ((), ()))
@@ -861,7 +869,7 @@
     sums_two, from_two = after((sums_two, from_two), sent)
     sends_two, keeps_two = first_shed(place, sums_two[0], from_two[0], sums_two[1], from_two[1])
     gots_two = swap_all(sends_two, 0)
-    activations = deliver(core, delivered_one, delivered_two)
+    activations = deliver(core, half, delivered_one, delivered_two)
     grad_x_two, grad, small_two = front_back(after(got, activations, *sends_two), grad_mixed, out_one, vec_two, known, lay)
     grads_two = send_out(grad_x_two, 1)
     grad_hidden, in_bias_one, grad_norm = dense_back(place, grad, pairs, bend_one, 0)
@@ -869,26 +877,28 @@
     gots_two = swap_all(sends_two, 1)
     sent, grad_mixed, small_one = middle_back(after(grad_norm, *sends_two), mixed_one, grad, vec_one, lay)
     got = exchange(sent)
-    norm_one, activated_one = after((norm_one, activated_one), sent)
+    norm_one, activated_one = after((norm_one, activated_one), sent, *gots_two)
     norm_one = after(norm_one, *grads_two)
     grad_out = lax.dot_general(activated_one, grad, ACROSS, preferred_element_type=F32).astype(BF16)
-    grad_out_got = lax.ppermute(grad_out, "section", [(1, 0)])
     grad_in = lax.dot_general(norm_one, grad_hidden, ACROSS, preferred_element_type=F32).astype(BF16)
-    grad_in_got = lax.ppermute(grad_in, "section", [(0, 1)])
     for at in range(2, levels):
         sends_two, keeps_two = shed(bits[at], keeps_two, gots_two)
         gots_two = swap_all(sends_two, at)
     got = after(got, grad_in, grad_out, *sends_two)
+    grad_in, grad_out = after((grad_in, grad_out), *sends_two)
+    grad_out_got = lax.ppermute(grad_out, "section", [(1, 0)])
+    grad_in_got = lax.ppermute(grad_in, "section", [(0, 1)])
     sent, grad_second, grad_first = spectral_back(got, one_a, two_a, slope_one, factor_one, lay)
-    stacked_two = stack(keeps_two, after(gots_two, sent))
+    sent, gots_two = together(sent, gots_two)
+    stacked_two = stack(keeps_two, gots_two)
     halved_two = across_halves(stacked_two)
-    grad_in, grad_in_got, grad_out, grad_out_got = after((grad_in, grad_in_got, grad_out, grad_out_got), sent)
+    grad_in, grad_in_got, grad_out, grad_out_got = after((grad_in, grad_in_got, grad_out, grad_out_got), sent, stacked_two)
     sends, keeps = first_shed(place, grad_in, grad_in_got, grad_out, grad_out_got)
     gots = swap_all(sends, 0)
     got = exchange(sent)
     blocks_one, known = spectral_grads(low_one, grad_first, active_one, grad_second, small_one, in_bias_one)
     grad_x_one, _, small_one = front_back(after(got, *sends), grad_mixed, x, vec_one, known, lay)
-    gots = after(gots, grad_x_one)
+    gots = after(gots, grad_x_one, halved_two)
     for at in range(1, levels):
         sends, keeps = shed(bits[at], keeps, gots)
         gots = swap_all(sends, at)
@@ -898,19 +908,21 @@
     for at in reversed(range(levels)):
         gots = swap_all(own, at)
         if at > 0:
-            own = double(bits[at], own, gots)
-    total, other = small_sums(after([blocks_one, blocks_two, small_one, small_two], mine), core)
+            own = double(bits[at], own, after(gots, *grads_one) if at == 1 else gots)
+    total, other = small_sums([blocks_one, blocks_two, small_one, small_two], [stacked])
     row = ((1, width), F32)
     outs = [((2, BLOCKS, size, size), F32)] * 2 + [((2, width), F32)] * 2 + [row] * 4 + [((4, width), F32), row]
     one, two, bias_one, bias_two, gain_one, shift_one, gain_two, shift_two, in_bias, out_bias = call(
         small_finish_kernel, outs, [(G_ROWS, width)] * 2, place, total, other, scalars=1, blocks=blocks
     )
     dense_grads = finish(place, own, dense_in.shape, False)
+    input_grads = deliver(core, half, grads_one, grads_two)
+    bias_one, bias_two, in_bias = bias_one.reshape(1, 2, BLOCKS, size), bias_two.reshape(1, 2, BLOCKS, size), in_bias.reshape(1, -1)
+    gots = after(gots, input_grads, bias_one, bias_two, in_bias, gain_one)
     grad_in, grad_out = finish(place, gots, dense_in.shape, True, dense_grads)
     return (
-        activations, deliver(core, grads_one, grads_two),
-        gain_one, shift_one, one[None], bias_one.reshape(1, 2, BLOCKS, size), two[None], bias_two.reshape(1, 2, BLOCKS, size),
-        gain_two, shift_two, grad_in[None], in_bias.reshape(1, -1), grad_out[None], out_bias,
+        activations, input_grads, gain_one, shift_one, one[None], bias_one, two[None], bias_two,
+        gain_two, shift_two, grad_in[None], in_bias, grad_out[None], out_bias,
     )
 
 

time: 831 us -> 794 us (0.955)
  waiting for transfers between devices: 143 us -> 116 us
  starting transfers between devices: 171 us -> 159 us
    ppermute x27, waiting for transfers between devices: 69.7 us -> 20.6 us  [swap(): lax.ppermute(item, 'lane', [(i, i ^ bit) for i in range(lax.axis_size('la...]
    ppermute x8, waiting for transfers between devices: 0.02 us -> 28.1 us  [send_out(): lax.ppermute(item, ('section', 'half'), [p for p in pairs(micro) if p[0]...]
    ppermute x8, starting transfers between devices: 33.2 us -> 20.4 us  [send_out(): lax.ppermute(item, ('section', 'half'), [p for p in pairs(micro) if p[0]...]
    ppermute x2, starting transfers between devices: 14.7 us -> 2.4 us  [across_halves(): return lax.ppermute(item, 'half', [(0, 1), (1, 0)])]
    ppermute x2, waiting for transfers between devices: 42 us -> 30.9 us  [across_halves(): return lax.ppermute(item, 'half', [(0, 1), (1, 0)])]
    unnamed x109 -> x79, local copies, waits for them, and re-layouts: 24.8 us -> 26.6 us
  transfers between devices with their start and end apart: 59 -> 59, of which waited for: 20 -> 16; matrix products, arithmetic and copies ran while one was open for 8% -> 10% of each run, Pallas kernels for 35% -> 35%
where the time goes in v4:
time: 794 us; the launch traced here: 785 us
  Pallas kernels  320 us (40%)
  starting transfers between devices  159 us (20%)
  waiting for transfers between devices  116 us (15%)
  blocking collectives  86.5 us (11%)
  matrix products  45.1 us (6%)
  local copies, waits for them, and re-layouts  43.1 us (5%)
  other arithmetic  13.5 us (2%)
    pallas_call x27, Pallas kernels, call(): pl.pallas_call(functools.partial(body, **named), out_shape=[jax.ShapeDtyp...  175 us
    all_to_all x3, blocking collectives, exchange(): lax.all_to_all(pieces, ROWS_AXES, 0, 0, tiled=True).reshape(item.shape)  86.5 us
    pallas_call x2, Pallas kernels, dense(): pl.pallas_call(functools.partial(dense_kernel, level=level), grid_spec=pl...  60.2 us
    all_to_all x5, starting transfers between devices, exchange(): lax.all_to_all(pieces, ROWS_AXES, 0, 0, tiled=True).reshape(item.shape)  45.2 us
    pallas_call x2, Pallas kernels, dense_back(): pl.pallas_call(functools.partial(dense_back_kernel, level=level), grid_sp...  41.5 us
    ppermute x27, starting transfers between devices, swap(): lax.ppermute(item, 'lane', [(i, i ^ bit) for i in range(lax.axis_size('la...  33.4 us
    ppermute x2, waiting for transfers between devices, across_halves(): return lax.ppermute(item, 'half', [(0, 1), (1, 0)])  30.9 us
    ppermute x8, waiting for transfers between devices, send_out(): lax.ppermute(item, ('section', 'half'), [p for p in pairs(micro) if p[0]...  28.1 us
  transfers between devices with their start and end apart: 59, of which 16 were waited for; matrix products, arithmetic and copies ran while one was open for 10% of the time, Pallas kernels for 35%

profile of v4, /device:TPU:0, one launch (start us, length us, event | category | flops | bytes accessed | tf_op | source)
XLA Modules:
  0.0 785.1 jit_solution(10483252498929176883)
XLA Ops:
  24.4 12.5 %collective-permute-done = bf16[6,180,768]{2,1,0:T(8,128)(2,1)} collective-permute-done((bf16[6,180,768]{2,1,0:T(8,128)(2,1)}, bf16[6,180,768]{2,1,0:T(8,128)(2,1)}, u32[]{:S(2)}, u32[]{:S(2)}) %collective-permute-start) | collective-permute-done | bytes 1658912 | tf_op jit(solution)/shard_map/ppermute | solution.py:778
  46.2 24.5 %all-to-all-start = ((bf16[16,72,768]{2,1,0:T(8,128)(2,1)}), bf16[16,72,768]{2,1,0:T(8,128)(2,1)S(1)}, u32[]{:S(2)}, u32[]{:S(2)}) async-start(bf16[16,72,768]{2,1,0:T(8,128)(2,1)} %bitcast.91), calls=%async_computation | async-start | bytes 3538944 | tf_op jit(solution)/shard_map/all_to_all | solution.py:729
  78.9 14.6 %all-to-all-done = bf16[16,72,768]{2,1,0:T(8,128)(2,1)S(1)} async-done(((bf16[16,72,768]{2,1,0:T(8,128)(2,1)}), bf16[16,72,768]{2,1,0:T(8,128)(2,1)S(1)}, u32[]{:S(2)}, u32[]{:S(2)}) %all-to-all-start) | async-done | bytes 1769504 | tf_op jit(solution)/shard_map/all_to_all | solution.py:729
  94.7 14.8 %shard_map.292 = (bf16[1152,768]{1,0:T(8,128)(2,1)}, bf16[1152,768]{1,0:T(8,128)(2,1)}, bf16[1152,768]{1,0:T(8,128)(2,1)}, bf16[1152,768]{1,0:T(8,128)(2,1)}, bf16[1152,768]{1,0:T(8,128)(2,1)}) custom-call(bf16[1152,768]{1,0:T(8,128)(2,1)} %bitcast.88, bf16[384,96]{1,0:T(8,128)(2,1)} %constant.48.clone.table_ref, ...), custom_call_target="tpu_custom_call" | custom-call | flops 4294967296 | bytes 13083648 | tf_op jit(solution)/shard_map/pallas_call | solution.py:511
  109.5 29.6 %all_to_all.50 = bf16[16,72,768]{2,1,0:T(8,128)(2,1)} all-to-all(bf16[16,72,768]{2,1,0:T(8,128)(2,1)} %bitcast.98), channel_id=1, replica_groups=mesh['section'=2,'half'=2,'lane'=8] {'section','lane'}, dimensions={0} | all-to-all | bytes 3538944 | tf_op jit(solution)/shard_map/all_to_all | solution.py:729
  154.2 29.9 %shard_map.294 = (bf16[6,180,768]{2,1,0:T(8,128)(2,1)}, bf16[1080,3072]{1,0:T(8,128)(2,1)}, bf16[1080,3072]{1,0:T(8,128)(2,1)}) custom-call(s32[5]{0:T(128)} %concatenate.12.place_ref, bf16[1080,768]{1,0:T(8,128)(2,1)} %get-tuple-element.233.norm_ref, bf16[768,3072]{1,0:T(8,128)(2,1)} %bitcast.109, bf16[768,3072]{1,0:T(8,128)(2,1)} %collective-permute-done.5.in_other_ref, ...), custom_call_target="tpu_custom_call" | custom-call | flops 10192158720 | bytes 31457280 | tf_op jit(solution)/shard_map/pallas_call | solution.py:575
  189.7 28.6 %all_to_all.51 = bf16[16,72,768]{2,1,0:T(8,128)(2,1)} all-to-all(bf16[16,72,768]{2,1,0:T(8,128)(2,1)} %bitcast.100), channel_id=1, replica_groups=mesh['section'=2,'half'=2,'lane'=8] {'section','lane'}, dimensions={0} | all-to-all | bytes 3538944 | tf_op jit(solution)/shard_map/all_to_all | solution.py:729
  218.4 14.8 %shard_map.296 = (bf16[1152,768]{1,0:T(8,128)(2,1)}, bf16[1152,768]{1,0:T(8,128)(2,1)}, bf16[1152,768]{1,0:T(8,128)(2,1)}, bf16[1152,768]{1,0:T(8,128)(2,1)}, bf16[1152,768]{1,0:T(8,128)(2,1)}) custom-call(bf16[1152,768]{1,0:T(8,128)(2,1)} %bitcast.97, bf16[384,96]{1,0:T(8,128)(2,1)} %constant.48.clone.table_ref, ...), custom_call_target="tpu_custom_call" | custom-call | flops 4294967296 | bytes 13083648 | tf_op jit(solution)/shard_map/pallas_call | solution.py:511
  233.1 28.3 %all_to_all.52 = bf16[16,72,768]{2,1,0:T(8,128)(2,1)} all-to-all(bf16[16,72,768]{2,1,0:T(8,128)(2,1)} %bitcast.99), channel_id=1, replica_groups=mesh['section'=2,'half'=2,'lane'=8] {'section','lane'}, dimensions={0} | all-to-all | bytes 3538944 | tf_op jit(solution)/shard_map/all_to_all | solution.py:729
  273.9 30.3 %shard_map.298 = (bf16[6,180,768]{2,1,0:T(8,128)(2,1)}, bf16[1080,3072]{1,0:T(8,128)(2,1)}, bf16[1080,3072]{1,0:T(8,128)(2,1)}) custom-call(s32[5]{0:T(128)} %concatenate.12.place_ref, bf16[1080,768]{1,0:T(8,128)(2,1)} %get-tuple-element.193.norm_ref, bf16[768,3072]{1,0:T(8,128)(2,1)} %bitcast.110, bf16[768,3072]{1,0:T(8,128)(2,1)} %collective-permute-done.5.in_other_ref, ...), custom_call_target="tpu_custom_call" | custom-call | flops 10192158720 | bytes 31457280 | tf_op jit(solution)/shard_map/pallas_call | solution.py:575
  314.0 20.6 %shard_map.299 = (bf16[1080,3072]{1,0:T(8,128)(2,1)}, f32[4,768]{1,0:T(4,128)}, f32[1080,768]{1,0:T(8,128)}) custom-call(s32[5]{0:T(128)} %concatenate.12.place_ref, bf16[1080,768]{1,0:T(8,128)(2,1)} %reshape.111.grad_ref, bf16[3072,768]{1,0:T(8,128)(2,1)} %bitcast.116, bf16[3072,768]{1,0:T(8,128)(2,1)} %collective-permute-done.6.out_other_ref, ...), custom_call_target="tpu_custom_call" | custom-call | flops 10192158720 | bytes 31457280 | tf_op jit(solution)/shard_map/pallas_call | solution.py:599
  334.6 9.9 %shard_map.300 = (bf16[1152,768]{1,0:T(8,128)(2,1)}, f32[1080,768]{1,0:T(8,128)}, f32[3,768]{1,0:T(4,128)}) custom-call(f32[1080,768]{1,0:T(8,128)} %get-tuple-element.190.norm_ref, f32[1080,768]{1,0:T(8,128)} %get-tuple-element.186.mixed_ref, bf16[1080,768]{1,0:T(8,128)(2,1)} %reshape.111.grad_ref, f32[11,768]{1,0:T(8,128)} %get-tuple-element.346.vec_ref, ...), custom_call_target="tpu_custom_call" | custom-call | flops 1073741824 | bytes 13562880 | tf_op jit(solution)/shard_map/pallas_call | solution.py:511
  348.3 11.5 %convolution_convert_fusion.2.out_ref = bf16[3072,768]{1,0:T(8,128)(2,1)} fusion(bf16[1080,3072]{1,0:T(8,128)(2,1)} %get-tuple-element.195, bf16[1080,768]{1,0:T(8,128)(2,1)S(1)} %copy-done.3), kind=kOutput, calls=%fused_computation.2 | convolution fusion | flops 5098438656 | bytes 13012992 | tf_op jit(solution)/shard_map/dot_general | solution.py:863
  361.5 11.0 %convolution_convert_fusion.3.in_ref = bf16[768,3072]{1,0:T(8,128)(2,1)} fusion(bf16[1080,768]{1,0:T(8,128)(2,1)S(1)} %copy-done.34, bf16[1080,3072]{1,0:T(8,128)(2,1)} %get-tuple-element.194), kind=kOutput, calls=%fused_computation.3 | convolution fusion | flops 5098438656 | bytes 13012992 | tf_op jit(solution)/shard_map/dot_general | solution.py:862
  381.2 13.6 %shard_map.301 = (bf16[1152,768]{1,0:T(8,128)(2,1)}, bf16[1152,768]{1,0:T(8,128)(2,1)}, bf16[1152,768]{1,0:T(8,128)(2,1)}) custom-call(bf16[1152,768]{1,0:T(8,128)(2,1)} %bitcast.93, bf16[384,96]{1,0:T(8,128)(2,1)} %constant.48.clone.table_ref, bf16[768,768]{1,0:T(8,128)(2,1)} %get-tuple-element.181.one_ref, bf16[768,768]{1,0:T(8,128)(2,1)} %get-tuple-element.182.two_ref, ...), custom_call_target="tpu_custom_call" | custom-call | flops 4294967296 | bytes 13049856 | tf_op jit(solution)/shard_map/pallas_call | solution.py:511
  412.3 12.2 %shard_map.302 = (bf16[512,768]{1,0:T(8,128)(2,1)}, bf16[512,768]{1,0:T(8,128)(2,1)}, bf16[512,768]{1,0:T(8,128)(2,1)}, bf16[512,768]{1,0:T(8,128)(2,1)}, bf16[5...) custom-call(s32[5]{0:T(128)} %concatenate.12.place_ref, bf16[768,3072]{1,0:T(8,128)(2,1)} %convolution_convert_fusion.3.in_ref, ...), custom_call_target="tpu_custom_call" | custom-call | bytes 2359296 | tf_op jit(solution)/shard_map/pallas_call | solution.py:647
  437.8 20.9 %shard_map.305 = (bf16[1080,3072]{1,0:T(8,128)(2,1)}, f32[4,768]{1,0:T(4,128)}, f32[1080,768]{1,0:T(8,128)}) custom-call(s32[5]{0:T(128)} %concatenate.12.place_ref, bf16[1080,768]{1,0:T(8,128)(2,1)} %get-tuple-element.216.grad_ref, bf16[3072,768]{1,0:T(8,128)(2,1)} %bitcast.117, bf16[3072,768]{1,0:T(8,128)(2,1)} %collective-permute-done.6.out_other_ref, ...), custom_call_target="tpu_custom_call" | custom-call | flops 10192158720 | bytes 31457280 | tf_op jit(solution)/shard_map/pallas_call | solution.py:599
  487.3 11.5 %convolution_convert_fusion.out_ref = bf16[3072,768]{1,0:T(8,128)(2,1)} fusion(bf16[1080,3072]{1,0:T(8,128)(2,1)} %get-tuple-element.235, bf16[1080,768]{1,0:T(8,128)(2,1)S(1)} %copy-done.8), kind=kOutput, calls=%fused_computation | convolution fusion | flops 5098438656 | bytes 13012992 | tf_op jit(solution)/shard_map/dot_general | solution.py:882
  498.8 11.1 %convolution_convert_fusion.1.in_ref = bf16[768,3072]{1,0:T(8,128)(2,1)} fusion(bf16[1080,768]{1,0:T(8,128)(2,1)S(1)} %copy-done.33, bf16[1080,3072]{1,0:T(8,128)(2,1)} %get-tuple-element.234), kind=kOutput, calls=%fused_computation.1 | convolution fusion | flops 5098438656 | bytes 13012992 | tf_op jit(solution)/shard_map/dot_general | solution.py:883
  509.9 14.5 %collective-permute-start.26 = (bf16[768,3072]{1,0:T(8,128)(2,1)}, bf16[768,3072]{1,0:T(8,128)(2,1)}, u32[]{:S(2)}, u32[]{:S(2)}) collective-permute-start(bf16[768,3072]{1,0:T(8,128)(2,1)} %convolution_convert_fusion.1.in_ref), channel_id=1, source_target_pairs={{0,16},{1,17},{2,18},{3,19},{4,20},{5,21},{6,22},{7,23},{8,24},{9,... | collective-permute-start | bytes 14155784 | tf_op jit(solution)/shard_map/ppermute | solution.py:890
  528.8 13.5 %shard_map.309 = (bf16[1152,768]{1,0:T(8,128)(2,1)}, bf16[1152,768]{1,0:T(8,128)(2,1)}, bf16[1152,768]{1,0:T(8,128)(2,1)}) custom-call(bf16[1152,768]{1,0:T(8,128)(2,1)} %bitcast.33.got_ref, bf16[384,96]{1,0:T(8,128)(2,1)} %constant.48.clone.table_ref, bf16[768,768]{1,0:T(8,128)(2,1)} %get-tuple-element.171.one_ref, ...), custom_call_target="tpu_custom_call" | custom-call | flops 4294967296 | bytes 13049856 | tf_op jit(solution)/shard_map/pallas_call | solution.py:511
  550.5 12.2 %shard_map.311 = (bf16[512,768]{1,0:T(8,128)(2,1)}, bf16[512,768]{1,0:T(8,128)(2,1)}, bf16[512,768]{1,0:T(8,128)(2,1)}, bf16[512,768]{1,0:T(8,128)(2,1)}, bf16[5...) custom-call(s32[5]{0:T(128)} %concatenate.12.place_ref, bf16[768,3072]{1,0:T(8,128)(2,1)} %convolution_convert_fusion.1.in_ref, ...), custom_call_target="tpu_custom_call" | custom-call | bytes 2359296 | tf_op jit(solution)/shard_map/pallas_call | solution.py:647
  639.9 24.7 %collective-permute-done.38.one_got_ref = bf16[384,768]{1,0:T(8,128)(2,1)S(1)} collective-permute-done((bf16[384,768]{1,0:T(8,128)(2,1)}, bf16[384,768]{1,0:T(8,128)(2,1)S(1)}, u32[]{:S(2)}, u32[]{:S(2)}) %collective-permute-start.38) | collective-permute-done | bytes 589856 | tf_op jit(solution)/shard_map/ppermute | solution.py:755
  697.1 28.1 %collective-permute-done.40 = bf16[6,180,768]{2,1,0:T(8,128)(2,1)} collective-permute-done((bf16[6,180,768]{2,1,0:T(8,128)(2,1)}, bf16[6,180,768]{2,1,0:T(8,128)(2,1)}, u32[]{:S(2)}, u32[]{:S(2)}) %collective-permute-start.40) | collective-permute-done | bytes 1658912 | tf_op jit(solution)/shard_map/ppermute | solution.py:786
  (244 shorter events, 340.6 us)
Async XLA Ops:
  46.2 47.2 %all-to-all-start = ((bf16[16,72,768]{2,1,0:T(8,128)(2,1)}), bf16[16,72,768]{2,1,0:T(8,128)(2,1)S(1)}, u32[]{:S(2)}, u32[]{:S(2)}) async-start(bf16[16,72,768]{2,1,0:T(8,128)(2,1)} %bitcast.91), calls=%async_computation | async-start | bytes 3538944 | tf_op jit(solution)/shard_map/all_to_all | solution.py:729
  93.5 60.7 %collective-permute-start.5 = (bf16[768,3072]{1,0:T(8,128)(2,1)}, bf16[768,3072]{1,0:T(8,128)(2,1)}, u32[]{:S(2)}, u32[]{:S(2)}) collective-permute-start(bf16[768,3072]{1,0:T(8,128)(2,1)} %bitcast.108), channel_id=1, source_target_pairs={{0,16},{16,0},{1,17},{17,1},{2,18},{18,2},{3,19},{19,3},{4,20},{20... | collective-permute-start | bytes 14155784 | tf_op jit(solution)/shard_map/ppermute | solution.py:793
  93.7 60.5 %collective-permute-start.6 = (bf16[3072,768]{1,0:T(8,128)(2,1)}, bf16[3072,768]{1,0:T(8,128)(2,1)}, u32[]{:S(2)}, u32[]{:S(2)}) collective-permute-start(bf16[3072,768]{1,0:T(8,128)(2,1)} %bitcast.113), channel_id=1, source_target_pairs={{0,16},{16,0},{1,17},{17,1},{2,18},{18,2},{3,19},{19,3},{4,20},{20... | collective-permute-start | bytes 14155784 | tf_op jit(solution)/shard_map/ppermute | solution.py:793
  140.9 43.3 %collective-permute-start.7 = (bf16[6,180,768]{2,1,0:T(8,128)(2,1)}, bf16[6,180,768]{2,1,0:T(8,128)(2,1)S(1)}, u32[]{:S(2)}, u32[]{:S(2)}) collective-permute-start(bf16[6,180,768]{2,1,0:T(8,128)(2,1)} %get-tuple-element.343), channel_id=1, source_target_pairs={{0,8},{1,9},{2,10},{3,11},{4,12},{5,13},{6,14},{7,15}} | collective-permute-start | bytes 4976648 | tf_op jit(solution)/shard_map/ppermute | solution.py:778
  144.7 39.4 %collective-permute-start.8 = (bf16[6,180,768]{2,1,0:T(8,128)(2,1)S(1)}, bf16[6,180,768]{2,1,0:T(8,128)(2,1)}, u32[]{:S(2)}, u32[]{:S(2)}) collective-permute-start(bf16[6,180,768]{2,1,0:T(8,128)(2,1)S(1)} %get-tuple-element.342), channel_id=1, source_target_pairs={{24,16},{25,17},{26,18},{27,19},{28,20},{29,21},{30,22},{31,23}} | collective-permute-start | bytes 4976648 | tf_op jit(solution)/shard_map/ppermute | solution.py:779
  261.4 52.5 %collective-permute-start.11 = (bf16[6,180,768]{2,1,0:T(8,128)(2,1)S(1)}, bf16[6,180,768]{2,1,0:T(8,128)(2,1)}, u32[]{:S(2)}, u32[]{:S(2)}) collective-permute-start(bf16[6,180,768]{2,1,0:T(8,128)(2,1)S(1)} %copy-done.1), channel_id=1, source_target_pairs={{8,0},{24,8},{9,1},{25,9},{10,2},{26,10},{11,3},{27,11},{12,4},{28... | collective-permute-start | bytes 4976648 | tf_op jit(solution)/shard_map/ppermute | solution.py:786
  262.7 51.2 %collective-permute-start.9 = (bf16[6,180,768]{2,1,0:T(8,128)(2,1)S(1)}, bf16[6,180,768]{2,1,0:T(8,128)(2,1)}, u32[]{:S(2)}, u32[]{:S(2)}) collective-permute-start(bf16[6,180,768]{2,1,0:T(8,128)(2,1)S(1)} %copy-done.1), channel_id=1, source_target_pairs={{16,8},{17,9},{18,10},{19,11},{20,12},{21,13},{22,14},{23,15}} | collective-permute-start | bytes 4976648 | tf_op jit(solution)/shard_map/ppermute | solution.py:786
  304.2 75.8 %collective-permute-start.10 = (bf16[6,180,768]{2,1,0:T(8,128)(2,1)}, bf16[6,180,768]{2,1,0:T(8,128)(2,1)}, u32[]{:S(2)}, u32[]{:S(2)}) collective-permute-start(bf16[6,180,768]{2,1,0:T(8,128)(2,1)} %get-tuple-element.187), channel_id=1, source_target_pairs={{0,16},{16,24},{1,17},{17,25},{2,18},{18,26},{3,19},{19,27},{4,20}... | collective-permute-start | bytes 4976648 | tf_op jit(solution)/shard_map/ppermute | solution.py:786
  311.9 68.1 %collective-permute-start.12 = (bf16[6,180,768]{2,1,0:T(8,128)(2,1)}, bf16[6,180,768]{2,1,0:T(8,128)(2,1)}, u32[]{:S(2)}, u32[]{:S(2)}) collective-permute-start(bf16[6,180,768]{2,1,0:T(8,128)(2,1)} %get-tuple-element.187), channel_id=1, source_target_pairs={{8,16},{9,17},{10,18},{11,19},{12,20},{13,21},{14,22},{15,23}} | collective-permute-start | bytes 4976648 | tf_op jit(solution)/shard_map/ppermute | solution.py:786
  344.4 35.6 %all-to-all-start.4 = ((bf16[16,72,768]{2,1,0:T(8,128)(2,1)}), bf16[16,72,768]{2,1,0:T(8,128)(2,1)S(1)}, u32[]{:S(2)}, u32[]{:S(2)}) async-start(bf16[16,72,768]{2,1,0:T(8,128)(2,1)} %bitcast.94), calls=%async_computation.4 | async-start | bytes 3538944 | tf_op jit(solution)/shard_map/all_to_all | solution.py:729
  359.8 52.4 %collective-permute-start.14 = (bf16[3072,768]{1,0:T(8,128)(2,1)}, bf16[3072,768]{1,0:T(8,128)(2,1)}, u32[]{:S(2)}, u32[]{:S(2)}) collective-permute-start(bf16[3072,768]{1,0:T(8,128)(2,1)} %convolution_convert_fusion.2.out_ref), channel_id=1, source_target_pairs={{16,0},{17,1},{18,2},{19,3},{20,4},{21,5},{22,6},{23,7},{24,8},{25... | collective-permute-start | bytes 14155784 | tf_op jit(solution)/shard_map/ppermute | solution.py:865
  372.6 39.7 %collective-permute-start.13 = (bf16[768,3072]{1,0:T(8,128)(2,1)}, bf16[768,3072]{1,0:T(8,128)(2,1)}, u32[]{:S(2)}, u32[]{:S(2)}) collective-permute-start(bf16[768,3072]{1,0:T(8,128)(2,1)} %convolution_convert_fusion.3.in_ref), channel_id=1, source_target_pairs={{0,16},{1,17},{2,18},{3,19},{4,20},{5,21},{6,22},{7,23},{8,24},{9,... | collective-permute-start | bytes 14155784 | tf_op jit(solution)/shard_map/ppermute | solution.py:865
  478.7 50.1 %all-to-all-start.6 = ((bf16[16,72,768]{2,1,0:T(8,128)(2,1)}), bf16[16,72,768]{2,1,0:T(8,128)(2,1)}, u32[]{:S(2)}, u32[]{:S(2)}) async-start(bf16[16,72,768]{2,1,0:T(8,128)(2,1)} %bitcast.90), calls=%async_computation.6 | async-start | bytes 3538944 | tf_op jit(solution)/shard_map/all_to_all | solution.py:729
  509.9 40.7 %collective-permute-start.26 = (bf16[768,3072]{1,0:T(8,128)(2,1)}, bf16[768,3072]{1,0:T(8,128)(2,1)}, u32[]{:S(2)}, u32[]{:S(2)}) collective-permute-start(bf16[768,3072]{1,0:T(8,128)(2,1)} %convolution_convert_fusion.1.in_ref), channel_id=1, source_target_pairs={{0,16},{1,17},{2,18},{3,19},{4,20},{5,21},{6,22},{7,23},{8,24},{9,... | collective-permute-start | bytes 14155784 | tf_op jit(solution)/shard_map/ppermute | solution.py:890
  542.4 41.6 %all-to-all-start.7 = ((bf16[16,72,768]{2,1,0:T(8,128)(2,1)}), bf16[16,72,768]{2,1,0:T(8,128)(2,1)}, u32[]{:S(2)}, u32[]{:S(2)}) async-start(bf16[16,72,768]{2,1,0:T(8,128)(2,1)} %bitcast.89), calls=%async_computation.7 | async-start | bytes 3538944 | tf_op jit(solution)/shard_map/all_to_all | solution.py:729
  562.7 35.9 %collective-permute-start.28 = (bf16[512,768]{1,0:T(8,128)(2,1)}, bf16[512,768]{1,0:T(8,128)(2,1)}, u32[]{:S(2)}, u32[]{:S(2)}) collective-permute-start(bf16[512,768]{1,0:T(8,128)(2,1)} %get-tuple-element.259), channel_id=1, source_target_pairs={{0,1},{1,0},{2,3},{3,2},{4,5},{5,4},{6,7},{7,6},{8,9},{9,8},{10,11... | collective-permute-start | bytes 2359304 | tf_op jit(solution)/shard_map/ppermute | solution.py:742
  610.5 67.6 %all-to-all-start.8 = ((bf16[16,208,128]{2,1,0:T(8,128)(2,1)}), bf16[16,208,128]{2,1,0:T(8,128)(2,1)}, u32[]{:S(2)}, u32[]{:S(2)}) async-start(bf16[16,208,128]{2,1,0:T(8,128)(2,1)} %bitcast.87), calls=%async_computation.8 | async-start | bytes 1703936 | tf_op jit(solution)/shard_map/all_to_all | solution.py:771
  670.2 55.0 %collective-permute-start.40 = (bf16[6,180,768]{2,1,0:T(8,128)(2,1)}, bf16[6,180,768]{2,1,0:T(8,128)(2,1)}, u32[]{:S(2)}, u32[]{:S(2)}) collective-permute-start(bf16[6,180,768]{2,1,0:T(8,128)(2,1)} %get-tuple-element.292), channel_id=1, source_target_pairs={{8,0},{24,8},{9,1},{25,9},{10,2},{26,10},{11,3},{27,11},{12,4},{28... | collective-permute-start | bytes 4976648 | tf_op jit(solution)/shard_map/ppermute | solution.py:786
  680.3 63.2 %all-to-all-start.9 = ((bf16[16,208,128]{2,1,0:T(8,128)(2,1)}), bf16[16,208,128]{2,1,0:T(8,128)(2,1)}, u32[]{:S(2)}, u32[]{:S(2)}) async-start(bf16[16,208,128]{2,1,0:T(8,128)(2,1)} %shard_map.318), calls=%async_computation.9 | async-start | bytes 1703936 | tf_op jit(solution)/shard_map/all_to_all | solution.py:773
  694.5 35.5 %collective-permute-start.47 = (bf16[2,256,768]{2,1,0:T(8,128)(2,1)}, bf16[2,256,768]{2,1,0:T(8,128)(2,1)S(1)}, u32[]{:S(2)}, u32[]{:S(2)}) collective-permute-start(bf16[2,256,768]{2,1,0:T(8,128)(2,1)} %get-tuple-element.311.refs_1_), channel_id=1, source_target_pairs={{0,4},{1,5},{2,6},{3,7},{4,0},{5,1},{6,2},{7,3},{8,12},{9,13},{10,... | collective-permute-start | bytes 2359304 | tf_op jit(solution)/shard_map/ppermute | solution.py:742
  695.3 34.7 %collective-permute-start.48 = (bf16[2,256,768]{2,1,0:T(8,128)(2,1)}, bf16[2,256,768]{2,1,0:T(8,128)(2,1)S(1)}, u32[]{:S(2)}, u32[]{:S(2)}) collective-permute-start(bf16[2,256,768]{2,1,0:T(8,128)(2,1)} %get-tuple-element.312.refs_2_), channel_id=1, source_target_pairs={{0,1},{1,0},{2,3},{3,2},{4,5},{5,4},{6,7},{7,6},{8,9},{9,8},{10,11... | collective-permute-start | bytes 2359304 | tf_op jit(solution)/shard_map/ppermute | solution.py:742
  736.6 38.6 %collective-permute-start.49 = (bf16[2,512,768]{2,1,0:T(8,128)(2,1)}, bf16[2,512,768]{2,1,0:T(8,128)(2,1)}, u32[]{:S(2)}, u32[]{:S(2)}) collective-permute-start(bf16[2,512,768]{2,1,0:T(8,128)(2,1)} %get-tuple-element.316.refs_0_), channel_id=1, source_target_pairs={{0,1},{1,0},{2,3},{3,2},{4,5},{5,4},{6,7},{7,6},{8,9},{9,8},{10,11... | collective-permute-start | bytes 4718600 | tf_op jit(solution)/shard_map/ppermute | solution.py:742
  738.7 36.4 %collective-permute-start.50 = (bf16[2,512,768]{2,1,0:T(8,128)(2,1)}, bf16[2,512,768]{2,1,0:T(8,128)(2,1)}, u32[]{:S(2)}, u32[]{:S(2)}) collective-permute-start(bf16[2,512,768]{2,1,0:T(8,128)(2,1)} %get-tuple-element.317.refs_1_), channel_id=1, source_target_pairs={{0,2},{1,3},{2,0},{3,1},{4,6},{5,7},{6,4},{7,5},{8,10},{9,11},{10,... | collective-permute-start | bytes 4718600 | tf_op jit(solution)/shard_map/ppermute | solution.py:742
  739.2 35.9 %collective-permute-start.51 = (bf16[2,512,768]{2,1,0:T(8,128)(2,1)}, bf16[2,512,768]{2,1,0:T(8,128)(2,1)}, u32[]{:S(2)}, u32[]{:S(2)}) collective-permute-start(bf16[2,512,768]{2,1,0:T(8,128)(2,1)} %get-tuple-element.318.refs_2_), channel_id=1, source_target_pairs={{0,4},{1,5},{2,6},{3,7},{4,0},{5,1},{6,2},{7,3},{8,12},{9,13},{10,... | collective-permute-start | bytes 4718600 | tf_op jit(solution)/shard_map/ppermute | solution.py:742
  (70 other events, 928.6 us)

commit v5 on v4

--- a/solution.py
+++ b/solution.py
@@ -62,16 +62,23 @@
     return lax.dot_general(left, right, (((1,), (1,)), ((), ())), preferred_element_type=F32)
 
 
+def both_parts(table_ref, value):
+    count = table_ref.shape[0] // 2
+    if count % 16:
+        return dot(table_ref[:count, :], value) + dot(table_ref[count:, :], value)
+    full = dot(table_ref[...], value)
+    return full[:count, :] + full[count:, :]
+
+
 def table_times_low(table_ref, low):
-    count = table_ref.shape[0] // 2
-    return dot(table_ref[:count, :], low) + dot(table_ref[count:, :], low)
+    return both_parts(table_ref, low)
 
 
 def table_times(table_ref, value):
     count = table_ref.shape[0] // 2
     high = value.astype(BF16)
     rest = (value - high.astype(F32)).astype(BF16)
-    return dot(table_ref[:count, :], high) + dot(table_ref[:count, :], rest) + dot(table_ref[count:, :], high)
+    return both_parts(table_ref, high) + dot(table_ref[:count, :], rest)
 
 
 def gelu_pair(value):
@@ -258,20 +265,16 @@
     step = pl.program_id(0)
     choose(place_ref, level, in_ref, in_other_ref, in_kept)
     choose(place_ref, level, out_ref, out_other_ref, out_kept)
-    hidden = dot(norm_ref[...], in_kept[...]) + vec_ref[pl.ds(IN_BIAS + step, 1), :]
-    active, slope = gelu_pair(hidden)
-    active = active.astype(BF16)
-    active_ref[...] = active
-    slope_ref[...] = slope.astype(BF16)
-    part = dot(active, out_kept[...])
-
-    @pl.when(step == 0)
-    def _():
-        total[...] = part + mixed_ref[...] + row_of(vec_ref, OUT_BIAS)
-
-    @pl.when(step > 0)
-    def _():
-        total[...] += part
+    tokens = norm_ref.shape[0]
+    middle = -(-tokens // 32) * 16
+    for span in (slice(0, middle), slice(middle, tokens)):
+        hidden = dot(norm_ref[span, :], in_kept[...]) + vec_ref[pl.ds(IN_BIAS + step, 1), :]
+        active, slope = gelu_pair(hidden)
+        active = active.astype(BF16)
+        active_ref[span, :] = active
+        slope_ref[span, :] = slope.astype(BF16)
+        before = jnp.where(step == 0, mixed_ref[span, :] + row_of(vec_ref, OUT_BIAS), total[span, :])
+        total[span, :] = before + dot(active, out_kept[...])
 
     @pl.when(step == pl.num_programs(0) - 1)
     def _():

time: 794 us -> 790 us (level)
  no operation moved by 1% of the time
where the time goes in v5:
time: 790 us; the launch traced here: 781 us
  Pallas kernels  317 us (40%)
  starting transfers between devices  159 us (20%)
  waiting for transfers between devices  116 us (15%)
  blocking collectives  86.2 us (11%)
  matrix products  45.1 us (6%)
  local copies, waits for them, and re-layouts  43.1 us (5%)
  other arithmetic  13.5 us (2%)
    pallas_call x27, Pallas kernels, call(): pl.pallas_call(functools.partial(body, **named), out_shape=[jax.ShapeDtyp...  174 us
    all_to_all x3, blocking collectives, exchange(): lax.all_to_all(pieces, ROWS_AXES, 0, 0, tiled=True).reshape(item.shape)  86.2 us
    pallas_call x2, Pallas kernels, dense(): pl.pallas_call(functools.partial(dense_kernel, level=level), grid_spec=pl...  56.8 us
    all_to_all x5, starting transfers between devices, exchange(): lax.all_to_all(pieces, ROWS_AXES, 0, 0, tiled=True).reshape(item.shape)  44.9 us
    pallas_call x2, Pallas kernels, dense_back(): pl.pallas_call(functools.partial(dense_back_kernel, level=level), grid_sp...  41.7 us
    ppermute x27, starting transfers between devices, swap(): lax.ppermute(item, 'lane', [(i, i ^ bit) for i in range(lax.axis_size('la...  33.3 us
    ppermute x2, waiting for transfers between devices, across_halves(): return lax.ppermute(item, 'half', [(0, 1), (1, 0)])  31 us
    ppermute x8, waiting for transfers between devices, send_out(): lax.ppermute(item, ('section', 'half'), [p for p in pairs(micro) if p[0]...  28.2 us
  transfers between devices with their start and end apart: 59, of which 16 were waited for; matrix products, arithmetic and copies ran while one was open for 10% of the time, Pallas kernels for 35%

profile of v5, /device:TPU:0, one launch (start us, length us, event | category | flops | bytes accessed | tf_op | source)
XLA Modules:
  0.0 781.1 jit_solution(16916930221667761937)
XLA Ops:
  24.4 12.5 %collective-permute-done = bf16[6,180,768]{2,1,0:T(8,128)(2,1)} collective-permute-done((bf16[6,180,768]{2,1,0:T(8,128)(2,1)}, bf16[6,180,768]{2,1,0:T(8,128)(2,1)}, u32[]{:S(2)}, u32[]{:S(2)}) %collective-permute-start) | collective-permute-done | bytes 1658912 | tf_op jit(solution)/shard_map/ppermute | solution.py:781
  46.0 24.5 %all-to-all-start = ((bf16[16,72,768]{2,1,0:T(8,128)(2,1)}), bf16[16,72,768]{2,1,0:T(8,128)(2,1)S(1)}, u32[]{:S(2)}, u32[]{:S(2)}) async-start(bf16[16,72,768]{2,1,0:T(8,128)(2,1)} %bitcast.91), calls=%async_computation | async-start | bytes 3538944 | tf_op jit(solution)/shard_map/all_to_all | solution.py:732
  79.0 14.3 %all-to-all-done = bf16[16,72,768]{2,1,0:T(8,128)(2,1)S(1)} async-done(((bf16[16,72,768]{2,1,0:T(8,128)(2,1)}), bf16[16,72,768]{2,1,0:T(8,128)(2,1)S(1)}, u32[]{:S(2)}, u32[]{:S(2)}) %all-to-all-start) | async-done | bytes 1769504 | tf_op jit(solution)/shard_map/all_to_all | solution.py:732
  94.4 14.8 %shard_map.292 = (bf16[1152,768]{1,0:T(8,128)(2,1)}, bf16[1152,768]{1,0:T(8,128)(2,1)}, bf16[1152,768]{1,0:T(8,128)(2,1)}, bf16[1152,768]{1,0:T(8,128)(2,1)}, bf16[1152,768]{1,0:T(8,128)(2,1)}) custom-call(bf16[1152,768]{1,0:T(8,128)(2,1)} %bitcast.88, bf16[384,96]{1,0:T(8,128)(2,1)} %constant.48.clone.table_ref, ...), custom_call_target="tpu_custom_call" | custom-call | flops 4294967296 | bytes 13083648 | tf_op jit(solution)/shard_map/pallas_call | solution.py:514
  109.3 29.6 %all_to_all.50 = bf16[16,72,768]{2,1,0:T(8,128)(2,1)} all-to-all(bf16[16,72,768]{2,1,0:T(8,128)(2,1)} %bitcast.98), channel_id=1, replica_groups=mesh['section'=2,'half'=2,'lane'=8] {'section','lane'}, dimensions={0} | all-to-all | bytes 3538944 | tf_op jit(solution)/shard_map/all_to_all | solution.py:732
  153.9 28.2 %shard_map.294 = (bf16[6,180,768]{2,1,0:T(8,128)(2,1)}, bf16[1080,3072]{1,0:T(8,128)(2,1)}, bf16[1080,3072]{1,0:T(8,128)(2,1)}) custom-call(s32[5]{0:T(128)} %concatenate.12.place_ref, bf16[1080,768]{1,0:T(8,128)(2,1)} %get-tuple-element.233.norm_ref, bf16[768,3072]{1,0:T(8,128)(2,1)} %bitcast.109, bf16[768,3072]{1,0:T(8,128)(2,1)} %collective-permute-done.5.in_other_ref, ...), custom_call_target="tpu_custom_call" | custom-call | flops 10192158720 | bytes 31457280 | tf_op jit(solution)/shard_map/pallas_call | solution.py:578
  187.5 28.4 %all_to_all.51 = bf16[16,72,768]{2,1,0:T(8,128)(2,1)} all-to-all(bf16[16,72,768]{2,1,0:T(8,128)(2,1)} %bitcast.100), channel_id=1, replica_groups=mesh['section'=2,'half'=2,'lane'=8] {'section','lane'}, dimensions={0} | all-to-all | bytes 3538944 | tf_op jit(solution)/shard_map/all_to_all | solution.py:732
  215.9 14.8 %shard_map.296 = (bf16[1152,768]{1,0:T(8,128)(2,1)}, bf16[1152,768]{1,0:T(8,128)(2,1)}, bf16[1152,768]{1,0:T(8,128)(2,1)}, bf16[1152,768]{1,0:T(8,128)(2,1)}, bf16[1152,768]{1,0:T(8,128)(2,1)}) custom-call(bf16[1152,768]{1,0:T(8,128)(2,1)} %bitcast.97, bf16[384,96]{1,0:T(8,128)(2,1)} %constant.48.clone.table_ref, ...), custom_call_target="tpu_custom_call" | custom-call | flops 4294967296 | bytes 13083648 | tf_op jit(solution)/shard_map/pallas_call | solution.py:514
  230.7 28.3 %all_to_all.52 = bf16[16,72,768]{2,1,0:T(8,128)(2,1)} all-to-all(bf16[16,72,768]{2,1,0:T(8,128)(2,1)} %bitcast.99), channel_id=1, replica_groups=mesh['section'=2,'half'=2,'lane'=8] {'section','lane'}, dimensions={0} | all-to-all | bytes 3538944 | tf_op jit(solution)/shard_map/all_to_all | solution.py:732
  271.7 28.6 %shard_map.298 = (bf16[6,180,768]{2,1,0:T(8,128)(2,1)}, bf16[1080,3072]{1,0:T(8,128)(2,1)}, bf16[1080,3072]{1,0:T(8,128)(2,1)}) custom-call(s32[5]{0:T(128)} %concatenate.12.place_ref, bf16[1080,768]{1,0:T(8,128)(2,1)} %get-tuple-element.193.norm_ref, bf16[768,3072]{1,0:T(8,128)(2,1)} %bitcast.110, bf16[768,3072]{1,0:T(8,128)(2,1)} %collective-permute-done.5.in_other_ref, ...), custom_call_target="tpu_custom_call" | custom-call | flops 10192158720 | bytes 31457280 | tf_op jit(solution)/shard_map/pallas_call | solution.py:578
  310.0 20.6 %shard_map.299 = (bf16[1080,3072]{1,0:T(8,128)(2,1)}, f32[4,768]{1,0:T(4,128)}, f32[1080,768]{1,0:T(8,128)}) custom-call(s32[5]{0:T(128)} %concatenate.12.place_ref, bf16[1080,768]{1,0:T(8,128)(2,1)} %reshape.111.grad_ref, bf16[3072,768]{1,0:T(8,128)(2,1)} %bitcast.116, bf16[3072,768]{1,0:T(8,128)(2,1)} %collective-permute-done.6.out_other_ref, ...), custom_call_target="tpu_custom_call" | custom-call | flops 10192158720 | bytes 31457280 | tf_op jit(solution)/shard_map/pallas_call | solution.py:602
  344.1 11.5 %convolution_convert_fusion.2.out_ref = bf16[3072,768]{1,0:T(8,128)(2,1)} fusion(bf16[1080,3072]{1,0:T(8,128)(2,1)} %get-tuple-element.195, bf16[1080,768]{1,0:T(8,128)(2,1)S(1)} %copy-done.3), kind=kOutput, calls=%fused_computation.2 | convolution fusion | flops 5098438656 | bytes 13012992 | tf_op jit(solution)/shard_map/dot_general | solution.py:866
  357.1 11.0 %convolution_convert_fusion.3.in_ref = bf16[768,3072]{1,0:T(8,128)(2,1)} fusion(bf16[1080,768]{1,0:T(8,128)(2,1)S(1)} %copy-done.34, bf16[1080,3072]{1,0:T(8,128)(2,1)} %get-tuple-element.194), kind=kOutput, calls=%fused_computation.3 | convolution fusion | flops 5098438656 | bytes 13012992 | tf_op jit(solution)/shard_map/dot_general | solution.py:865
  376.7 13.6 %shard_map.301 = (bf16[1152,768]{1,0:T(8,128)(2,1)}, bf16[1152,768]{1,0:T(8,128)(2,1)}, bf16[1152,768]{1,0:T(8,128)(2,1)}) custom-call(bf16[1152,768]{1,0:T(8,128)(2,1)} %bitcast.93, bf16[384,96]{1,0:T(8,128)(2,1)} %constant.48.clone.table_ref, bf16[768,768]{1,0:T(8,128)(2,1)} %get-tuple-element.181.one_ref, bf16[768,768]{1,0:T(8,128)(2,1)} %get-tuple-element.182.two_ref, ...), custom_call_target="tpu_custom_call" | custom-call | flops 4294967296 | bytes 13049856 | tf_op jit(solution)/shard_map/pallas_call | solution.py:514
  407.9 12.2 %shard_map.302 = (bf16[512,768]{1,0:T(8,128)(2,1)}, bf16[512,768]{1,0:T(8,128)(2,1)}, bf16[512,768]{1,0:T(8,128)(2,1)}, bf16[512,768]{1,0:T(8,128)(2,1)}, bf16[5...) custom-call(s32[5]{0:T(128)} %concatenate.12.place_ref, bf16[768,3072]{1,0:T(8,128)(2,1)} %convolution_convert_fusion.3.in_ref, ...), custom_call_target="tpu_custom_call" | custom-call | bytes 2359296 | tf_op jit(solution)/shard_map/pallas_call | solution.py:650
  433.5 21.1 %shard_map.305 = (bf16[1080,3072]{1,0:T(8,128)(2,1)}, f32[4,768]{1,0:T(4,128)}, f32[1080,768]{1,0:T(8,128)}) custom-call(s32[5]{0:T(128)} %concatenate.12.place_ref, bf16[1080,768]{1,0:T(8,128)(2,1)} %get-tuple-element.216.grad_ref, bf16[3072,768]{1,0:T(8,128)(2,1)} %bitcast.117, bf16[3072,768]{1,0:T(8,128)(2,1)} %collective-permute-done.6.out_other_ref, ...), custom_call_target="tpu_custom_call" | custom-call | flops 10192158720 | bytes 31457280 | tf_op jit(solution)/shard_map/pallas_call | solution.py:602
  482.8 11.4 %convolution_convert_fusion.out_ref = bf16[3072,768]{1,0:T(8,128)(2,1)} fusion(bf16[1080,3072]{1,0:T(8,128)(2,1)} %get-tuple-element.235, bf16[1080,768]{1,0:T(8,128)(2,1)S(1)} %copy-done.8), kind=kOutput, calls=%fused_computation | convolution fusion | flops 5098438656 | bytes 13012992 | tf_op jit(solution)/shard_map/dot_general | solution.py:885
  494.2 11.1 %convolution_convert_fusion.1.in_ref = bf16[768,3072]{1,0:T(8,128)(2,1)} fusion(bf16[1080,768]{1,0:T(8,128)(2,1)S(1)} %copy-done.33, bf16[1080,3072]{1,0:T(8,128)(2,1)} %get-tuple-element.234), kind=kOutput, calls=%fused_computation.1 | convolution fusion | flops 5098438656 | bytes 13012992 | tf_op jit(solution)/shard_map/dot_general | solution.py:886
  505.3 14.9 %collective-permute-start.26 = (bf16[768,3072]{1,0:T(8,128)(2,1)}, bf16[768,3072]{1,0:T(8,128)(2,1)}, u32[]{:S(2)}, u32[]{:S(2)}) collective-permute-start(bf16[768,3072]{1,0:T(8,128)(2,1)} %convolution_convert_fusion.1.in_ref), channel_id=1, source_target_pairs={{0,16},{1,17},{2,18},{3,19},{4,20},{5,21},{6,22},{7,23},{8,24},{9,... | collective-permute-start | bytes 14155784 | tf_op jit(solution)/shard_map/ppermute | solution.py:893
  524.8 13.6 %shard_map.309 = (bf16[1152,768]{1,0:T(8,128)(2,1)}, bf16[1152,768]{1,0:T(8,128)(2,1)}, bf16[1152,768]{1,0:T(8,128)(2,1)}) custom-call(bf16[1152,768]{1,0:T(8,128)(2,1)} %bitcast.33.got_ref, bf16[384,96]{1,0:T(8,128)(2,1)} %constant.48.clone.table_ref, bf16[768,768]{1,0:T(8,128)(2,1)} %get-tuple-element.171.one_ref, ...), custom_call_target="tpu_custom_call" | custom-call | flops 4294967296 | bytes 13049856 | tf_op jit(solution)/shard_map/pallas_call | solution.py:514
  546.4 12.2 %shard_map.311 = (bf16[512,768]{1,0:T(8,128)(2,1)}, bf16[512,768]{1,0:T(8,128)(2,1)}, bf16[512,768]{1,0:T(8,128)(2,1)}, bf16[512,768]{1,0:T(8,128)(2,1)}, bf16[5...) custom-call(s32[5]{0:T(128)} %concatenate.12.place_ref, bf16[768,3072]{1,0:T(8,128)(2,1)} %convolution_convert_fusion.1.in_ref, ...), custom_call_target="tpu_custom_call" | custom-call | bytes 2359296 | tf_op jit(solution)/shard_map/pallas_call | solution.py:650
  635.8 24.8 %collective-permute-done.38.one_got_ref = bf16[384,768]{1,0:T(8,128)(2,1)S(1)} collective-permute-done((bf16[384,768]{1,0:T(8,128)(2,1)}, bf16[384,768]{1,0:T(8,128)(2,1)S(1)}, u32[]{:S(2)}, u32[]{:S(2)}) %collective-permute-start.38) | collective-permute-done | bytes 589856 | tf_op jit(solution)/shard_map/ppermute | solution.py:758
  692.9 28.2 %collective-permute-done.40 = bf16[6,180,768]{2,1,0:T(8,128)(2,1)} collective-permute-done((bf16[6,180,768]{2,1,0:T(8,128)(2,1)}, bf16[6,180,768]{2,1,0:T(8,128)(2,1)}, u32[]{:S(2)}, u32[]{:S(2)}) %collective-permute-start.40) | collective-permute-done | bytes 1658912 | tf_op jit(solution)/shard_map/ppermute | solution.py:789
  770.9 9.7 %shard_map.324 = (f32[768,3072]{1,0:T(8,128)}, f32[3072,768]{1,0:T(8,128)}) custom-call(s32[5]{0:T(128)} %concatenate.12.place_ref, bf16[2,512,768]{2,1,0:T(8,128)(2,1)} %collective-permute-done.49.refs_0_, bf16[2,512,768]{2,1,0:T(8,128)(2,1)} %collective-permute-done.50.refs_1_, ...), custom_call_target="tpu_custom_call", output_to_operand_aliasing={{0}: (4, {}), {1}: (5, {})} | custom-call | bytes 14155776 | tf_op jit(solution)/shard_map/pallas_call | solution.py:696
  (244 shorter events, 339.4 us)
Async XLA Ops:
  46.0 47.3 %all-to-all-start = ((bf16[16,72,768]{2,1,0:T(8,128)(2,1)}), bf16[16,72,768]{2,1,0:T(8,128)(2,1)S(1)}, u32[]{:S(2)}, u32[]{:S(2)}) async-start(bf16[16,72,768]{2,1,0:T(8,128)(2,1)} %bitcast.91), calls=%async_computation | async-start | bytes 3538944 | tf_op jit(solution)/shard_map/all_to_all | solution.py:732
  93.2 60.7 %collective-permute-start.5 = (bf16[768,3072]{1,0:T(8,128)(2,1)}, bf16[768,3072]{1,0:T(8,128)(2,1)}, u32[]{:S(2)}, u32[]{:S(2)}) collective-permute-start(bf16[768,3072]{1,0:T(8,128)(2,1)} %bitcast.108), channel_id=1, source_target_pairs={{0,16},{16,0},{1,17},{17,1},{2,18},{18,2},{3,19},{19,3},{4,20},{20... | collective-permute-start | bytes 14155784 | tf_op jit(solution)/shard_map/ppermute | solution.py:796
  93.4 60.5 %collective-permute-start.6 = (bf16[3072,768]{1,0:T(8,128)(2,1)}, bf16[3072,768]{1,0:T(8,128)(2,1)}, u32[]{:S(2)}, u32[]{:S(2)}) collective-permute-start(bf16[3072,768]{1,0:T(8,128)(2,1)} %bitcast.113), channel_id=1, source_target_pairs={{0,16},{16,0},{1,17},{17,1},{2,18},{18,2},{3,19},{19,3},{4,20},{20... | collective-permute-start | bytes 14155784 | tf_op jit(solution)/shard_map/ppermute | solution.py:796
  140.7 41.5 %collective-permute-start.7 = (bf16[6,180,768]{2,1,0:T(8,128)(2,1)}, bf16[6,180,768]{2,1,0:T(8,128)(2,1)S(1)}, u32[]{:S(2)}, u32[]{:S(2)}) collective-permute-start(bf16[6,180,768]{2,1,0:T(8,128)(2,1)} %get-tuple-element.343), channel_id=1, source_target_pairs={{0,8},{1,9},{2,10},{3,11},{4,12},{5,13},{6,14},{7,15}} | collective-permute-start | bytes 4976648 | tf_op jit(solution)/shard_map/ppermute | solution.py:781
  144.5 37.6 %collective-permute-start.8 = (bf16[6,180,768]{2,1,0:T(8,128)(2,1)S(1)}, bf16[6,180,768]{2,1,0:T(8,128)(2,1)}, u32[]{:S(2)}, u32[]{:S(2)}) collective-permute-start(bf16[6,180,768]{2,1,0:T(8,128)(2,1)S(1)} %get-tuple-element.342), channel_id=1, source_target_pairs={{24,16},{25,17},{26,18},{27,19},{28,20},{29,21},{30,22},{31,23}} | collective-permute-start | bytes 4976648 | tf_op jit(solution)/shard_map/ppermute | solution.py:782
  259.0 51.0 %collective-permute-start.11 = (bf16[6,180,768]{2,1,0:T(8,128)(2,1)S(1)}, bf16[6,180,768]{2,1,0:T(8,128)(2,1)}, u32[]{:S(2)}, u32[]{:S(2)}) collective-permute-start(bf16[6,180,768]{2,1,0:T(8,128)(2,1)S(1)} %copy-done.1), channel_id=1, source_target_pairs={{8,0},{24,8},{9,1},{25,9},{10,2},{26,10},{11,3},{27,11},{12,4},{28... | collective-permute-start | bytes 4976648 | tf_op jit(solution)/shard_map/ppermute | solution.py:789
  260.3 49.7 %collective-permute-start.9 = (bf16[6,180,768]{2,1,0:T(8,128)(2,1)S(1)}, bf16[6,180,768]{2,1,0:T(8,128)(2,1)}, u32[]{:S(2)}, u32[]{:S(2)}) collective-permute-start(bf16[6,180,768]{2,1,0:T(8,128)(2,1)S(1)} %copy-done.1), channel_id=1, source_target_pairs={{16,8},{17,9},{18,10},{19,11},{20,12},{21,13},{22,14},{23,15}} | collective-permute-start | bytes 4976648 | tf_op jit(solution)/shard_map/ppermute | solution.py:789
  300.3 75.2 %collective-permute-start.10 = (bf16[6,180,768]{2,1,0:T(8,128)(2,1)}, bf16[6,180,768]{2,1,0:T(8,128)(2,1)}, u32[]{:S(2)}, u32[]{:S(2)}) collective-permute-start(bf16[6,180,768]{2,1,0:T(8,128)(2,1)} %get-tuple-element.187), channel_id=1, source_target_pairs={{0,16},{16,24},{1,17},{17,25},{2,18},{18,26},{3,19},{19,27},{4,20}... | collective-permute-start | bytes 4976648 | tf_op jit(solution)/shard_map/ppermute | solution.py:789
  307.9 67.6 %collective-permute-start.12 = (bf16[6,180,768]{2,1,0:T(8,128)(2,1)}, bf16[6,180,768]{2,1,0:T(8,128)(2,1)}, u32[]{:S(2)}, u32[]{:S(2)}) collective-permute-start(bf16[6,180,768]{2,1,0:T(8,128)(2,1)} %get-tuple-element.187), channel_id=1, source_target_pairs={{8,16},{9,17},{10,18},{11,19},{12,20},{13,21},{14,22},{15,23}} | collective-permute-start | bytes 4976648 | tf_op jit(solution)/shard_map/ppermute | solution.py:789
  340.2 35.3 %all-to-all-start.4 = ((bf16[16,72,768]{2,1,0:T(8,128)(2,1)}), bf16[16,72,768]{2,1,0:T(8,128)(2,1)S(1)}, u32[]{:S(2)}, u32[]{:S(2)}) async-start(bf16[16,72,768]{2,1,0:T(8,128)(2,1)} %bitcast.94), calls=%async_computation.4 | async-start | bytes 3538944 | tf_op jit(solution)/shard_map/all_to_all | solution.py:732
  355.6 52.3 %collective-permute-start.14 = (bf16[3072,768]{1,0:T(8,128)(2,1)}, bf16[3072,768]{1,0:T(8,128)(2,1)}, u32[]{:S(2)}, u32[]{:S(2)}) collective-permute-start(bf16[3072,768]{1,0:T(8,128)(2,1)} %convolution_convert_fusion.2.out_ref), channel_id=1, source_target_pairs={{16,0},{17,1},{18,2},{19,3},{20,4},{21,5},{22,6},{23,7},{24,8},{25... | collective-permute-start | bytes 14155784 | tf_op jit(solution)/shard_map/ppermute | solution.py:868
  368.1 39.8 %collective-permute-start.13 = (bf16[768,3072]{1,0:T(8,128)(2,1)}, bf16[768,3072]{1,0:T(8,128)(2,1)}, u32[]{:S(2)}, u32[]{:S(2)}) collective-permute-start(bf16[768,3072]{1,0:T(8,128)(2,1)} %convolution_convert_fusion.3.in_ref), channel_id=1, source_target_pairs={{0,16},{1,17},{2,18},{3,19},{4,20},{5,21},{6,22},{7,23},{8,24},{9,... | collective-permute-start | bytes 14155784 | tf_op jit(solution)/shard_map/ppermute | solution.py:868
  474.4 50.4 %all-to-all-start.6 = ((bf16[16,72,768]{2,1,0:T(8,128)(2,1)}), bf16[16,72,768]{2,1,0:T(8,128)(2,1)}, u32[]{:S(2)}, u32[]{:S(2)}) async-start(bf16[16,72,768]{2,1,0:T(8,128)(2,1)} %bitcast.90), calls=%async_computation.6 | async-start | bytes 3538944 | tf_op jit(solution)/shard_map/all_to_all | solution.py:732
  505.3 41.0 %collective-permute-start.26 = (bf16[768,3072]{1,0:T(8,128)(2,1)}, bf16[768,3072]{1,0:T(8,128)(2,1)}, u32[]{:S(2)}, u32[]{:S(2)}) collective-permute-start(bf16[768,3072]{1,0:T(8,128)(2,1)} %convolution_convert_fusion.1.in_ref), channel_id=1, source_target_pairs={{0,16},{1,17},{2,18},{3,19},{4,20},{5,21},{6,22},{7,23},{8,24},{9,... | collective-permute-start | bytes 14155784 | tf_op jit(solution)/shard_map/ppermute | solution.py:893
  538.4 41.4 %all-to-all-start.7 = ((bf16[16,72,768]{2,1,0:T(8,128)(2,1)}), bf16[16,72,768]{2,1,0:T(8,128)(2,1)}, u32[]{:S(2)}, u32[]{:S(2)}) async-start(bf16[16,72,768]{2,1,0:T(8,128)(2,1)} %bitcast.89), calls=%async_computation.7 | async-start | bytes 3538944 | tf_op jit(solution)/shard_map/all_to_all | solution.py:732
  558.6 35.9 %collective-permute-start.28 = (bf16[512,768]{1,0:T(8,128)(2,1)}, bf16[512,768]{1,0:T(8,128)(2,1)}, u32[]{:S(2)}, u32[]{:S(2)}) collective-permute-start(bf16[512,768]{1,0:T(8,128)(2,1)} %get-tuple-element.259), channel_id=1, source_target_pairs={{0,1},{1,0},{2,3},{3,2},{4,5},{5,4},{6,7},{7,6},{8,9},{9,8},{10,11... | collective-permute-start | bytes 2359304 | tf_op jit(solution)/shard_map/ppermute | solution.py:745
  606.4 67.6 %all-to-all-start.8 = ((bf16[16,208,128]{2,1,0:T(8,128)(2,1)}), bf16[16,208,128]{2,1,0:T(8,128)(2,1)}, u32[]{:S(2)}, u32[]{:S(2)}) async-start(bf16[16,208,128]{2,1,0:T(8,128)(2,1)} %bitcast.87), calls=%async_computation.8 | async-start | bytes 1703936 | tf_op jit(solution)/shard_map/all_to_all | solution.py:774
  666.2 54.9 %collective-permute-start.40 = (bf16[6,180,768]{2,1,0:T(8,128)(2,1)}, bf16[6,180,768]{2,1,0:T(8,128)(2,1)}, u32[]{:S(2)}, u32[]{:S(2)}) collective-permute-start(bf16[6,180,768]{2,1,0:T(8,128)(2,1)} %get-tuple-element.292), channel_id=1, source_target_pairs={{8,0},{24,8},{9,1},{25,9},{10,2},{26,10},{11,3},{27,11},{12,4},{28... | collective-permute-start | bytes 4976648 | tf_op jit(solution)/shard_map/ppermute | solution.py:789
  676.1 63.2 %all-to-all-start.9 = ((bf16[16,208,128]{2,1,0:T(8,128)(2,1)}), bf16[16,208,128]{2,1,0:T(8,128)(2,1)}, u32[]{:S(2)}, u32[]{:S(2)}) async-start(bf16[16,208,128]{2,1,0:T(8,128)(2,1)} %shard_map.318), calls=%async_computation.9 | async-start | bytes 1703936 | tf_op jit(solution)/shard_map/all_to_all | solution.py:776
  690.3 35.5 %collective-permute-start.47 = (bf16[2,256,768]{2,1,0:T(8,128)(2,1)}, bf16[2,256,768]{2,1,0:T(8,128)(2,1)S(1)}, u32[]{:S(2)}, u32[]{:S(2)}) collective-permute-start(bf16[2,256,768]{2,1,0:T(8,128)(2,1)} %get-tuple-element.311.refs_1_), channel_id=1, source_target_pairs={{0,4},{1,5},{2,6},{3,7},{4,0},{5,1},{6,2},{7,3},{8,12},{9,13},{10,... | collective-permute-start | bytes 2359304 | tf_op jit(solution)/shard_map/ppermute | solution.py:745
  691.1 34.8 %collective-permute-start.48 = (bf16[2,256,768]{2,1,0:T(8,128)(2,1)}, bf16[2,256,768]{2,1,0:T(8,128)(2,1)S(1)}, u32[]{:S(2)}, u32[]{:S(2)}) collective-permute-start(bf16[2,256,768]{2,1,0:T(8,128)(2,1)} %get-tuple-element.312.refs_2_), channel_id=1, source_target_pairs={{0,1},{1,0},{2,3},{3,2},{4,5},{5,4},{6,7},{7,6},{8,9},{9,8},{10,11... | collective-permute-start | bytes 2359304 | tf_op jit(solution)/shard_map/ppermute | solution.py:745
  732.4 38.5 %collective-permute-start.49 = (bf16[2,512,768]{2,1,0:T(8,128)(2,1)}, bf16[2,512,768]{2,1,0:T(8,128)(2,1)}, u32[]{:S(2)}, u32[]{:S(2)}) collective-permute-start(bf16[2,512,768]{2,1,0:T(8,128)(2,1)} %get-tuple-element.316.refs_0_), channel_id=1, source_target_pairs={{0,1},{1,0},{2,3},{3,2},{4,5},{5,4},{6,7},{7,6},{8,9},{9,8},{10,11... | collective-permute-start | bytes 4718600 | tf_op jit(solution)/shard_map/ppermute | solution.py:745
  734.5 36.4 %collective-permute-start.50 = (bf16[2,512,768]{2,1,0:T(8,128)(2,1)}, bf16[2,512,768]{2,1,0:T(8,128)(2,1)}, u32[]{:S(2)}, u32[]{:S(2)}) collective-permute-start(bf16[2,512,768]{2,1,0:T(8,128)(2,1)} %get-tuple-element.317.refs_1_), channel_id=1, source_target_pairs={{0,2},{1,3},{2,0},{3,1},{4,6},{5,7},{6,4},{7,5},{8,10},{9,11},{10,... | collective-permute-start | bytes 4718600 | tf_op jit(solution)/shard_map/ppermute | solution.py:745
  735.0 35.9 %collective-permute-start.51 = (bf16[2,512,768]{2,1,0:T(8,128)(2,1)}, bf16[2,512,768]{2,1,0:T(8,128)(2,1)}, u32[]{:S(2)}, u32[]{:S(2)}) collective-permute-start(bf16[2,512,768]{2,1,0:T(8,128)(2,1)} %get-tuple-element.318.refs_2_), channel_id=1, source_target_pairs={{0,4},{1,5},{2,6},{3,7},{4,0},{5,1},{6,2},{7,3},{8,12},{9,13},{10,... | collective-permute-start | bytes 4718600 | tf_op jit(solution)/shard_map/ppermute | solution.py:745
  (70 other events, 928.1 us)

commit v6 on v5

--- a/solution.py
+++ b/solution.py
@@ -288,19 +288,17 @@
     step = pl.program_id(0)
     choose(place_ref, level, in_ref, in_other_ref, in_kept)
     choose(place_ref, level, out_ref, out_other_ref, out_kept)
-    grad_active = dot_transposed(grad_ref[...], out_kept[...])
-    hidden = (grad_active * slope_ref[...].astype(F32)).astype(BF16)
-    hidden_ref[...] = hidden
-    bias_ref[pl.ds(step, 1), :] = jnp.sum(hidden.astype(F32), axis=0, keepdims=True)
-    part = dot_transposed(hidden, in_kept[...])
-
-    @pl.when(step == 0)
-    def _():
-        norm_ref[...] = part
-
-    @pl.when(step > 0)
-    def _():
-        norm_ref[...] += part
+    tokens = grad_ref.shape[0]
+    middle = -(-tokens // 32) * 16
+    bias = 0.0
+    for span in (slice(0, middle), slice(middle, tokens)):
+        grad_active = dot_transposed(grad_ref[span, :], out_kept[...])
+        hidden = (grad_active * slope_ref[span, :].astype(F32)).astype(BF16)
+        hidden_ref[span, :] = hidden
+        bias += jnp.sum(hidden.astype(F32), axis=0, keepdims=True)
+        before = jnp.where(step == 0, 0.0, norm_ref[span, :])
+        norm_ref[span, :] = before + dot_transposed(hidden, in_kept[...])
+    bias_ref[pl.ds(step, 1), :] = bias
 
 
 def middle_back_kernel(norm_ref, mixed_ref, grad_ref, vec_ref, table_ref, sent_ref, grad_mixed_ref, small_ref, grad32, sent32, *, rows, lanes, per):

time: 790 us -> 786 us (level)
  no operation moved by 1% of the time
where the time goes in v6:
time: 786 us; the launch traced here: 777 us
  Pallas kernels  312 us (40%)
  starting transfers between devices  158 us (20%)
  waiting for transfers between devices  117 us (15%)
  blocking collectives  86.2 us (11%)
  matrix products  45.1 us (6%)
  local copies, waits for them, and re-layouts  43.1 us (5%)
  other arithmetic  13.5 us (2%)
    pallas_call x27, Pallas kernels, call(): pl.pallas_call(functools.partial(body, **named), out_shape=[jax.ShapeDtyp...  174 us
    all_to_all x3, blocking collectives, exchange(): lax.all_to_all(pieces, ROWS_AXES, 0, 0, tiled=True).reshape(item.shape)  86.2 us
    pallas_call x2, Pallas kernels, dense(): pl.pallas_call(functools.partial(dense_kernel, level=level), grid_spec=pl...  56.8 us
    all_to_all x5, starting transfers between devices, exchange(): lax.all_to_all(pieces, ROWS_AXES, 0, 0, tiled=True).reshape(item.shape)  44.3 us
    pallas_call x2, Pallas kernels, dense_back(): pl.pallas_call(functools.partial(dense_back_kernel, level=level), grid_sp...  37.9 us
    ppermute x27, starting transfers between devices, swap(): lax.ppermute(item, 'lane', [(i, i ^ bit) for i in range(lax.axis_size('la...  32.9 us
    ppermute x2, waiting for transfers between devices, across_halves(): return lax.ppermute(item, 'half', [(0, 1), (1, 0)])  31 us
    ppermute x8, waiting for transfers between devices, send_out(): lax.ppermute(item, ('section', 'half'), [p for p in pairs(micro) if p[0]...  28.2 us
  transfers between devices with their start and end apart: 59, of which 16 were waited for; matrix products, arithmetic and copies ran while one was open for 10% of the time, Pallas kernels for 35%

profile of v6, /device:TPU:0, one launch (start us, length us, event | category | flops | bytes accessed | tf_op | source)
XLA Modules:
  0.0 777.1 jit_solution(3949842183737583063)
XLA Ops:
  24.4 12.5 %collective-permute-done = bf16[6,180,768]{2,1,0:T(8,128)(2,1)} collective-permute-done((bf16[6,180,768]{2,1,0:T(8,128)(2,1)}, bf16[6,180,768]{2,1,0:T(8,128)(2,1)}, u32[]{:S(2)}, u32[]{:S(2)}) %collective-permute-start) | collective-permute-done | bytes 1658912 | tf_op jit(solution)/shard_map/ppermute | solution.py:779
  46.0 24.5 %all-to-all-start = ((bf16[16,72,768]{2,1,0:T(8,128)(2,1)}), bf16[16,72,768]{2,1,0:T(8,128)(2,1)S(1)}, u32[]{:S(2)}, u32[]{:S(2)}) async-start(bf16[16,72,768]{2,1,0:T(8,128)(2,1)} %bitcast.91), calls=%async_computation | async-start | bytes 3538944 | tf_op jit(solution)/shard_map/all_to_all | solution.py:730
  78.8 14.5 %all-to-all-done = bf16[16,72,768]{2,1,0:T(8,128)(2,1)S(1)} async-done(((bf16[16,72,768]{2,1,0:T(8,128)(2,1)}), bf16[16,72,768]{2,1,0:T(8,128)(2,1)S(1)}, u32[]{:S(2)}, u32[]{:S(2)}) %all-to-all-start) | async-done | bytes 1769504 | tf_op jit(solution)/shard_map/all_to_all | solution.py:730
  94.4 14.8 %shard_map.292 = (bf16[1152,768]{1,0:T(8,128)(2,1)}, bf16[1152,768]{1,0:T(8,128)(2,1)}, bf16[1152,768]{1,0:T(8,128)(2,1)}, bf16[1152,768]{1,0:T(8,128)(2,1)}, bf16[1152,768]{1,0:T(8,128)(2,1)}) custom-call(bf16[1152,768]{1,0:T(8,128)(2,1)} %bitcast.88, bf16[384,96]{1,0:T(8,128)(2,1)} %constant.48.clone.table_ref, ...), custom_call_target="tpu_custom_call" | custom-call | flops 4294967296 | bytes 13083648 | tf_op jit(solution)/shard_map/pallas_call | solution.py:512
  109.3 29.6 %all_to_all.50 = bf16[16,72,768]{2,1,0:T(8,128)(2,1)} all-to-all(bf16[16,72,768]{2,1,0:T(8,128)(2,1)} %bitcast.98), channel_id=1, replica_groups=mesh['section'=2,'half'=2,'lane'=8] {'section','lane'}, dimensions={0} | all-to-all | bytes 3538944 | tf_op jit(solution)/shard_map/all_to_all | solution.py:730
  154.3 28.2 %shard_map.294 = (bf16[6,180,768]{2,1,0:T(8,128)(2,1)}, bf16[1080,3072]{1,0:T(8,128)(2,1)}, bf16[1080,3072]{1,0:T(8,128)(2,1)}) custom-call(s32[5]{0:T(128)} %concatenate.12.place_ref, bf16[1080,768]{1,0:T(8,128)(2,1)} %get-tuple-element.233.norm_ref, bf16[768,3072]{1,0:T(8,128)(2,1)} %bitcast.109, bf16[768,3072]{1,0:T(8,128)(2,1)} %collective-permute-done.5.in_other_ref, ...), custom_call_target="tpu_custom_call" | custom-call | flops 10192158720 | bytes 31457280 | tf_op jit(solution)/shard_map/pallas_call | solution.py:576
  187.8 28.3 %all_to_all.51 = bf16[16,72,768]{2,1,0:T(8,128)(2,1)} all-to-all(bf16[16,72,768]{2,1,0:T(8,128)(2,1)} %bitcast.100), channel_id=1, replica_groups=mesh['section'=2,'half'=2,'lane'=8] {'section','lane'}, dimensions={0} | all-to-all | bytes 3538944 | tf_op jit(solution)/shard_map/all_to_all | solution.py:730
  216.2 14.8 %shard_map.296 = (bf16[1152,768]{1,0:T(8,128)(2,1)}, bf16[1152,768]{1,0:T(8,128)(2,1)}, bf16[1152,768]{1,0:T(8,128)(2,1)}, bf16[1152,768]{1,0:T(8,128)(2,1)}, bf16[1152,768]{1,0:T(8,128)(2,1)}) custom-call(bf16[1152,768]{1,0:T(8,128)(2,1)} %bitcast.97, bf16[384,96]{1,0:T(8,128)(2,1)} %constant.48.clone.table_ref, ...), custom_call_target="tpu_custom_call" | custom-call | flops 4294967296 | bytes 13083648 | tf_op jit(solution)/shard_map/pallas_call | solution.py:512
  231.0 28.3 %all_to_all.52 = bf16[16,72,768]{2,1,0:T(8,128)(2,1)} all-to-all(bf16[16,72,768]{2,1,0:T(8,128)(2,1)} %bitcast.99), channel_id=1, replica_groups=mesh['section'=2,'half'=2,'lane'=8] {'section','lane'}, dimensions={0} | all-to-all | bytes 3538944 | tf_op jit(solution)/shard_map/all_to_all | solution.py:730
  271.8 28.6 %shard_map.298 = (bf16[6,180,768]{2,1,0:T(8,128)(2,1)}, bf16[1080,3072]{1,0:T(8,128)(2,1)}, bf16[1080,3072]{1,0:T(8,128)(2,1)}) custom-call(s32[5]{0:T(128)} %concatenate.12.place_ref, bf16[1080,768]{1,0:T(8,128)(2,1)} %get-tuple-element.193.norm_ref, bf16[768,3072]{1,0:T(8,128)(2,1)} %bitcast.110, bf16[768,3072]{1,0:T(8,128)(2,1)} %collective-permute-done.5.in_other_ref, ...), custom_call_target="tpu_custom_call" | custom-call | flops 10192158720 | bytes 31457280 | tf_op jit(solution)/shard_map/pallas_call | solution.py:576
  310.4 18.7 %shard_map.299 = (bf16[1080,3072]{1,0:T(8,128)(2,1)}, f32[4,768]{1,0:T(4,128)}, f32[1080,768]{1,0:T(8,128)}) custom-call(s32[5]{0:T(128)} %concatenate.12.place_ref, bf16[1080,768]{1,0:T(8,128)(2,1)} %reshape.111.grad_ref, bf16[3072,768]{1,0:T(8,128)(2,1)} %bitcast.116, bf16[3072,768]{1,0:T(8,128)(2,1)} %collective-permute-done.6.out_other_ref, ...), custom_call_target="tpu_custom_call" | custom-call | flops 10192158720 | bytes 31457280 | tf_op jit(solution)/shard_map/pallas_call | solution.py:600
  342.6 11.5 %convolution_convert_fusion.2.out_ref = bf16[3072,768]{1,0:T(8,128)(2,1)} fusion(bf16[1080,3072]{1,0:T(8,128)(2,1)} %get-tuple-element.195, bf16[1080,768]{1,0:T(8,128)(2,1)S(1)} %copy-done.3), kind=kOutput, calls=%fused_computation.2 | convolution fusion | flops 5098438656 | bytes 13012992 | tf_op jit(solution)/shard_map/dot_general | solution.py:864
  355.4 11.0 %convolution_convert_fusion.3.in_ref = bf16[768,3072]{1,0:T(8,128)(2,1)} fusion(bf16[1080,768]{1,0:T(8,128)(2,1)S(1)} %copy-done.34, bf16[1080,3072]{1,0:T(8,128)(2,1)} %get-tuple-element.194), kind=kOutput, calls=%fused_computation.3 | convolution fusion | flops 5098438656 | bytes 13012992 | tf_op jit(solution)/shard_map/dot_general | solution.py:863
  375.3 13.7 %shard_map.301 = (bf16[1152,768]{1,0:T(8,128)(2,1)}, bf16[1152,768]{1,0:T(8,128)(2,1)}, bf16[1152,768]{1,0:T(8,128)(2,1)}) custom-call(bf16[1152,768]{1,0:T(8,128)(2,1)} %bitcast.93, bf16[384,96]{1,0:T(8,128)(2,1)} %constant.48.clone.table_ref, bf16[768,768]{1,0:T(8,128)(2,1)} %get-tuple-element.181.one_ref, bf16[768,768]{1,0:T(8,128)(2,1)} %get-tuple-element.182.two_ref, ...), custom_call_target="tpu_custom_call" | custom-call | flops 4294967296 | bytes 13049856 | tf_op jit(solution)/shard_map/pallas_call | solution.py:512
  406.2 12.2 %shard_map.302 = (bf16[512,768]{1,0:T(8,128)(2,1)}, bf16[512,768]{1,0:T(8,128)(2,1)}, bf16[512,768]{1,0:T(8,128)(2,1)}, bf16[512,768]{1,0:T(8,128)(2,1)}, bf16[5...) custom-call(s32[5]{0:T(128)} %concatenate.12.place_ref, bf16[768,3072]{1,0:T(8,128)(2,1)} %convolution_convert_fusion.3.in_ref, ...), custom_call_target="tpu_custom_call" | custom-call | bytes 2359296 | tf_op jit(solution)/shard_map/pallas_call | solution.py:648
  431.6 19.2 %shard_map.305 = (bf16[1080,3072]{1,0:T(8,128)(2,1)}, f32[4,768]{1,0:T(4,128)}, f32[1080,768]{1,0:T(8,128)}) custom-call(s32[5]{0:T(128)} %concatenate.12.place_ref, bf16[1080,768]{1,0:T(8,128)(2,1)} %get-tuple-element.216.grad_ref, bf16[3072,768]{1,0:T(8,128)(2,1)} %bitcast.117, bf16[3072,768]{1,0:T(8,128)(2,1)} %collective-permute-done.6.out_other_ref, ...), custom_call_target="tpu_custom_call" | custom-call | flops 10192158720 | bytes 31457280 | tf_op jit(solution)/shard_map/pallas_call | solution.py:600
  478.8 11.5 %convolution_convert_fusion.out_ref = bf16[3072,768]{1,0:T(8,128)(2,1)} fusion(bf16[1080,3072]{1,0:T(8,128)(2,1)} %get-tuple-element.235, bf16[1080,768]{1,0:T(8,128)(2,1)S(1)} %copy-done.8), kind=kOutput, calls=%fused_computation | convolution fusion | flops 5098438656 | bytes 13012992 | tf_op jit(solution)/shard_map/dot_general | solution.py:883
  490.2 11.1 %convolution_convert_fusion.1.in_ref = bf16[768,3072]{1,0:T(8,128)(2,1)} fusion(bf16[1080,768]{1,0:T(8,128)(2,1)S(1)} %copy-done.33, bf16[1080,3072]{1,0:T(8,128)(2,1)} %get-tuple-element.234), kind=kOutput, calls=%fused_computation.1 | convolution fusion | flops 5098438656 | bytes 13012992 | tf_op jit(solution)/shard_map/dot_general | solution.py:884
  501.3 15.1 %collective-permute-start.26 = (bf16[768,3072]{1,0:T(8,128)(2,1)}, bf16[768,3072]{1,0:T(8,128)(2,1)}, u32[]{:S(2)}, u32[]{:S(2)}) collective-permute-start(bf16[768,3072]{1,0:T(8,128)(2,1)} %convolution_convert_fusion.1.in_ref), channel_id=1, source_target_pairs={{0,16},{1,17},{2,18},{3,19},{4,20},{5,21},{6,22},{7,23},{8,24},{9,... | collective-permute-start | bytes 14155784 | tf_op jit(solution)/shard_map/ppermute | solution.py:891
  521.0 13.6 %shard_map.309 = (bf16[1152,768]{1,0:T(8,128)(2,1)}, bf16[1152,768]{1,0:T(8,128)(2,1)}, bf16[1152,768]{1,0:T(8,128)(2,1)}) custom-call(bf16[1152,768]{1,0:T(8,128)(2,1)} %bitcast.33.got_ref, bf16[384,96]{1,0:T(8,128)(2,1)} %constant.48.clone.table_ref, bf16[768,768]{1,0:T(8,128)(2,1)} %get-tuple-element.171.one_ref, ...), custom_call_target="tpu_custom_call" | custom-call | flops 4294967296 | bytes 13049856 | tf_op jit(solution)/shard_map/pallas_call | solution.py:512
  542.5 12.2 %shard_map.311 = (bf16[512,768]{1,0:T(8,128)(2,1)}, bf16[512,768]{1,0:T(8,128)(2,1)}, bf16[512,768]{1,0:T(8,128)(2,1)}, bf16[512,768]{1,0:T(8,128)(2,1)}, bf16[5...) custom-call(s32[5]{0:T(128)} %concatenate.12.place_ref, bf16[768,3072]{1,0:T(8,128)(2,1)} %convolution_convert_fusion.1.in_ref, ...), custom_call_target="tpu_custom_call" | custom-call | bytes 2359296 | tf_op jit(solution)/shard_map/pallas_call | solution.py:648
  631.9 24.9 %collective-permute-done.38.one_got_ref = bf16[384,768]{1,0:T(8,128)(2,1)S(1)} collective-permute-done((bf16[384,768]{1,0:T(8,128)(2,1)}, bf16[384,768]{1,0:T(8,128)(2,1)S(1)}, u32[]{:S(2)}, u32[]{:S(2)}) %collective-permute-start.38) | collective-permute-done | bytes 589856 | tf_op jit(solution)/shard_map/ppermute | solution.py:756
  689.0 28.2 %collective-permute-done.40 = bf16[6,180,768]{2,1,0:T(8,128)(2,1)} collective-permute-done((bf16[6,180,768]{2,1,0:T(8,128)(2,1)}, bf16[6,180,768]{2,1,0:T(8,128)(2,1)}, u32[]{:S(2)}, u32[]{:S(2)}) %collective-permute-start.40) | collective-permute-done | bytes 1658912 | tf_op jit(solution)/shard_map/ppermute | solution.py:787
  767.1 9.7 %shard_map.324 = (f32[768,3072]{1,0:T(8,128)}, f32[3072,768]{1,0:T(8,128)}) custom-call(s32[5]{0:T(128)} %concatenate.12.place_ref, bf16[2,512,768]{2,1,0:T(8,128)(2,1)} %collective-permute-done.49.refs_0_, bf16[2,512,768]{2,1,0:T(8,128)(2,1)} %collective-permute-done.50.refs_1_, ...), custom_call_target="tpu_custom_call", output_to_operand_aliasing={{0}: (4, {}), {1}: (5, {})} | custom-call | bytes 14155776 | tf_op jit(solution)/shard_map/pallas_call | solution.py:694
  (244 shorter events, 339.0 us)
Async XLA Ops:
  46.0 47.3 %all-to-all-start = ((bf16[16,72,768]{2,1,0:T(8,128)(2,1)}), bf16[16,72,768]{2,1,0:T(8,128)(2,1)S(1)}, u32[]{:S(2)}, u32[]{:S(2)}) async-start(bf16[16,72,768]{2,1,0:T(8,128)(2,1)} %bitcast.91), calls=%async_computation | async-start | bytes 3538944 | tf_op jit(solution)/shard_map/all_to_all | solution.py:730
  93.2 61.0 %collective-permute-start.5 = (bf16[768,3072]{1,0:T(8,128)(2,1)}, bf16[768,3072]{1,0:T(8,128)(2,1)}, u32[]{:S(2)}, u32[]{:S(2)}) collective-permute-start(bf16[768,3072]{1,0:T(8,128)(2,1)} %bitcast.108), channel_id=1, source_target_pairs={{0,16},{16,0},{1,17},{17,1},{2,18},{18,2},{3,19},{19,3},{4,20},{20... | collective-permute-start | bytes 14155784 | tf_op jit(solution)/shard_map/ppermute | solution.py:794
  93.4 60.8 %collective-permute-start.6 = (bf16[3072,768]{1,0:T(8,128)(2,1)}, bf16[3072,768]{1,0:T(8,128)(2,1)}, u32[]{:S(2)}, u32[]{:S(2)}) collective-permute-start(bf16[3072,768]{1,0:T(8,128)(2,1)} %bitcast.113), channel_id=1, source_target_pairs={{0,16},{16,0},{1,17},{17,1},{2,18},{18,2},{3,19},{19,3},{4,20},{20... | collective-permute-start | bytes 14155784 | tf_op jit(solution)/shard_map/ppermute | solution.py:794
  140.7 41.8 %collective-permute-start.7 = (bf16[6,180,768]{2,1,0:T(8,128)(2,1)}, bf16[6,180,768]{2,1,0:T(8,128)(2,1)S(1)}, u32[]{:S(2)}, u32[]{:S(2)}) collective-permute-start(bf16[6,180,768]{2,1,0:T(8,128)(2,1)} %get-tuple-element.343), channel_id=1, source_target_pairs={{0,8},{1,9},{2,10},{3,11},{4,12},{5,13},{6,14},{7,15}} | collective-permute-start | bytes 4976648 | tf_op jit(solution)/shard_map/ppermute | solution.py:779
  144.5 38.0 %collective-permute-start.8 = (bf16[6,180,768]{2,1,0:T(8,128)(2,1)S(1)}, bf16[6,180,768]{2,1,0:T(8,128)(2,1)}, u32[]{:S(2)}, u32[]{:S(2)}) collective-permute-start(bf16[6,180,768]{2,1,0:T(8,128)(2,1)S(1)} %get-tuple-element.342), channel_id=1, source_target_pairs={{24,16},{25,17},{26,18},{27,19},{28,20},{29,21},{30,22},{31,23}} | collective-permute-start | bytes 4976648 | tf_op jit(solution)/shard_map/ppermute | solution.py:780
  259.3 51.1 %collective-permute-start.11 = (bf16[6,180,768]{2,1,0:T(8,128)(2,1)S(1)}, bf16[6,180,768]{2,1,0:T(8,128)(2,1)}, u32[]{:S(2)}, u32[]{:S(2)}) collective-permute-start(bf16[6,180,768]{2,1,0:T(8,128)(2,1)S(1)} %copy-done.1), channel_id=1, source_target_pairs={{8,0},{24,8},{9,1},{25,9},{10,2},{26,10},{11,3},{27,11},{12,4},{28... | collective-permute-start | bytes 4976648 | tf_op jit(solution)/shard_map/ppermute | solution.py:787
  260.6 49.8 %collective-permute-start.9 = (bf16[6,180,768]{2,1,0:T(8,128)(2,1)S(1)}, bf16[6,180,768]{2,1,0:T(8,128)(2,1)}, u32[]{:S(2)}, u32[]{:S(2)}) collective-permute-start(bf16[6,180,768]{2,1,0:T(8,128)(2,1)S(1)} %copy-done.1), channel_id=1, source_target_pairs={{16,8},{17,9},{18,10},{19,11},{20,12},{21,13},{22,14},{23,15}} | collective-permute-start | bytes 4976648 | tf_op jit(solution)/shard_map/ppermute | solution.py:787
  300.4 73.6 %collective-permute-start.10 = (bf16[6,180,768]{2,1,0:T(8,128)(2,1)}, bf16[6,180,768]{2,1,0:T(8,128)(2,1)}, u32[]{:S(2)}, u32[]{:S(2)}) collective-permute-start(bf16[6,180,768]{2,1,0:T(8,128)(2,1)} %get-tuple-element.187), channel_id=1, source_target_pairs={{0,16},{16,24},{1,17},{17,25},{2,18},{18,26},{3,19},{19,27},{4,20}... | collective-permute-start | bytes 4976648 | tf_op jit(solution)/shard_map/ppermute | solution.py:787
  308.1 66.0 %collective-permute-start.12 = (bf16[6,180,768]{2,1,0:T(8,128)(2,1)}, bf16[6,180,768]{2,1,0:T(8,128)(2,1)}, u32[]{:S(2)}, u32[]{:S(2)}) collective-permute-start(bf16[6,180,768]{2,1,0:T(8,128)(2,1)} %get-tuple-element.187), channel_id=1, source_target_pairs={{8,16},{9,17},{10,18},{11,19},{12,20},{13,21},{14,22},{15,23}} | collective-permute-start | bytes 4976648 | tf_op jit(solution)/shard_map/ppermute | solution.py:787
  338.7 35.3 %all-to-all-start.4 = ((bf16[16,72,768]{2,1,0:T(8,128)(2,1)}), bf16[16,72,768]{2,1,0:T(8,128)(2,1)S(1)}, u32[]{:S(2)}, u32[]{:S(2)}) async-start(bf16[16,72,768]{2,1,0:T(8,128)(2,1)} %bitcast.94), calls=%async_computation.4 | async-start | bytes 3538944 | tf_op jit(solution)/shard_map/all_to_all | solution.py:730
  354.1 52.1 %collective-permute-start.14 = (bf16[3072,768]{1,0:T(8,128)(2,1)}, bf16[3072,768]{1,0:T(8,128)(2,1)}, u32[]{:S(2)}, u32[]{:S(2)}) collective-permute-start(bf16[3072,768]{1,0:T(8,128)(2,1)} %convolution_convert_fusion.2.out_ref), channel_id=1, source_target_pairs={{16,0},{17,1},{18,2},{19,3},{20,4},{21,5},{22,6},{23,7},{24,8},{25... | collective-permute-start | bytes 14155784 | tf_op jit(solution)/shard_map/ppermute | solution.py:866
  366.5 39.7 %collective-permute-start.13 = (bf16[768,3072]{1,0:T(8,128)(2,1)}, bf16[768,3072]{1,0:T(8,128)(2,1)}, u32[]{:S(2)}, u32[]{:S(2)}) collective-permute-start(bf16[768,3072]{1,0:T(8,128)(2,1)} %convolution_convert_fusion.3.in_ref), channel_id=1, source_target_pairs={{0,16},{1,17},{2,18},{3,19},{4,20},{5,21},{6,22},{7,23},{8,24},{9,... | collective-permute-start | bytes 14155784 | tf_op jit(solution)/shard_map/ppermute | solution.py:866
  470.7 50.3 %all-to-all-start.6 = ((bf16[16,72,768]{2,1,0:T(8,128)(2,1)}), bf16[16,72,768]{2,1,0:T(8,128)(2,1)}, u32[]{:S(2)}, u32[]{:S(2)}) async-start(bf16[16,72,768]{2,1,0:T(8,128)(2,1)} %bitcast.90), calls=%async_computation.6 | async-start | bytes 3538944 | tf_op jit(solution)/shard_map/all_to_all | solution.py:730
  501.3 41.2 %collective-permute-start.26 = (bf16[768,3072]{1,0:T(8,128)(2,1)}, bf16[768,3072]{1,0:T(8,128)(2,1)}, u32[]{:S(2)}, u32[]{:S(2)}) collective-permute-start(bf16[768,3072]{1,0:T(8,128)(2,1)} %convolution_convert_fusion.1.in_ref), channel_id=1, source_target_pairs={{0,16},{1,17},{2,18},{3,19},{4,20},{5,21},{6,22},{7,23},{8,24},{9,... | collective-permute-start | bytes 14155784 | tf_op jit(solution)/shard_map/ppermute | solution.py:891
  534.5 41.4 %all-to-all-start.7 = ((bf16[16,72,768]{2,1,0:T(8,128)(2,1)}), bf16[16,72,768]{2,1,0:T(8,128)(2,1)}, u32[]{:S(2)}, u32[]{:S(2)}) async-start(bf16[16,72,768]{2,1,0:T(8,128)(2,1)} %bitcast.89), calls=%async_computation.7 | async-start | bytes 3538944 | tf_op jit(solution)/shard_map/all_to_all | solution.py:730
  554.7 35.9 %collective-permute-start.28 = (bf16[512,768]{1,0:T(8,128)(2,1)}, bf16[512,768]{1,0:T(8,128)(2,1)}, u32[]{:S(2)}, u32[]{:S(2)}) collective-permute-start(bf16[512,768]{1,0:T(8,128)(2,1)} %get-tuple-element.259), channel_id=1, source_target_pairs={{0,1},{1,0},{2,3},{3,2},{4,5},{5,4},{6,7},{7,6},{8,9},{9,8},{10,11... | collective-permute-start | bytes 2359304 | tf_op jit(solution)/shard_map/ppermute | solution.py:743
  602.4 67.6 %all-to-all-start.8 = ((bf16[16,208,128]{2,1,0:T(8,128)(2,1)}), bf16[16,208,128]{2,1,0:T(8,128)(2,1)}, u32[]{:S(2)}, u32[]{:S(2)}) async-start(bf16[16,208,128]{2,1,0:T(8,128)(2,1)} %bitcast.87), calls=%async_computation.8 | async-start | bytes 1703936 | tf_op jit(solution)/shard_map/all_to_all | solution.py:772
  662.4 54.8 %collective-permute-start.40 = (bf16[6,180,768]{2,1,0:T(8,128)(2,1)}, bf16[6,180,768]{2,1,0:T(8,128)(2,1)}, u32[]{:S(2)}, u32[]{:S(2)}) collective-permute-start(bf16[6,180,768]{2,1,0:T(8,128)(2,1)} %get-tuple-element.292), channel_id=1, source_target_pairs={{8,0},{24,8},{9,1},{25,9},{10,2},{26,10},{11,3},{27,11},{12,4},{28... | collective-permute-start | bytes 4976648 | tf_op jit(solution)/shard_map/ppermute | solution.py:787
  672.2 63.3 %all-to-all-start.9 = ((bf16[16,208,128]{2,1,0:T(8,128)(2,1)}), bf16[16,208,128]{2,1,0:T(8,128)(2,1)}, u32[]{:S(2)}, u32[]{:S(2)}) async-start(bf16[16,208,128]{2,1,0:T(8,128)(2,1)} %shard_map.318), calls=%async_computation.9 | async-start | bytes 1703936 | tf_op jit(solution)/shard_map/all_to_all | solution.py:774
  686.4 35.6 %collective-permute-start.47 = (bf16[2,256,768]{2,1,0:T(8,128)(2,1)}, bf16[2,256,768]{2,1,0:T(8,128)(2,1)S(1)}, u32[]{:S(2)}, u32[]{:S(2)}) collective-permute-start(bf16[2,256,768]{2,1,0:T(8,128)(2,1)} %get-tuple-element.311.refs_1_), channel_id=1, source_target_pairs={{0,4},{1,5},{2,6},{3,7},{4,0},{5,1},{6,2},{7,3},{8,12},{9,13},{10,... | collective-permute-start | bytes 2359304 | tf_op jit(solution)/shard_map/ppermute | solution.py:743
  687.2 34.9 %collective-permute-start.48 = (bf16[2,256,768]{2,1,0:T(8,128)(2,1)}, bf16[2,256,768]{2,1,0:T(8,128)(2,1)S(1)}, u32[]{:S(2)}, u32[]{:S(2)}) collective-permute-start(bf16[2,256,768]{2,1,0:T(8,128)(2,1)} %get-tuple-element.312.refs_2_), channel_id=1, source_target_pairs={{0,1},{1,0},{2,3},{3,2},{4,5},{5,4},{6,7},{7,6},{8,9},{9,8},{10,11... | collective-permute-start | bytes 2359304 | tf_op jit(solution)/shard_map/ppermute | solution.py:743
  728.6 38.5 %collective-permute-start.49 = (bf16[2,512,768]{2,1,0:T(8,128)(2,1)}, bf16[2,512,768]{2,1,0:T(8,128)(2,1)}, u32[]{:S(2)}, u32[]{:S(2)}) collective-permute-start(bf16[2,512,768]{2,1,0:T(8,128)(2,1)} %get-tuple-element.316.refs_0_), channel_id=1, source_target_pairs={{0,1},{1,0},{2,3},{3,2},{4,5},{5,4},{6,7},{7,6},{8,9},{9,8},{10,11... | collective-permute-start | bytes 4718600 | tf_op jit(solution)/shard_map/ppermute | solution.py:743
  730.7 36.4 %collective-permute-start.50 = (bf16[2,512,768]{2,1,0:T(8,128)(2,1)}, bf16[2,512,768]{2,1,0:T(8,128)(2,1)}, u32[]{:S(2)}, u32[]{:S(2)}) collective-permute-start(bf16[2,512,768]{2,1,0:T(8,128)(2,1)} %get-tuple-element.317.refs_1_), channel_id=1, source_target_pairs={{0,2},{1,3},{2,0},{3,1},{4,6},{5,7},{6,4},{7,5},{8,10},{9,11},{10,... | collective-permute-start | bytes 4718600 | tf_op jit(solution)/shard_map/ppermute | solution.py:743
  731.2 35.9 %collective-permute-start.51 = (bf16[2,512,768]{2,1,0:T(8,128)(2,1)}, bf16[2,512,768]{2,1,0:T(8,128)(2,1)}, u32[]{:S(2)}, u32[]{:S(2)}) collective-permute-start(bf16[2,512,768]{2,1,0:T(8,128)(2,1)} %get-tuple-element.318.refs_2_), channel_id=1, source_target_pairs={{0,4},{1,5},{2,6},{3,7},{4,0},{5,1},{6,2},{7,3},{8,12},{9,13},{10,... | collective-permute-start | bytes 4718600 | tf_op jit(solution)/shard_map/ppermute | solution.py:743
  (70 other events, 920.5 us)
